TPU v7x, 32 devices: a whole 2x2x4 slice. The times are simulated.
32 devices in a mesh: tiles: 2 (over y), band: 4 (over x, core), head: 4 (over z).
Axes of the slice: x: 2, y: 2, z: 4, core: 2. Of those that a mesh axis runs over, the one named last changes fastest.
Arguments:
- tokens: bfloat16 [8192, 1024], P(('tiles', 'band')), parts along dimension 0, may hold values from -24 to 24
- w_query: bfloat16 [1024, 1024], P(None, 'head'), may hold values from -0.375 to 0.375
- w_key: bfloat16 [1024, 1024], P(None, 'head'), may hold values from -0.1875 to 0.1875
- w_value: bfloat16 [1024, 1024], P(None, 'head'), may hold values from -0.1875 to 0.1875
- w_out: bfloat16 [1024, 1024], P('head'), may hold values from -0.75 to 0.75
- block_mask: int32 [64, 32], P('tiles'), parts along dimension 0, may hold values from 0 to 1, as said below
Outputs:
- projected: bfloat16 [8192, 1024], P(('tiles', 'band', 'head')), parts along dimension 0
There are 2 independent parts, one for each index of `tiles`. A program takes and returns all parts, laid end to end along the dimension named above; an argument that names none is the same for every part. Nothing has to cross between parts.
Inputs may be any that keep to these rules, and one draw needn't show every extreme that they name: `block_mask`: entries are 0 or 1. Every query block may attend to at least one key block. Among the 8 key blocks of one band at most 6 are named by some query block, and some band has exactly 6.
All inputs are finite; a program needn't handle non-finite values.
Results may differ from a plain program's by a relative error of at most 0.02.
Values may be sent and summed in bfloat16 or wider, within the bound.
No kernel may reach another device: no remote copies, remote signals or barrier semaphores. Data moves between devices by JAX's collectives and lax.ppermute only.
A program may use at most 128 MiB of HBM per device.

v0:
```python
import jax
import jax.numpy as jnp
from jax import lax
from jax.sharding import PartitionSpec as P

HD = 64
BLK = 128


rows_per_turn = 8192
neg_large = -1e30


def attend(item_rows, item_block, block_mask, kv_table, kv_where, head_count):
    item_count, item_len, local_cols = item_rows.shape
    key_blocks = block_mask.shape[1]
    head_dim = local_cols // head_count
    score_scale = head_dim ** (-0.5)
    allowed = jnp.take(block_mask, item_block, axis=0).reshape(-1)
    pair_total = item_count * key_blocks
    pair_order = jnp.argsort((1 - allowed) * pair_total + jnp.arange(pair_total, dtype=jnp.int32))
    pair_count = jnp.sum(allowed)
    per_turn = max(1, rows_per_turn // item_len)
    padded_len = -(-pair_total // per_turn) * per_turn
    pair_order = jnp.concatenate([pair_order, jnp.zeros((padded_len - pair_total,), jnp.int32)])
    turn_count = (pair_count + per_turn - 1) // per_turn
    slot_ids = jnp.arange(per_turn, dtype=jnp.int32)
    table_rows = kv_table.shape[0]

    def one_turn(turn_index, carried):
        run_peak, run_mass, run_sum = carried
        chosen = lax.dynamic_slice_in_dim(pair_order, turn_index * per_turn, per_turn)
        is_live = turn_index * per_turn + slot_ids < pair_count
        owners = chosen // key_blocks
        key_block = chosen % key_blocks
        query_rows = jnp.take(item_rows, owners, axis=0).reshape(
            per_turn, item_len, head_count, head_dim
        )
        table_pos = jnp.clip(jnp.take(kv_where, key_block), 0, table_rows - 1)
        pair_rows = jnp.take(kv_table, table_pos, axis=0)
        key_rows = pair_rows[:, :, :local_cols].reshape(per_turn, -1, head_count, head_dim)
        value_rows = pair_rows[:, :, local_cols:].reshape(per_turn, -1, head_count, head_dim)
        scores = (
            jnp.einsum("prhd,pkhd->prhk", query_rows, key_rows, preferred_element_type=jnp.float32)
            * score_scale
        )
        row_peak = jnp.max(scores, axis=3)
        exponent = jnp.exp(scores - row_peak[..., None])
        row_mass = jnp.sum(exponent, axis=3)
        weights = exponent.astype(jnp.bfloat16)
        partial_out = jnp.einsum(
            "prhk,pkhd->prhd", weights, value_rows, preferred_element_type=jnp.float32
        )
        live_peak = jnp.where(is_live[:, None, None], row_peak, neg_large)
        turn_peak = jax.ops.segment_max(live_peak, owners, num_segments=item_count)
        new_peak = jnp.maximum(run_peak, turn_peak)
        factor = jnp.exp(run_peak - new_peak)
        pair_scale = jnp.where(
            is_live[:, None, None], jnp.exp(live_peak - jnp.take(new_peak, owners, axis=0)), 0.0
        )
        mass_terms = jnp.where(is_live[:, None, None], row_mass * pair_scale, 0.0)
        sum_terms = jnp.where(
            is_live[:, None, None, None], partial_out * pair_scale[..., None], 0.0
        )
        run_mass = run_mass * factor + jax.ops.segment_sum(
            mass_terms, owners, num_segments=item_count
        )
        run_sum = run_sum * factor[..., None] + jax.ops.segment_sum(
            sum_terms, owners, num_segments=item_count
        )
        return (new_peak, run_mass, run_sum)

    start_state = (
        jnp.full((item_count, item_len, head_count), neg_large, jnp.float32),
        jnp.zeros((item_count, item_len, head_count), jnp.float32),
        jnp.zeros((item_count, item_len, head_count, head_dim), jnp.float32),
    )
    run_peak, run_mass, run_sum = lax.fori_loop(0, turn_count, one_turn, start_state)
    return (
        (run_sum / run_mass[..., None])
        .reshape(item_count, item_len, local_cols)
        .astype(jnp.bfloat16)
    )


def on_device(tokens, w_query, w_key, w_value, w_out, block_mask):
    band_place = lax.axis_index("band")
    tok_rows = tokens.shape[0]
    local_cols = w_query.shape[1]
    head_count = local_cols // HD
    own_blocks = tok_rows // BLK
    key_blocks = block_mask.shape[1]
    queries = jnp.dot(tokens, w_query, preferred_element_type=jnp.float32).astype(jnp.bfloat16)
    key_part = jnp.dot(tokens, w_key, preferred_element_type=jnp.float32).astype(jnp.bfloat16)
    value_part = jnp.dot(tokens, w_value, preferred_element_type=jnp.float32).astype(jnp.bfloat16)
    key_value = jnp.concatenate([key_part, value_part], axis=1)
    kv_table = lax.all_gather(key_value, "band", axis=0, tiled=True).reshape(
        key_blocks, BLK, 2 * local_cols
    )
    kv_where = jnp.arange(key_blocks, dtype=jnp.int32)
    item_rows = queries.reshape(own_blocks, BLK, local_cols)
    item_block = band_place * own_blocks + jnp.arange(own_blocks, dtype=jnp.int32)
    attended = attend(item_rows, item_block, block_mask, kv_table, kv_where, head_count).reshape(
        tok_rows, local_cols
    )
    projected = lax.psum_scatter(
        jnp.dot(attended, w_out, preferred_element_type=jnp.float32).astype(jnp.bfloat16),
        "head",
        scatter_dimension=0,
        tiled=True,
    )
    return projected


def solution(mesh):
    return jax.shard_map(
        on_device,
        mesh=mesh,
        in_specs=(
            P(("tiles", "band"), None),
            P(None, "head"),
            P(None, "head"),
            P(None, "head"),
            P("head", None),
            P("tiles", None),
        ),
        out_specs=P(("tiles", "band", "head"), None),
        check_vma=False,
    )
```

profile of v0, /device:TPU:0, one launch (start us, length us, event | category | flops | bytes accessed | tf_op | source)
XLA Modules:
  0.0 415.9 jit_solution(12742740644684946796)
XLA Ops:
  8.1 1.8 convolution_convert_fusion.2
  9.9 1.8 convolution_convert_fusion.3
  15.0 3.2 sort.17
  18.2 2.5 convolution_convert_fusion.1
  20.7 29.4 %all-gather.2.cloned.1.call-done = bf16[4096,512]{0,1:T(8,128)(2,1)} async-done(((bf16[1024,512]{0,1:T(8,128)(2,1)}), bf16[4096,512]{0,1:T(8,128)(2,1)}) %all-gather.2.cloned.1.call-update) | async-done | bytes 4194320 | tf_op jit(solution)/shard_map/all_gather | solution.py:97
  50.1 6.5 %copy.24 = bf16[4096,512]{1,0:T(8,128)(2,1)} copy(bf16[4096,512]{0,1:T(8,128)(2,1)} %all-gather.2.cloned.1.call-done) | data formatting | bytes 8388608
  56.8 305.3 %while.17 = (s32[]{:T(128)}, f32[8,128,4]{1,2,0:T(4,128)S(1)}, f32[8,128,4]{1,2,0:T(4,128)S(1)}, f32[8,128,4,64]{1,3,2,0:T(8,128)S(1)}, s32[]{:T(128)}, /*index=...) while((s32[]{:T(128)}, f32[8,128,4]{1,2,0:T(4,128)S(1)}, ...), condition=%wide.region_8.9_spmd.clone, body=%wide.region_2.8_spmd.clone.sunk | while | flops 1120389376 | bytes 185223568 | solution.py:78
  58.6 7.7 %gather_fusion.1 = bf16[64,128,512]{2,1,0:T(8,128)(2,1)} fusion(bf16[32,128,512]{2,1,0:T(8,128)(2,1)} %get-tuple-element.364, s32[1024]{0:T(1024)S(1)} %pad_clamp_fusion.8), kind=kCustom, calls=%fused_computation.1.clone.clone.1 | custom fusion | bytes 16777472 | tf_op jit(solution)/shard_map/while/body/jit(_take)/gather | solution.py:40
  66.3 7.5 %broadcast_select_fusion.4 = bf16[64,128,512]{2,1,0:T(8,128)(2,1)} fusion(bf16[64,128,512]{2,1,0:T(8,128)(2,1)} %gather_fusion.1, pred[64]{0:T(512)(128)(4,1)S(1)} %get-tuple-element.317), kind=kLoop, calls=%fused_computation.20.clone.1 | loop fusion | flops 4194304 | bytes 16777280 | tf_op jit(solution)/shard_map/while/body/jit(_take)/select_n | solution.py:40
  73.8 6.0 %fusion.45 = (bf16[64,128,256]{2,1,0:T(8,128)(2,1)}, bf16[64,128,256]{2,1,0:T(8,128)(2,1)}) fusion(bf16[64,128,512]{2,1,0:T(8,128)(2,1)} %broadcast_select_fusion.4), kind=kLoop, calls=%fused_computation.65.clone.1 | loop fusion | bytes 16777216 | tf_op jit(solution)/shard_map/while/body/slice | solution.py:42
  79.8 6.4 %copy.33 = bf16[64,128,256]{1,2,0:T(8,128)(2,1)} copy(bf16[64,128,256]{2,1,0:T(8,128)(2,1)} %get-tuple-element.318) | data formatting | bytes 8388608 | tf_op jit(solution)/shard_map/while/body/slice | solution.py:41
  86.1 2.7 gather_fusion.2
  88.9 6.4 %copy.34 = bf16[64,128,256]{1,2,0:T(8,128)(2,1)} copy(bf16[64,128,256]{2,1,0:T(8,128)(2,1)} %gather_fusion.2) | data formatting | bytes 8388608 | tf_op jit(solution)/shard_map/while/body/jit(_take)/gather | solution.py:36
  95.3 12.2 %bitcast_reduce_fusion.2 = (f32[64,128,4]{1,2,0:T(4,128)S(1)}, f32[64,4,128,128]{3,2,1,0:T(8,128)}) fusion(bf16[64,128,4,64]{1,3,2,0:T(8,128)(2,1)} %bitcast.83, bf16[64,128,4,64]{1,3,2,0:T(8,128)(2,1)} %bitcast.85, pred[64]{0:T(512)(128)(4,1)S(1)} %get-tuple-element.319), kind=kOutput, calls=%fused_computation.11.clone.1 | convolution fusion | flops 547323904 | bytes 25296960 | tf_op jit(solution)/shard_map/while/body/prhd,pkhd->prhk/dot_general | solution.py:44
  107.7 2.9 scatter_fusion
  110.6 10.7 %fusion.47 = f32[64,128,4]{1,2,0:T(4,128)S(1)} fusion(f32[64,4,128,128]{3,2,1,0:T(8,128)} %get-tuple-element.325, f32[64,128,4]{1,2,0:T(4,128)S(1)} %get-tuple-element.320), kind=kLoop, calls=%fused_computation.14.clone.1 | loop fusion | flops 12550144 | bytes 17039360 | tf_op jit(solution)/shard_map/while/body/reduce_sum | solution.py:49
  122.2 2.9 scatter_fusion.1
  125.4 6.4 %copy.35 = bf16[64,128,256]{1,2,0:T(8,128)(2,1)} copy(bf16[64,128,256]{2,1,0:T(8,128)(2,1)} %get-tuple-element.328) | data formatting | bytes 8388608 | tf_op jit(solution)/shard_map/while/body/slice | solution.py:42
  131.8 14.6 %fusion.48 = f32[64,128,4,64]{1,3,2,0:T(8,128)} fusion(f32[64,128,4]{1,2,0:T(4,128)S(1)} %get-tuple-element.327, pred[64]{0:T(512)(128)(4,1)S(1)} %get-tuple-element.321, bf16[64,128,4,64]{1,3,2,0:T(8,128)(2,1)} %bitcast.84, f32[64,4,128,128]{3,2,1,0:T(8,128)} %get-tuple-element.325, f32[64,128,4]{1,2,0:T(4,128)S(1)} %get-tuple-element.320), kind=kOutput, calls=%fused_computation.17.clone.1 | convolution fusion | flops 553648128 | bytes 29622336 | tf_op jit(solution)/shard_map/while/body/prhk,pkhd->prhd/dot_general | solution.py:51
  146.3 12.3 %scatter_fusion.2 = f32[8,128,4,64]{1,3,2,0:T(8,128)S(1)} fusion(f32[8,128,4,64]{1,3,2,0:T(8,128)S(1)} %broadcast_multiply_fusion.2, s32[64]{0:T(128)S(1)} %get-tuple-element.314, f32[64,128,4,64]{1,3,2,0:T(8,128)} %fusion.48), kind=kCustom, calls=%fused_computation.7.clone.clone.1 | custom fusion | flops 2097152 | bytes 25166080 | tf_op jit(solution)/shard_map/while/body/scatter-add | solution.py:68
  160.2 7.7 %gather_fusion.1 = bf16[64,128,512]{2,1,0:T(8,128)(2,1)} fusion(bf16[32,128,512]{2,1,0:T(8,128)(2,1)} %get-tuple-element.364, s32[1024]{0:T(1024)S(1)} %pad_clamp_fusion.8), kind=kCustom, calls=%fused_computation.1.clone.clone.1 | custom fusion | bytes 16777472 | tf_op jit(solution)/shard_map/while/body/jit(_take)/gather | solution.py:40
  167.9 7.5 %broadcast_select_fusion.4 = bf16[64,128,512]{2,1,0:T(8,128)(2,1)} fusion(bf16[64,128,512]{2,1,0:T(8,128)(2,1)} %gather_fusion.1, pred[64]{0:T(512)(128)(4,1)S(1)} %get-tuple-element.317), kind=kLoop, calls=%fused_computation.20.clone.1 | loop fusion | flops 4194304 | bytes 16777280 | tf_op jit(solution)/shard_map/while/body/jit(_take)/select_n | solution.py:40
  175.4 6.0 %fusion.45 = (bf16[64,128,256]{2,1,0:T(8,128)(2,1)}, bf16[64,128,256]{2,1,0:T(8,128)(2,1)}) fusion(bf16[64,128,512]{2,1,0:T(8,128)(2,1)} %broadcast_select_fusion.4), kind=kLoop, calls=%fused_computation.65.clone.1 | loop fusion | bytes 16777216 | tf_op jit(solution)/shard_map/while/body/slice | solution.py:42
  181.4 6.4 %copy.33 = bf16[64,128,256]{1,2,0:T(8,128)(2,1)} copy(bf16[64,128,256]{2,1,0:T(8,128)(2,1)} %get-tuple-element.318) | data formatting | bytes 8388608 | tf_op jit(solution)/shard_map/while/body/slice | solution.py:41
  187.8 2.7 gather_fusion.2
  190.5 6.4 %copy.34 = bf16[64,128,256]{1,2,0:T(8,128)(2,1)} copy(bf16[64,128,256]{2,1,0:T(8,128)(2,1)} %gather_fusion.2) | data formatting | bytes 8388608 | tf_op jit(solution)/shard_map/while/body/jit(_take)/gather | solution.py:36
  196.9 12.2 %bitcast_reduce_fusion.2 = (f32[64,128,4]{1,2,0:T(4,128)S(1)}, f32[64,4,128,128]{3,2,1,0:T(8,128)}) fusion(bf16[64,128,4,64]{1,3,2,0:T(8,128)(2,1)} %bitcast.83, bf16[64,128,4,64]{1,3,2,0:T(8,128)(2,1)} %bitcast.85, pred[64]{0:T(512)(128)(4,1)S(1)} %get-tuple-element.319), kind=kOutput, calls=%fused_computation.11.clone.1 | convolution fusion | flops 547323904 | bytes 25296960 | tf_op jit(solution)/shard_map/while/body/prhd,pkhd->prhk/dot_general | solution.py:44
  209.3 2.9 scatter_fusion
  212.2 10.7 %fusion.47 = f32[64,128,4]{1,2,0:T(4,128)S(1)} fusion(f32[64,4,128,128]{3,2,1,0:T(8,128)} %get-tuple-element.325, f32[64,128,4]{1,2,0:T(4,128)S(1)} %get-tuple-element.320), kind=kLoop, calls=%fused_computation.14.clone.1 | loop fusion | flops 12550144 | bytes 17039360 | tf_op jit(solution)/shard_map/while/body/reduce_sum | solution.py:49
  223.9 2.9 scatter_fusion.1
  227.0 6.4 %copy.35 = bf16[64,128,256]{1,2,0:T(8,128)(2,1)} copy(bf16[64,128,256]{2,1,0:T(8,128)(2,1)} %get-tuple-element.328) | data formatting | bytes 8388608 | tf_op jit(solution)/shard_map/while/body/slice | solution.py:42
  233.4 14.5 %fusion.48 = f32[64,128,4,64]{1,3,2,0:T(8,128)} fusion(f32[64,128,4]{1,2,0:T(4,128)S(1)} %get-tuple-element.327, pred[64]{0:T(512)(128)(4,1)S(1)} %get-tuple-element.321, bf16[64,128,4,64]{1,3,2,0:T(8,128)(2,1)} %bitcast.84, f32[64,4,128,128]{3,2,1,0:T(8,128)} %get-tuple-element.325, f32[64,128,4]{1,2,0:T(4,128)S(1)} %get-tuple-element.320), kind=kOutput, calls=%fused_computation.17.clone.1 | convolution fusion | flops 553648128 | bytes 29622336 | tf_op jit(solution)/shard_map/while/body/prhk,pkhd->prhd/dot_general | solution.py:51
  247.9 12.3 %scatter_fusion.2 = f32[8,128,4,64]{1,3,2,0:T(8,128)S(1)} fusion(f32[8,128,4,64]{1,3,2,0:T(8,128)S(1)} %broadcast_multiply_fusion.2, s32[64]{0:T(128)S(1)} %get-tuple-element.314, f32[64,128,4,64]{1,3,2,0:T(8,128)} %fusion.48), kind=kCustom, calls=%fused_computation.7.clone.clone.1 | custom fusion | flops 2097152 | bytes 25166080 | tf_op jit(solution)/shard_map/while/body/scatter-add | solution.py:68
  261.8 7.7 %gather_fusion.1 = bf16[64,128,512]{2,1,0:T(8,128)(2,1)} fusion(bf16[32,128,512]{2,1,0:T(8,128)(2,1)} %get-tuple-element.364, s32[1024]{0:T(1024)S(1)} %pad_clamp_fusion.8), kind=kCustom, calls=%fused_computation.1.clone.clone.1 | custom fusion | bytes 16777472 | tf_op jit(solution)/shard_map/while/body/jit(_take)/gather | solution.py:40
  269.6 7.5 %broadcast_select_fusion.4 = bf16[64,128,512]{2,1,0:T(8,128)(2,1)} fusion(bf16[64,128,512]{2,1,0:T(8,128)(2,1)} %gather_fusion.1, pred[64]{0:T(512)(128)(4,1)S(1)} %get-tuple-element.317), kind=kLoop, calls=%fused_computation.20.clone.1 | loop fusion | flops 4194304 | bytes 16777280 | tf_op jit(solution)/shard_map/while/body/jit(_take)/select_n | solution.py:40
  277.0 6.0 %fusion.45 = (bf16[64,128,256]{2,1,0:T(8,128)(2,1)}, bf16[64,128,256]{2,1,0:T(8,128)(2,1)}) fusion(bf16[64,128,512]{2,1,0:T(8,128)(2,1)} %broadcast_select_fusion.4), kind=kLoop, calls=%fused_computation.65.clone.1 | loop fusion | bytes 16777216 | tf_op jit(solution)/shard_map/while/body/slice | solution.py:42
  283.0 6.4 %copy.33 = bf16[64,128,256]{1,2,0:T(8,128)(2,1)} copy(bf16[64,128,256]{2,1,0:T(8,128)(2,1)} %get-tuple-element.318) | data formatting | bytes 8388608 | tf_op jit(solution)/shard_map/while/body/slice | solution.py:41
  289.4 2.7 gather_fusion.2
  292.2 6.4 %copy.34 = bf16[64,128,256]{1,2,0:T(8,128)(2,1)} copy(bf16[64,128,256]{2,1,0:T(8,128)(2,1)} %gather_fusion.2) | data formatting | bytes 8388608 | tf_op jit(solution)/shard_map/while/body/jit(_take)/gather | solution.py:36
  298.5 12.2 %bitcast_reduce_fusion.2 = (f32[64,128,4]{1,2,0:T(4,128)S(1)}, f32[64,4,128,128]{3,2,1,0:T(8,128)}) fusion(bf16[64,128,4,64]{1,3,2,0:T(8,128)(2,1)} %bitcast.83, bf16[64,128,4,64]{1,3,2,0:T(8,128)(2,1)} %bitcast.85, pred[64]{0:T(512)(128)(4,1)S(1)} %get-tuple-element.319), kind=kOutput, calls=%fused_computation.11.clone.1 | convolution fusion | flops 547323904 | bytes 25296960 | tf_op jit(solution)/shard_map/while/body/prhd,pkhd->prhk/dot_general | solution.py:44
  310.9 2.9 scatter_fusion
  313.9 10.7 %fusion.47 = f32[64,128,4]{1,2,0:T(4,128)S(1)} fusion(f32[64,4,128,128]{3,2,1,0:T(8,128)} %get-tuple-element.325, f32[64,128,4]{1,2,0:T(4,128)S(1)} %get-tuple-element.320), kind=kLoop, calls=%fused_computation.14.clone.1 | loop fusion | flops 12550144 | bytes 17039360 | tf_op jit(solution)/shard_map/while/body/reduce_sum | solution.py:49
  325.5 2.9 scatter_fusion.1
  328.7 6.4 %copy.35 = bf16[64,128,256]{1,2,0:T(8,128)(2,1)} copy(bf16[64,128,256]{2,1,0:T(8,128)(2,1)} %get-tuple-element.328) | data formatting | bytes 8388608 | tf_op jit(solution)/shard_map/while/body/slice | solution.py:42
  335.0 14.5 %fusion.48 = f32[64,128,4,64]{1,3,2,0:T(8,128)} fusion(f32[64,128,4]{1,2,0:T(4,128)S(1)} %get-tuple-element.327, pred[64]{0:T(512)(128)(4,1)S(1)} %get-tuple-element.321, bf16[64,128,4,64]{1,3,2,0:T(8,128)(2,1)} %bitcast.84, f32[64,4,128,128]{3,2,1,0:T(8,128)} %get-tuple-element.325, f32[64,128,4]{1,2,0:T(4,128)S(1)} %get-tuple-element.320), kind=kOutput, calls=%fused_computation.17.clone.1 | convolution fusion | flops 553648128 | bytes 29622336 | tf_op jit(solution)/shard_map/while/body/prhk,pkhd->prhd/dot_general | solution.py:51
  349.6 12.3 %scatter_fusion.2 = f32[8,128,4,64]{1,3,2,0:T(8,128)S(1)} fusion(f32[8,128,4,64]{1,3,2,0:T(8,128)S(1)} %broadcast_multiply_fusion.2, s32[64]{0:T(128)S(1)} %get-tuple-element.314, f32[64,128,4,64]{1,3,2,0:T(8,128)} %fusion.48), kind=kCustom, calls=%fused_computation.7.clone.clone.1 | custom fusion | flops 2097152 | bytes 25166080 | tf_op jit(solution)/shard_map/while/body/scatter-add | solution.py:68
  362.6 3.3 convolution_convert_fusion
  365.9 43.1 %reduce-scatter.2.cloned.1.call-done = bf16[256,1024]{1,0:T(8,128)(2,1)} async-done(((bf16[1024,1024]{1,0:T(8,128)(2,1)}), bf16[256,1024]{1,0:T(8,128)(2,1)}) %reduce-scatter.2.cloned.1.call-update) | async-done | bytes 524304 | tf_op jit(solution)/shard_map/reduce_scatter | solution.py:106
  (71 shorter events, 13.3 us)
Async XLA Ops:
  6.5 1.6 copy-start
  6.5 6.3 %copy-start.3 = (s32[32,32]{1,0:T(8,128)S(1)}, s32[32,32]{1,0:T(8,128)}, u32[]{:S(2)}) copy-start(s32[32,32]{1,0:T(8,128)} %param.13) | copy-start | bytes 12292
  6.5 43.6 %all-gather.2.cloned.1.call-start = ((), (), s32[]{:S(2)}) async-start(), calls=%async_computation.1 | async-start | bytes 5242880 | tf_op jit(solution)/shard_map/all_gather | solution.py:97
  12.8 396.2 %reduce-scatter.2.cloned.1.call-start = ((), (), s32[]{:S(2)}) async-start(), calls=%async_computation.2 | async-start | bytes 2621440 | tf_op jit(solution)/shard_map/reduce_scatter | solution.py:106
  20.7 36.0 %copy-start.2 = (bf16[1024,256]{1,0:T(8,128)(2,1)S(1)}, bf16[1024,256]{1,0:T(8,128)(2,1)}, u32[]{:S(2)}) copy-start(bf16[1024,256]{1,0:T(8,128)(2,1)} %convolution_convert_fusion.1) | copy-start | bytes 1572868
  362.1 46.9 %copy-start.1 = (bf16[1024,1024]{1,0:T(8,128)(2,1)S(1)}, bf16[1024,1024]{1,0:T(8,128)(2,1)}, u32[]{:S(2)}) copy-start(bf16[1024,1024]{1,0:T(8,128)(2,1)} %param.8) | copy-start | bytes 6291460
Sparse Core Ops, SparseCore 0:
  12.9 37.1 all-gather.1
  366.0 42.9 reduce-scatter.1
where the time goes:
time: 418 us; the launch traced here: 416 us
  local copies, waits for them, and re-layouts  120 us (29%)
  other arithmetic  118 us (28%)
  matrix products  89.7 us (21%)
  waiting for transfers between devices  72.6 us (17%)
  between operations  14.2 us (3%)
    dot_general x3, matrix products, one_turn(): jnp.einsum('prhk,pkhd->prhd', weights, value_rows, preferred_element_type...  43.6 us
    reduce_scatter x1, waiting for transfers between devices, on_device(): lax.psum_scatter(jnp.dot(attended, w_out, preferred_element_type=jnp.floa...  43.1 us
    slice x6, local copies, waits for them, and re-layouts, one_turn(): pair_rows[:, :, local_cols:].reshape(per_turn, -1, head_count, head_dim)  37.2 us
    scatter-add x3, other arithmetic, one_turn(): jax.ops.segment_sum(sum_terms, owners, num_segments=item_count)  36.8 us
    dot_general x3, matrix products, one_turn(): jnp.einsum('prhd,pkhd->prhk', query_rows, key_rows, preferred_element_typ...  36.7 us
    reduce_sum x3, other arithmetic, one_turn(): row_mass = jnp.sum(exponent, axis=3)  32.2 us
    all_gather x1, waiting for transfers between devices, on_device(): lax.all_gather(key_value, 'band', axis=0, tiled=True)  29.4 us
    gather x6, local copies, waits for them, and re-layouts, one_turn(): jnp.take(item_rows, owners, axis=0)  27.4 us
  transfers between devices with their start and end apart: 2, of which 2 were waited for; matrix products, arithmetic and copies ran while one was open for 2% of the time, Pallas kernels for 0%

commit v1 on v0

v1 whole, which is shorter than its diff:
```python
import functools
import math

import jax
import jax.numpy as jnp
from jax import lax
from jax.experimental import pallas as pl
from jax.experimental.pallas import tpu as pltpu
from jax.sharding import PartitionSpec as P

HD = 64
BLK = 128
KEEP = 6
LANES = 128
NEG = -1e30
LOWEST = -3e38
CHUNK = 512
QUERY_SCALE = HD**-0.5 * math.log2(math.e)
PARAMS = pltpu.CompilerParams(vmem_limit_bytes=56 * 2**20)
ANY = pl.BlockSpec(memory_space=pl.ANY)
VMEM = pl.BlockSpec(memory_space=pltpu.VMEM)


def dot_f32(left, right):
    return jnp.dot(left, right, preferred_element_type=jnp.float32)


def low_lanes(shape):
    return lax.broadcasted_iota(jnp.int32, shape, len(shape) - 1) < HD


def swap_halves(array):
    return pltpu.roll(array, HD, array.ndim - 1)


def project_kv(place, block_mask, tokens, w_key, w_value):
    rows_in, width = tokens.shape
    per_band = rows_in // BLK
    local_cols = w_key.shape[1]
    pairs = local_cols // LANES
    rows = KEEP * BLK
    query_blocks = block_mask.shape[0]

    def kernel(place_ref, mask_ref, tok_ref, wk_ref, wv_ref, *rest):
        outs, (tok, wk, wv, sems) = rest[:pairs], rest[pairs:]
        copies = [
            pltpu.make_async_copy(wk_ref, wk, sems.at[KEEP]),
            pltpu.make_async_copy(wv_ref, wv, sems.at[KEEP + 1]),
        ]
        for copy in copies:
            copy.start()
        first = place_ref[0] * per_band

        def look(i, seen):
            return tuple(s | mask_ref[i, first + j] for j, s in enumerate(seen))

        seen = lax.fori_loop(0, query_blocks, look, (jnp.int32(0),) * per_band, unroll=8)
        order = [jnp.int32(0)] * KEEP
        count = jnp.int32(0)
        for j in range(per_band):
            for e in range(KEEP):
                order[e] = jnp.where((seen[j] > 0) & (count == e), j, order[e])
            count = count + seen[j]
        for e in range(KEEP):
            source = pl.ds(pl.multiple_of(order[e] * BLK, BLK), BLK)
            copy = pltpu.make_async_copy(tok_ref.at[source, :], tok.at[pl.ds(e * BLK, BLK), :], sems.at[e])
            copy.start()
            copies.append(copy)
        for copy in copies:
            copy.wait()
        keys = dot_f32(tok[...], wk[...])
        values = dot_f32(tok[...], wv[...])
        low = low_lanes((rows, LANES))
        for p in range(pairs):
            cols = slice(p * LANES, (p + 1) * LANES)
            k, v = keys[:, cols], values[:, cols]
            outs[p][0] = jnp.where(low, k, swap_halves(v)).astype(jnp.bfloat16)
            outs[p][1] = jnp.where(low, swap_halves(k), v).astype(jnp.bfloat16)

    return pl.pallas_call(
        kernel,
        out_shape=[jax.ShapeDtypeStruct((2, rows, LANES), jnp.bfloat16)] * pairs,
        grid_spec=pltpu.PrefetchScalarGridSpec(
            num_scalar_prefetch=2,
            grid=(),
            in_specs=[ANY, ANY, ANY],
            out_specs=[VMEM] * pairs,
            scratch_shapes=[
                pltpu.VMEM((rows, width), jnp.bfloat16),
                pltpu.VMEM(w_key.shape, jnp.bfloat16),
                pltpu.VMEM(w_value.shape, jnp.bfloat16),
                pltpu.SemaphoreType.DMA((KEEP + 2,)),
            ],
        ),
        compiler_params=PARAMS,
        name="project_kv",
    )(place, block_mask, tokens, w_key, w_value)


def project_q(place, tokens, w_query, parts):
    rows, width = tokens.shape
    pairs = w_query.shape[1] // LANES
    part = rows // parts

    def kernel(place_ref, tok_ref, w_ref, *outs):
        me = place_ref[1]
        for k in range(parts):
            begin = pl.multiple_of((me ^ k) * part, part)
            q = dot_f32(tok_ref[pl.ds(begin, part), :], w_ref[...]) * QUERY_SCALE
            lane = lax.broadcasted_iota(jnp.int32, (part, LANES), 1)
            row = lax.broadcasted_iota(jnp.int32, (part, LANES), 0) + begin
            hot = (lane == HD + row // BLK).astype(jnp.float32)
            at = pl.ds(k * part, part)
            for p in range(pairs):
                pair = q[:, p * LANES : (p + 1) * LANES]
                outs[p][0, at, :] = jnp.where(lane < HD, pair, hot).astype(jnp.bfloat16)
                outs[p][1, at, :] = jnp.where(lane < HD, swap_halves(pair), hot).astype(jnp.bfloat16)

    return pl.pallas_call(
        kernel,
        out_shape=[jax.ShapeDtypeStruct((2, rows, LANES), jnp.bfloat16)] * pairs,
        grid_spec=pltpu.PrefetchScalarGridSpec(
            num_scalar_prefetch=1, grid=(), in_specs=[VMEM, VMEM], out_specs=[VMEM] * pairs
        ),
        compiler_params=PARAMS,
        cost_estimate=pl.CostEstimate(flops=2 * rows * width * w_query.shape[1], bytes_accessed=3 * 2**20, transcendentals=0),
        name="project_q",
    )(place, tokens, w_query)


def attend(queries, sources, bias, parts):
    rows = queries.shape[1]
    part = rows // parts
    held = KEEP * BLK
    total = held * len(sources)

    def kernel(q_ref, bias_ref, *rest):
        srcs = rest[: len(sources)]
        outs = rest[len(sources) : len(sources) + parts]
        table, key_tab, value_tab, sems = rest[len(sources) + parts :]
        copies = []
        for s, src in enumerate(srcs):
            copy = pltpu.make_async_copy(src, table.at[:, pl.ds(s * held, held), :], sems.at[s])
            copy.start()
            copies.append(copy)
        low = low_lanes((BLK, LANES)).astype(jnp.float32).astype(jnp.bfloat16)
        high = (1.0 - low_lanes((BLK, LANES)).astype(jnp.float32)).astype(jnp.bfloat16)
        for s in range(len(srcs)):
            copies[s].wait()
            for e in range(KEEP):
                block = s * KEEP + e
                at = pl.ds(block * BLK, BLK)
                add = jnp.broadcast_to(bias_ref[block : block + 1, :], (BLK, LANES)).astype(jnp.bfloat16)
                for h in range(2):
                    kv = table[h, at, :]
                    key_tab[h, at, :] = kv * low + add
                    value_tab[h, at, :] = kv * high + low
        sums = []
        for h in range(2):
            q = q_ref[h]
            peak = jnp.full((rows, 1), LOWEST, jnp.float32)
            total_sum = jnp.zeros((rows, LANES), jnp.float32)
            for c in range(-(-total // CHUNK)):
                at = pl.ds(c * CHUNK, min(CHUNK, total - c * CHUNK))
                scores = lax.dot_general(
                    q, key_tab[h, at, :], (((1,), (1,)), ((), ())), preferred_element_type=jnp.float32
                )
                new_peak = jnp.maximum(peak, jnp.max(scores, axis=1, keepdims=True))
                weights = jnp.exp2(scores - new_peak).astype(jnp.bfloat16)
                total_sum = total_sum * jnp.exp2(peak - new_peak) + dot_f32(weights, value_tab[h, at, :])
                peak = new_peak
            sums.append(total_sum)
        first, second = sums
        low = low_lanes((rows, LANES))
        top = jnp.where(low, swap_halves(first), second)
        mass = jnp.where(low, first, swap_halves(second))
        out = (top / mass).astype(jnp.bfloat16)
        for k in range(parts):
            outs[k][...] = out[k * part : (k + 1) * part, :]

    return pl.pallas_call(
        kernel,
        out_shape=[jax.ShapeDtypeStruct((part, LANES), jnp.bfloat16)] * parts,
        in_specs=[VMEM, VMEM] + [ANY] * len(sources),
        out_specs=[VMEM] * parts,
        scratch_shapes=[
            pltpu.VMEM((2, total, LANES), jnp.bfloat16),
            pltpu.VMEM((2, total, LANES), jnp.bfloat16),
            pltpu.VMEM((2, total, LANES), jnp.bfloat16),
            pltpu.SemaphoreType.DMA((len(sources),)),
        ],
        compiler_params=PARAMS,
        cost_estimate=pl.CostEstimate(flops=2 * rows * total * 1024, bytes_accessed=8 * 2**20, transcendentals=2 * rows * total),
        name="attend",
    )(queries, bias, *sources)


def project_out(place, attended, w_slots):
    parts, pairs = len(attended), len(attended[0])
    rows = attended[0][0].shape[0]
    slots = len(w_slots)
    piece, width = w_slots[0].shape[1:]
    depth = parts * pairs * LANES

    def kernel(place_ref, *rest):
        parts_in = rest[: parts * pairs]
        w_refs = rest[parts * pairs : parts * pairs + slots]
        out_ref, w, sems = rest[parts * pairs + slots :]
        mine = place_ref[2]
        copies = []
        for s in range(slots):
            for k in range(parts):
                begin = pl.multiple_of(k * pairs * LANES + (mine ^ s) * piece, piece)
                copy = pltpu.make_async_copy(w_refs[s].at[k], w.at[pl.ds(begin, piece), :], sems.at[s * parts + k])
                copy.start()
                copies.append(copy)
        rows_all = jnp.concatenate([ref[...] for ref in parts_in], axis=1)
        for copy in copies:
            copy.wait()
        out_ref[...] = dot_f32(rows_all, w[...]).astype(jnp.bfloat16)

    return pl.pallas_call(
        kernel,
        out_shape=jax.ShapeDtypeStruct((rows, width), jnp.bfloat16),
        grid_spec=pltpu.PrefetchScalarGridSpec(
            num_scalar_prefetch=1,
            grid=(),
            in_specs=[VMEM] * (parts * pairs) + [ANY] * slots,
            out_specs=VMEM,
            scratch_shapes=[
                pltpu.VMEM((depth, width), jnp.bfloat16),
                pltpu.SemaphoreType.DMA((slots * parts,)),
            ],
        ),
        compiler_params=PARAMS,
        name="project_out",
    )(place, *[a for group in attended for a in group], *w_slots)


def score_bias(block_mask, source_bands, bands, per_band, band):
    used = jnp.max(block_mask, axis=0).reshape(bands, per_band)
    rank = jnp.cumsum(used, axis=1) - 1
    slot = jnp.arange(KEEP, dtype=jnp.int32)
    chosen = (used[:, None, :] > 0) & (rank[:, None, :] == slot[None, :, None])
    chosen = jnp.take(chosen, source_bands, axis=0)
    rows = lax.dynamic_slice_in_dim(block_mask, band * per_band, per_band, 0)
    rows = jnp.take(rows.reshape(per_band, bands, per_band), source_bands, axis=1)
    allowed = jnp.any(chosen[:, :, :, None] & (rows.transpose(1, 2, 0)[:, None] > 0), axis=2)
    bias = jnp.where(allowed, 0.0, NEG).astype(jnp.float32).reshape(-1, per_band)
    return jnp.pad(bias, ((0, 0), (HD, LANES - HD - per_band)))


def on_device(sizes, tokens, w_query, w_key, w_value, w_out, block_mask):
    tiles, bands, heads = sizes
    band, head = lax.axis_index("band"), lax.axis_index("head")
    tile = lax.axis_index("tiles")
    per_band = tokens.shape[0] // BLK
    core = band % 2
    quarters = 2 * tiles
    quarter = core * tiles + tile
    place = jnp.stack([band, head, quarter]).astype(jnp.int32)

    def along_band(array, goes_to):
        return lax.ppermute(array, "band", [(i, goes_to(i)) for i in range(bands)])

    def along_head(array, k):
        return lax.ppermute(array, "head", [(i, i ^ k) for i in range(heads)])

    kv = project_kv(place, block_mask, tokens, w_key, w_value)
    pairs = len(kv)
    source_bands = [band, band ^ 1]
    tables = []
    for p in range(pairs):
        own = [kv[p]]
        for r in range(1, bands // 2):
            own.append(along_band(kv[p], lambda i: (i + 2 * r) % bands))
        tables.append([a for o in own for a in (o, along_band(o, lambda i: i ^ 1))])
    for r in range(1, bands // 2):
        far = (band + bands - 2 * r) % bands
        source_bands += [far, far ^ 1]
    queries = project_q(place, tokens, w_query, heads)
    bias = score_bias(block_mask, jnp.stack(source_bands), bands, per_band, band)

    piece = w_out.shape[0] // quarters
    w_mine = lax.dynamic_slice_in_dim(w_out, quarter * piece, piece, 0)
    w_own = jnp.stack([w_mine] + [along_head(w_mine, k) for k in range(1, heads)])
    w_tile = [w_own] + [
        lax.ppermute(w_own, "tiles", [(i, i ^ s) for i in range(tiles)]) for s in range(1, tiles)
    ]
    w_slots = w_tile + [along_band(w, lambda i: i ^ 1) for w in w_tile]

    attended = [[] for _ in range(heads)]
    for p in range(pairs):
        pieces = attend(queries[p], tables[p], bias, heads)
        attended[0].append(pieces[0])
        for k in range(1, heads):
            attended[k].append(along_head(pieces[k], k))
    return project_out(place, attended, w_slots)


def solution(mesh):
    sizes = tuple(mesh.shape[axis] for axis in ("tiles", "band", "head"))
    return jax.shard_map(
        functools.partial(on_device, sizes),
        mesh=mesh,
        in_specs=(
            P(("tiles", "band"), None),
            P(None, "head"),
            P(None, "head"),
            P(None, "head"),
            P("head", None),
            P("tiles", None),
        ),
        out_specs=P(("tiles", "band", "head"), None),
        check_vma=False,
    )
```

time: 418 us -> 78.8 us (0.19)
  local copies, waits for them, and re-layouts: 120 us -> 2.89 us
  other arithmetic: 118 us -> 1.29 us
  matrix products: 89.7 us -> 0 us
  waiting for transfers between devices: 72.6 us -> 18.6 us
  Pallas kernels: 0 us -> 36.1 us
  starting transfers between devices: 0.04 us -> 19.1 us
  between operations: 14.2 us -> 0.42 us
    dot_general x10 -> x0, matrix products: 89.7 us -> none  [the longest x3 43.6 us: one_turn(): jnp.einsum('prhk,pkhd->prhd', weights, value_rows, preferred_element_type...]
    slice x9 -> x0, local copies, waits for them, and re-layouts: 56.3 us -> none  [the longest x6 37.2 us: one_turn(): pair_rows[:, :, local_cols:].reshape(per_turn, -1, head_count, head_dim)]
    gather x16 -> x2, local copies, waits for them, and re-layouts: 55.4 us -> 1.11 us  [the longest x1 0.56 us: score_bias(): chosen = jnp.take(chosen, source_bands, axis=0)]
    scatter-add x6 -> x0, other arithmetic: 45.5 us -> none  [the longest x3 36.8 us: one_turn(): jax.ops.segment_sum(sum_terms, owners, num_segments=item_count)]
    reduce_scatter x1 -> x0, waiting for transfers between devices: 43.1 us -> none  [on_device(): lax.psum_scatter(jnp.dot(attended, w_out, preferred_element_type=jnp.floa...]
    pallas_call x0 -> x5, Pallas kernels: none -> 36.1 us  [the longest x2 21.7 us: attend(): pl.pallas_call(kernel, out_shape=[jax.ShapeDtypeStruct((part, LANES), jnp...]
    reduce_sum x3 -> x0, other arithmetic: 32.2 us -> none  [one_turn(): row_mass = jnp.sum(exponent, axis=3)]
    all_gather x1 -> x0, waiting for transfers between devices: 29.4 us -> none  [on_device(): lax.all_gather(key_value, 'band', axis=0, tiled=True)]
  transfers between devices with their start and end apart: 2 -> 18, of which waited for: 2 -> 5; matrix products, arithmetic and copies ran while one was open for 2% -> 4% of each run, Pallas kernels for 0% -> 33%
where the time goes in v1:
time: 78.8 us; the launch traced here: 78.4 us
  Pallas kernels  36.1 us (46%)
  starting transfers between devices  19.1 us (24%)
  waiting for transfers between devices  18.6 us (24%)
  local copies, waits for them, and re-layouts  2.89 us (4%)
  other arithmetic  1.29 us (2%)
    pallas_call x2, Pallas kernels, attend(): pl.pallas_call(kernel, out_shape=[jax.ShapeDtypeStruct((part, LANES), jnp...  21.7 us
    ppermute x9, starting transfers between devices, along_head(): return lax.ppermute(array, 'head', [(i, i ^ k) for i in range(heads)])  13.3 us
    ppermute x9, waiting for transfers between devices, along_head(): return lax.ppermute(array, 'head', [(i, i ^ k) for i in range(heads)])  11.9 us
    ppermute x1, waiting for transfers between devices, on_device(): lax.ppermute(w_own, 'tiles', [(i, i ^ s) for i in range(tiles)])  6.73 us
    pallas_call x1, Pallas kernels, project_kv(): pl.pallas_call(kernel, out_shape=[jax.ShapeDtypeStruct((2, rows, LANES),...  5.07 us
    pallas_call x1, Pallas kernels, project_out(): pl.pallas_call(kernel, out_shape=jax.ShapeDtypeStruct((rows, width), jnp....  4.97 us
    pallas_call x1, Pallas kernels, project_q(): pl.pallas_call(kernel, out_shape=[jax.ShapeDtypeStruct((2, rows, LANES),...  4.37 us
    ppermute x8, starting transfers between devices, along_band(): return lax.ppermute(array, 'band', [(i, goes_to(i)) for i in range(bands)])  4.13 us
  transfers between devices with their start and end apart: 18, of which 5 were waited for; matrix products, arithmetic and copies ran while one was open for 4% of the time, Pallas kernels for 33%

profile of v1, /device:TPU:0, one launch (start us, length us, event | category | flops | bytes accessed | tf_op | source)
XLA Modules:
  0.0 78.4 jit_solution(10243193185623250700)
XLA Ops:
  0.0 0.6 pad_add_fusion.place_ref
  0.6 5.1 %project_kv.1 = (bf16[2,768,128]{2,1,0:T(8,128)(2,1)}, bf16[2,768,128]{2,1,0:T(8,128)(2,1)}) custom-call(s32[3]{0:T(128)} %pad_add_fusion.place_ref, s32[32,32]{1,0:T(8,128)} %mask_ref.1, bf16[1024,1024]{1,0:T(8,128)(2,1)} %tok_ref.3, bf16[1024,256]{1,0:T(8,128)(2,1)} %wk_ref.1, bf16[1024,256]{1,0:T(8,128)(2,1)} %wv_ref.1), custom_call_target="tpu_custom_call" | custom-call | tf_op jit(solution)/shard_map/project_kv/pallas_call | solution.py:80
  5.6 3.0 %collective-permute-start.4 = (bf16[2,768,128]{2,1,0:T(8,128)(2,1)}, bf16[2,768,128]{2,1,0:T(8,128)(2,1)S(1)}, u32[]{:S(2)}, u32[]{:S(2)}) collective-permute-start(bf16[2,768,128]{2,1,0:T(8,128)(2,1)} %get-tuple-element.21.rest_0_), channel_id=1, source_target_pairs={{0,8},{4,12},{8,0},{12,4},{1,9},{5,13},{9,1},{13,5},{2,10},{6,14},... | collective-permute-start | bytes 1179656 | tf_op jit(solution)/shard_map/ppermute | solution.py:264
  8.7 1.6 %collective-permute-start.12 = (bf16[64,1024]{1,0:T(8,128)(2,1)S(1)}, bf16[64,1024]{1,0:T(8,128)(2,1)S(1)}, u32[]{:S(2)}, u32[]{:S(2)}) collective-permute-start(bf16[64,1024]{1,0:T(8,128)(2,1)S(1)} %constant_dynamic-slice_fusion), channel_id=1, source_target_pairs={{0,1},{1,0},{2,3},{3,2},{4,5},{5,4},{6,7},{7,6},{8,9},{9,8},{10,11... | collective-permute-start | bytes 393224 | tf_op jit(solution)/shard_map/ppermute | solution.py:267
  10.3 2.6 %collective-permute-start.13 = (bf16[64,1024]{1,0:T(8,128)(2,1)S(1)}, bf16[64,1024]{1,0:T(8,128)(2,1)S(1)}, u32[]{:S(2)}, u32[]{:S(2)}) collective-permute-start(bf16[64,1024]{1,0:T(8,128)(2,1)S(1)} %constant_dynamic-slice_fusion), channel_id=1, source_target_pairs={{0,2},{1,3},{2,0},{3,1},{4,6},{5,7},{6,4},{7,5},{8,10},{9,11},{10,... | collective-permute-start | bytes 393224 | tf_op jit(solution)/shard_map/ppermute | solution.py:267
  12.9 0.2 collective-permute-start.14
  13.1 0.1 broadcast_in_dim_reshape.3
  13.2 0.2 reduce_window_sum.11
  13.4 0.1 fusion.2
  13.5 0.1 reshape.210
  13.6 0.6 gather_fusion.1
  14.2 0.1 compare_and_fusion
  14.3 0.1 fusion.1
  14.4 0.1 copy.13
  14.5 0.6 gather_fusion
  15.0 1.9 %collective-permute-done.12 = bf16[64,1024]{1,0:T(8,128)(2,1)S(1)} collective-permute-done((bf16[64,1024]{1,0:T(8,128)(2,1)S(1)}, bf16[64,1024]{1,0:T(8,128)(2,1)S(1)}, u32[]{:S(2)}, u32[]{:S(2)}) %collective-permute-start.12) | collective-permute-done | bytes 131104 | tf_op jit(solution)/shard_map/ppermute | solution.py:267
  17.0 0.3 collective-permute-start.1
  17.3 5.9 %collective-permute-done.13 = bf16[64,1024]{1,0:T(8,128)(2,1)S(1)} collective-permute-done((bf16[64,1024]{1,0:T(8,128)(2,1)S(1)}, bf16[64,1024]{1,0:T(8,128)(2,1)S(1)}, u32[]{:S(2)}, u32[]{:S(2)}) %collective-permute-start.13) | collective-permute-done | bytes 131104 | tf_op jit(solution)/shard_map/ppermute | solution.py:267
  23.2 0.0 collective-permute-start
  23.2 0.0 collective-permute-done.14
  23.2 0.1 pad_maximum_fusion.rest_8_
  23.3 1.6 %collective-permute-start.15 = (bf16[4,64,1024]{2,1,0:T(8,128)(2,1)S(1)}, bf16[4,64,1024]{2,1,0:T(8,128)(2,1)S(1)}, u32[]{:S(2)}, u32[]{:S(2)}) collective-permute-start(bf16[4,64,1024]{2,1,0:T(8,128)(2,1)S(1)} %pad_maximum_fusion.rest_8_), channel_id=1, source_target_pairs={{0,16},{16,0},{1,17},{17,1},{2,18},{18,2},{3,19},{19,3},{4,20},{20... | collective-permute-start | bytes 1572872 | tf_op jit(solution)/shard_map/ppermute | solution.py:288
  24.9 0.1 broadcast_select_fusion.1
  24.9 0.0 collective-permute-done.4.rest_2_
  25.0 0.3 collective-permute-start.5
  25.2 0.1 and_reduce_fusion
  25.4 0.7 pad.4.bias_ref
  26.1 4.4 %project_q.1 = (bf16[2,1024,128]{2,1,0:T(8,128)(2,1)}, bf16[2,1024,128]{2,1,0:T(8,128)(2,1)}) custom-call(s32[3]{0:T(128)} %pad_add_fusion.place_ref, bf16[1024,1024]{1,0:T(8,128)(2,1)} %tok_ref.3, bf16[1024,256]{1,0:T(8,128)(2,1)} %w_ref.1), custom_call_target="tpu_custom_call" | custom-call | flops 536870912 | bytes 3145728 | tf_op jit(solution)/shard_map/project_q/pallas_call | solution.py:119
  30.4 0.0 collective-permute-done.3.rest_1_
  30.4 0.3 collective-permute-start.16
  30.7 0.0 collective-permute-done.1.rest_2_
  30.7 0.2 collective-permute-start.2
  31.0 6.7 %collective-permute-done.15.rest_9_ = bf16[4,64,1024]{2,1,0:T(8,128)(2,1)S(1)} collective-permute-done((bf16[4,64,1024]{2,1,0:T(8,128)(2,1)S(1)}, bf16[4,64,1024]{2,1,0:T(8,128)(2,1)S(1)}, u32[]{:S(2)}, u32[]{:S(2)}) %collective-permute-start.15) | collective-permute-done | bytes 524320 | tf_op jit(solution)/shard_map/ppermute | solution.py:288
  37.7 10.8 %attend.3 = (bf16[256,128]{1,0:T(8,128)(2,1)}, bf16[256,128]{1,0:T(8,128)(2,1)}, bf16[256,128]{1,0:T(8,128)(2,1)}, bf16[256,128]{1,0:T(8,128)(2,1)}) custom-call(bf16[2,1024,128]{2,1,0:T(8,128)(2,1)} %get-tuple-element.20.q_ref, f32[24,128]{1,0:T(8,128)} %pad.4.bias_ref, bf16[2,768,128]{2,1,0:T(8,128)(2,1)} %get-tuple-element.21.rest_0_, ...), custom_call_target="tpu_custom_call" | custom-call | flops 6442450944 | bytes 8388608 | tf_op jit(solution)/shard_map/attend/pallas_call | solution.py:181
  48.6 2.5 %collective-permute-start.11 = (bf16[256,128]{1,0:T(8,128)(2,1)}, bf16[256,128]{1,0:T(8,128)(2,1)S(1)}, u32[]{:S(2)}, u32[]{:S(2)}) collective-permute-start(bf16[256,128]{1,0:T(8,128)(2,1)} %get-tuple-element.28), channel_id=1, source_target_pairs={{0,3},{1,2},{2,1},{3,0},{4,7},{5,6},{6,5},{7,4},{8,11},{9,10},{10,... | collective-permute-start | bytes 196616 | tf_op jit(solution)/shard_map/ppermute | solution.py:267
  51.1 0.0 collective-permute-done.rest_1_
  51.1 0.7 collective-permute-start.7
  51.8 0.0 collective-permute-done.2.rest_3_
  51.8 1.3 %collective-permute-start.9 = (bf16[256,128]{1,0:T(8,128)(2,1)}, bf16[256,128]{1,0:T(8,128)(2,1)S(1)}, u32[]{:S(2)}, u32[]{:S(2)}) collective-permute-start(bf16[256,128]{1,0:T(8,128)(2,1)} %get-tuple-element.26), channel_id=1, source_target_pairs={{0,2},{1,3},{2,0},{3,1},{4,6},{5,7},{6,4},{7,5},{8,10},{9,11},{10,... | collective-permute-start | bytes 196616 | tf_op jit(solution)/shard_map/ppermute | solution.py:267
  53.1 10.9 %attend.2 = (bf16[256,128]{1,0:T(8,128)(2,1)}, bf16[256,128]{1,0:T(8,128)(2,1)}, bf16[256,128]{1,0:T(8,128)(2,1)}, bf16[256,128]{1,0:T(8,128)(2,1)}) custom-call(bf16[2,1024,128]{2,1,0:T(8,128)(2,1)} %get-tuple-element.17.q_ref, f32[24,128]{1,0:T(8,128)} %pad.4.bias_ref, bf16[2,768,128]{2,1,0:T(8,128)(2,1)} %get-tuple-element.18.rest_0_, ...), custom_call_target="tpu_custom_call" | custom-call | flops 6442450944 | bytes 8388608 | tf_op jit(solution)/shard_map/attend/pallas_call | solution.py:181
  63.9 2.5 %collective-permute-start.10 = (bf16[256,128]{1,0:T(8,128)(2,1)}, bf16[256,128]{1,0:T(8,128)(2,1)S(1)}, u32[]{:S(2)}, u32[]{:S(2)}) collective-permute-start(bf16[256,128]{1,0:T(8,128)(2,1)} %get-tuple-element.27), channel_id=1, source_target_pairs={{0,3},{1,2},{2,1},{3,0},{4,7},{5,6},{6,5},{7,4},{8,11},{9,10},{10,... | collective-permute-start | bytes 196616 | tf_op jit(solution)/shard_map/ppermute | solution.py:267
  66.5 1.9 %collective-permute-start.8 = (bf16[256,128]{1,0:T(8,128)(2,1)}, bf16[256,128]{1,0:T(8,128)(2,1)S(1)}, u32[]{:S(2)}, u32[]{:S(2)}) collective-permute-start(bf16[256,128]{1,0:T(8,128)(2,1)} %get-tuple-element.25), channel_id=1, source_target_pairs={{0,2},{1,3},{2,0},{3,1},{4,6},{5,7},{6,4},{7,5},{8,10},{9,11},{10,... | collective-permute-start | bytes 196616 | tf_op jit(solution)/shard_map/ppermute | solution.py:267
  68.4 2.1 %collective-permute-done.10.rest_6_ = bf16[256,128]{1,0:T(8,128)(2,1)S(1)} collective-permute-done((bf16[256,128]{1,0:T(8,128)(2,1)}, bf16[256,128]{1,0:T(8,128)(2,1)S(1)}, u32[]{:S(2)}, u32[]{:S(2)}) %collective-permute-start.10) | collective-permute-done | bytes 65568 | tf_op jit(solution)/shard_map/ppermute | solution.py:267
  70.5 1.9 %collective-permute-done.6.rest_2_ = bf16[256,128]{1,0:T(8,128)(2,1)S(1)} collective-permute-done((bf16[256,128]{1,0:T(8,128)(2,1)}, bf16[256,128]{1,0:T(8,128)(2,1)S(1)}, u32[]{:S(2)}, u32[]{:S(2)}) %collective-permute-start.6) | collective-permute-done | bytes 65568 | tf_op jit(solution)/shard_map/ppermute | solution.py:267
  72.5 0.5 copy-done.10
  73.0 0.0 copy-done.11
  73.0 0.2 copy-done.4
  73.2 5.0 %project_out.1 = bf16[256,1024]{1,0:T(8,128)(2,1)} custom-call(s32[3]{0:T(128)} %pad_add_fusion.place_ref, bf16[256,128]{1,0:T(8,128)(2,1)} %get-tuple-element.19.rest_0_, bf16[256,128]{1,0:T(8,128)(2,1)} %get-tuple-element.22.rest_1_, bf16[256,128]{1,0:T(8,128)(2,1)} %copy-done.10, bf16[256,128]{1,0:T(8,128)(2,1)} %copy-done.7, ...), custom_call_target="tpu_custom_call" | custom-call | tf_op jit(solution)/shard_map/project_out/pallas_call | solution.py:222
  (52 shorter events, 0.2 us)
Async XLA Ops:
  0.0 8.6 %copy-start = (bf16[256,1024]{1,0:T(8,128)(2,1)S(1)}, bf16[256,1024]{1,0:T(8,128)(2,1)}, u32[]{:S(2)}) copy-start(bf16[256,1024]{1,0:T(8,128)(2,1)} %param.10) | copy-start | bytes 1572868
  0.0 13.1 %copy-start.5 = (s32[32,32]{1,0:T(8,128)S(1)}, s32[32,32]{1,0:T(8,128)}, u32[]{:S(2)}) copy-start(s32[32,32]{1,0:T(8,128)} %mask_ref.1) | copy-start | bytes 12292
  5.6 19.3 %collective-permute-start.4 = (bf16[2,768,128]{2,1,0:T(8,128)(2,1)}, bf16[2,768,128]{2,1,0:T(8,128)(2,1)S(1)}, u32[]{:S(2)}, u32[]{:S(2)}) collective-permute-start(bf16[2,768,128]{2,1,0:T(8,128)(2,1)} %get-tuple-element.21.rest_0_), channel_id=1, source_target_pairs={{0,8},{4,12},{8,0},{12,4},{1,9},{5,13},{9,1},{13,5},{2,10},{6,14},... | collective-permute-start | bytes 1179656 | tf_op jit(solution)/shard_map/ppermute | solution.py:264
  8.6 21.8 %collective-permute-start.3 = (bf16[2,768,128]{2,1,0:T(8,128)(2,1)}, bf16[2,768,128]{2,1,0:T(8,128)(2,1)S(1)}, u32[]{:S(2)}, u32[]{:S(2)}) collective-permute-start(bf16[2,768,128]{2,1,0:T(8,128)(2,1)} %get-tuple-element.21.rest_0_), channel_id=1, source_target_pairs={{0,4},{4,0},{8,12},{12,8},{1,5},{5,1},{9,13},{13,9},{2,6},{6,2},{1... | collective-permute-start | bytes 1179656 | tf_op jit(solution)/shard_map/ppermute | solution.py:264
  8.7 8.3 %collective-permute-start.12 = (bf16[64,1024]{1,0:T(8,128)(2,1)S(1)}, bf16[64,1024]{1,0:T(8,128)(2,1)S(1)}, u32[]{:S(2)}, u32[]{:S(2)}) collective-permute-start(bf16[64,1024]{1,0:T(8,128)(2,1)S(1)} %constant_dynamic-slice_fusion), channel_id=1, source_target_pairs={{0,1},{1,0},{2,3},{3,2},{4,5},{5,4},{6,7},{7,6},{8,9},{9,8},{10,11... | collective-permute-start | bytes 393224 | tf_op jit(solution)/shard_map/ppermute | solution.py:267
  10.3 12.9 %collective-permute-start.13 = (bf16[64,1024]{1,0:T(8,128)(2,1)S(1)}, bf16[64,1024]{1,0:T(8,128)(2,1)S(1)}, u32[]{:S(2)}, u32[]{:S(2)}) collective-permute-start(bf16[64,1024]{1,0:T(8,128)(2,1)S(1)} %constant_dynamic-slice_fusion), channel_id=1, source_target_pairs={{0,2},{1,3},{2,0},{3,1},{4,6},{5,7},{6,4},{7,5},{8,10},{9,11},{10,... | collective-permute-start | bytes 393224 | tf_op jit(solution)/shard_map/ppermute | solution.py:267
  12.9 10.3 %collective-permute-start.14 = (bf16[64,1024]{1,0:T(8,128)(2,1)S(1)}, bf16[64,1024]{1,0:T(8,128)(2,1)S(1)}, u32[]{:S(2)}, u32[]{:S(2)}) collective-permute-start(bf16[64,1024]{1,0:T(8,128)(2,1)S(1)} %constant_dynamic-slice_fusion), channel_id=1, source_target_pairs={{0,3},{1,2},{2,1},{3,0},{4,7},{5,6},{6,5},{7,4},{8,11},{9,10},{10,... | collective-permute-start | bytes 393224 | tf_op jit(solution)/shard_map/ppermute | solution.py:267
  17.0 13.8 %collective-permute-start.1 = (bf16[2,768,128]{2,1,0:T(8,128)(2,1)}, bf16[2,768,128]{2,1,0:T(8,128)(2,1)S(1)}, u32[]{:S(2)}, u32[]{:S(2)}) collective-permute-start(bf16[2,768,128]{2,1,0:T(8,128)(2,1)} %get-tuple-element.18.rest_0_), channel_id=1, source_target_pairs={{0,8},{4,12},{8,0},{12,4},{1,9},{5,13},{9,1},{13,5},{2,10},{6,14},... | collective-permute-start | bytes 1179656 | tf_op jit(solution)/shard_map/ppermute | solution.py:264
  23.2 27.9 %collective-permute-start = (bf16[2,768,128]{2,1,0:T(8,128)(2,1)}, bf16[2,768,128]{2,1,0:T(8,128)(2,1)S(1)}, u32[]{:S(2)}, u32[]{:S(2)}) collective-permute-start(bf16[2,768,128]{2,1,0:T(8,128)(2,1)} %get-tuple-element.18.rest_0_), channel_id=1, source_target_pairs={{0,4},{4,0},{8,12},{12,8},{1,5},{5,1},{9,13},{13,9},{2,6},{6,2},{1... | collective-permute-start | bytes 1179656 | tf_op jit(solution)/shard_map/ppermute | solution.py:264
  23.3 25.3 %copy-start.1 = (bf16[4,64,1024]{2,1,0:T(8,128)(2,1)}, bf16[4,64,1024]{2,1,0:T(8,128)(2,1)S(1)}, u32[]{:S(2)}) copy-start(bf16[4,64,1024]{2,1,0:T(8,128)(2,1)S(1)} %pad_maximum_fusion.rest_8_) | copy-start | bytes 1572868
  23.3 14.4 %collective-permute-start.15 = (bf16[4,64,1024]{2,1,0:T(8,128)(2,1)S(1)}, bf16[4,64,1024]{2,1,0:T(8,128)(2,1)S(1)}, u32[]{:S(2)}, u32[]{:S(2)}) collective-permute-start(bf16[4,64,1024]{2,1,0:T(8,128)(2,1)S(1)} %pad_maximum_fusion.rest_8_), channel_id=1, source_target_pairs={{0,16},{16,0},{1,17},{17,1},{2,18},{18,2},{3,19},{19,3},{4,20},{20... | collective-permute-start | bytes 1572872 | tf_op jit(solution)/shard_map/ppermute | solution.py:288
  25.0 12.8 %copy-start.12 = (bf16[2,768,128]{2,1,0:T(8,128)(2,1)}, bf16[2,768,128]{2,1,0:T(8,128)(2,1)S(1)}, u32[]{:S(2)}) copy-start(bf16[2,768,128]{2,1,0:T(8,128)(2,1)S(1)} %collective-permute-done.4.rest_2_) | copy-start | bytes 1179652
  25.0 12.7 %collective-permute-start.5 = (bf16[2,768,128]{2,1,0:T(8,128)(2,1)S(1)}, bf16[2,768,128]{2,1,0:T(8,128)(2,1)}, u32[]{:S(2)}, u32[]{:S(2)}) collective-permute-start(bf16[2,768,128]{2,1,0:T(8,128)(2,1)S(1)} %collective-permute-done.4.rest_2_), channel_id=1, source_target_pairs={{0,4},{4,0},{8,12},{12,8},{1,5},{5,1},{9,13},{13,9},{2,6},{6,2},{1... | collective-permute-start | bytes 1179656 | tf_op jit(solution)/shard_map/ppermute | solution.py:264
  30.4 7.3 %copy-start.13 = (bf16[2,768,128]{2,1,0:T(8,128)(2,1)}, bf16[2,768,128]{2,1,0:T(8,128)(2,1)S(1)}, u32[]{:S(2)}) copy-start(bf16[2,768,128]{2,1,0:T(8,128)(2,1)S(1)} %collective-permute-done.3.rest_1_) | copy-start | bytes 1179652
  30.4 33.5 %collective-permute-start.16 = (bf16[4,64,1024]{2,1,0:T(8,128)(2,1)S(1)}, bf16[4,64,1024]{2,1,0:T(8,128)(2,1)S(1)}, u32[]{:S(2)}, u32[]{:S(2)}) collective-permute-start(bf16[4,64,1024]{2,1,0:T(8,128)(2,1)S(1)} %pad_maximum_fusion.rest_8_), channel_id=1, source_target_pairs={{0,4},{4,0},{8,12},{12,8},{1,5},{5,1},{9,13},{13,9},{2,6},{6,2},{1... | collective-permute-start | bytes 1572872 | tf_op jit(solution)/shard_map/ppermute | solution.py:264
  30.7 17.8 %copy-start.14 = (bf16[2,768,128]{2,1,0:T(8,128)(2,1)}, bf16[2,768,128]{2,1,0:T(8,128)(2,1)S(1)}, u32[]{:S(2)}) copy-start(bf16[2,768,128]{2,1,0:T(8,128)(2,1)S(1)} %collective-permute-done.1.rest_2_) | copy-start | bytes 1179652
  30.7 21.1 %collective-permute-start.2 = (bf16[2,768,128]{2,1,0:T(8,128)(2,1)S(1)}, bf16[2,768,128]{2,1,0:T(8,128)(2,1)S(1)}, u32[]{:S(2)}, u32[]{:S(2)}) collective-permute-start(bf16[2,768,128]{2,1,0:T(8,128)(2,1)S(1)} %collective-permute-done.1.rest_2_), channel_id=1, source_target_pairs={{0,4},{4,0},{8,12},{12,8},{1,5},{5,1},{9,13},{13,9},{2,6},{6,2},{1... | collective-permute-start | bytes 1179656 | tf_op jit(solution)/shard_map/ppermute | solution.py:264
  37.7 10.9 %copy-start.2 = (bf16[4,64,1024]{2,1,0:T(8,128)(2,1)}, bf16[4,64,1024]{2,1,0:T(8,128)(2,1)S(1)}, u32[]{:S(2)}) copy-start(bf16[4,64,1024]{2,1,0:T(8,128)(2,1)S(1)} %collective-permute-done.15.rest_9_) | copy-start | bytes 1572868
  37.7 34.7 %collective-permute-start.17 = (bf16[4,64,1024]{2,1,0:T(8,128)(2,1)S(1)}, bf16[4,64,1024]{2,1,0:T(8,128)(2,1)S(1)}, u32[]{:S(2)}, u32[]{:S(2)}) collective-permute-start(bf16[4,64,1024]{2,1,0:T(8,128)(2,1)S(1)} %collective-permute-done.15.rest_9_), channel_id=1, source_target_pairs={{0,4},{4,0},{8,12},{12,8},{1,5},{5,1},{9,13},{13,9},{2,6},{6,2},{1... | collective-permute-start | bytes 1572872 | tf_op jit(solution)/shard_map/ppermute | solution.py:264
  48.6 17.9 %collective-permute-start.11 = (bf16[256,128]{1,0:T(8,128)(2,1)}, bf16[256,128]{1,0:T(8,128)(2,1)S(1)}, u32[]{:S(2)}, u32[]{:S(2)}) collective-permute-start(bf16[256,128]{1,0:T(8,128)(2,1)} %get-tuple-element.28), channel_id=1, source_target_pairs={{0,3},{1,2},{2,1},{3,0},{4,7},{5,6},{6,5},{7,4},{8,11},{9,10},{10,... | collective-permute-start | bytes 196616 | tf_op jit(solution)/shard_map/ppermute | solution.py:267
  51.1 1.9 %copy-start.15 = (bf16[2,768,128]{2,1,0:T(8,128)(2,1)}, bf16[2,768,128]{2,1,0:T(8,128)(2,1)S(1)}, u32[]{:S(2)}) copy-start(bf16[2,768,128]{2,1,0:T(8,128)(2,1)S(1)} %collective-permute-done.rest_1_) | copy-start | bytes 1179652
  51.1 15.4 %collective-permute-start.7 = (bf16[256,128]{1,0:T(8,128)(2,1)}, bf16[256,128]{1,0:T(8,128)(2,1)S(1)}, u32[]{:S(2)}, u32[]{:S(2)}) collective-permute-start(bf16[256,128]{1,0:T(8,128)(2,1)} %get-tuple-element.24), channel_id=1, source_target_pairs={{0,1},{1,0},{2,3},{3,2},{4,5},{5,4},{6,7},{7,6},{8,9},{9,8},{10,11... | collective-permute-start | bytes 196616 | tf_op jit(solution)/shard_map/ppermute | solution.py:267
  51.8 1.3 %copy-start.16 = (bf16[2,768,128]{2,1,0:T(8,128)(2,1)}, bf16[2,768,128]{2,1,0:T(8,128)(2,1)S(1)}, u32[]{:S(2)}) copy-start(bf16[2,768,128]{2,1,0:T(8,128)(2,1)S(1)} %collective-permute-done.2.rest_3_) | copy-start | bytes 1179652
  51.8 16.6 %collective-permute-start.9 = (bf16[256,128]{1,0:T(8,128)(2,1)}, bf16[256,128]{1,0:T(8,128)(2,1)S(1)}, u32[]{:S(2)}, u32[]{:S(2)}) collective-permute-start(bf16[256,128]{1,0:T(8,128)(2,1)} %get-tuple-element.26), channel_id=1, source_target_pairs={{0,2},{1,3},{2,0},{3,1},{4,6},{5,7},{6,4},{7,5},{8,10},{9,11},{10,... | collective-permute-start | bytes 196616 | tf_op jit(solution)/shard_map/ppermute | solution.py:267
  63.9 8.5 %copy-start.3 = (bf16[4,64,1024]{2,1,0:T(8,128)(2,1)}, bf16[4,64,1024]{2,1,0:T(8,128)(2,1)S(1)}, u32[]{:S(2)}) copy-start(bf16[4,64,1024]{2,1,0:T(8,128)(2,1)S(1)} %collective-permute-done.16.rest_10_) | copy-start | bytes 1572868
  63.9 6.5 %collective-permute-start.10 = (bf16[256,128]{1,0:T(8,128)(2,1)}, bf16[256,128]{1,0:T(8,128)(2,1)S(1)}, u32[]{:S(2)}, u32[]{:S(2)}) collective-permute-start(bf16[256,128]{1,0:T(8,128)(2,1)} %get-tuple-element.27), channel_id=1, source_target_pairs={{0,3},{1,2},{2,1},{3,0},{4,7},{5,6},{6,5},{7,4},{8,11},{9,10},{10,... | collective-permute-start | bytes 196616 | tf_op jit(solution)/shard_map/ppermute | solution.py:267
  66.5 6.0 %copy-start.6 = (bf16[256,128]{1,0:T(8,128)(2,1)}, bf16[256,128]{1,0:T(8,128)(2,1)S(1)}, u32[]{:S(2)}) copy-start(bf16[256,128]{1,0:T(8,128)(2,1)S(1)} %collective-permute-done.11.rest_7_) | copy-start | bytes 196612
  66.5 5.9 %collective-permute-start.6 = (bf16[256,128]{1,0:T(8,128)(2,1)}, bf16[256,128]{1,0:T(8,128)(2,1)S(1)}, u32[]{:S(2)}, u32[]{:S(2)}) collective-permute-start(bf16[256,128]{1,0:T(8,128)(2,1)} %get-tuple-element.23), channel_id=1, source_target_pairs={{0,1},{1,0},{2,3},{3,2},{4,5},{5,4},{6,7},{7,6},{8,9},{9,8},{10,11... | collective-permute-start | bytes 196616 | tf_op jit(solution)/shard_map/ppermute | solution.py:267
  66.5 5.9 %copy-start.7 = (bf16[256,128]{1,0:T(8,128)(2,1)}, bf16[256,128]{1,0:T(8,128)(2,1)S(1)}, u32[]{:S(2)}) copy-start(bf16[256,128]{1,0:T(8,128)(2,1)S(1)} %collective-permute-done.7.rest_3_) | copy-start | bytes 196612
  66.5 5.9 %collective-permute-start.8 = (bf16[256,128]{1,0:T(8,128)(2,1)}, bf16[256,128]{1,0:T(8,128)(2,1)S(1)}, u32[]{:S(2)}, u32[]{:S(2)}) collective-permute-start(bf16[256,128]{1,0:T(8,128)(2,1)} %get-tuple-element.25), channel_id=1, source_target_pairs={{0,2},{1,3},{2,0},{3,1},{4,6},{5,7},{6,4},{7,5},{8,10},{9,11},{10,... | collective-permute-start | bytes 196616 | tf_op jit(solution)/shard_map/ppermute | solution.py:267
  68.4 4.0 %copy-start.8 = (bf16[256,128]{1,0:T(8,128)(2,1)}, bf16[256,128]{1,0:T(8,128)(2,1)S(1)}, u32[]{:S(2)}) copy-start(bf16[256,128]{1,0:T(8,128)(2,1)S(1)} %collective-permute-done.9.rest_5_) | copy-start | bytes 196612
  70.5 2.0 %copy-start.9 = (bf16[256,128]{1,0:T(8,128)(2,1)}, bf16[256,128]{1,0:T(8,128)(2,1)S(1)}, u32[]{:S(2)}) copy-start(bf16[256,128]{1,0:T(8,128)(2,1)S(1)} %collective-permute-done.10.rest_6_) | copy-start | bytes 196612
  72.4 0.6 copy-start.10
  72.4 0.6 copy-start.11
  72.4 0.8 %copy-start.4 = (bf16[4,64,1024]{2,1,0:T(8,128)(2,1)}, bf16[4,64,1024]{2,1,0:T(8,128)(2,1)S(1)}, u32[]{:S(2)}) copy-start(bf16[4,64,1024]{2,1,0:T(8,128)(2,1)S(1)} %collective-permute-done.17.rest_11_) | copy-start | bytes 1572868

commit v2 on v0

v2 whole, which is shorter than its diff:
```python
import functools
import math

import jax
import jax.numpy as jnp
from jax import lax
from jax.experimental import pallas as pl
from jax.experimental.pallas import tpu as pltpu
from jax.sharding import PartitionSpec as P

HD = 64
BLK = 128
KEEP = 6
LANES = 128
NEG = -1e30
LOWEST = -3e38
HELD = KEEP * BLK
CHUNK = 512
GROUP = 2 * HELD // CHUNK
QUERY_SCALE = HD**-0.5 * math.log2(math.e)
BLK_BITS = 7
BAND_BITS = 3
SMALL = pltpu.CompilerParams(vmem_limit_bytes=16 * 2**20)
FREE = pl.CostEstimate(flops=0, bytes_accessed=0, transcendentals=0)
LARGE = pltpu.CompilerParams(vmem_limit_bytes=60 * 2**20)
PARAMS = pltpu.CompilerParams(vmem_limit_bytes=40 * 2**20)
ANY = pl.BlockSpec(memory_space=pl.ANY)
VMEM = pl.BlockSpec(memory_space=pltpu.VMEM)


def dot_f32(left, right):
    return jnp.dot(left, right, preferred_element_type=jnp.float32)


def low_lanes(shape):
    return lax.broadcasted_iota(jnp.int32, shape, len(shape) - 1) < HD


def swap_halves(array):
    return pltpu.roll(array, HD, array.ndim - 1)


def block_ranks(mask):
    blocks = mask.shape[1]
    used = jnp.max(mask.astype(jnp.float32), axis=0, keepdims=True)
    earlier = lax.broadcasted_iota(jnp.int32, (blocks, blocks), 0)
    later = lax.broadcasted_iota(jnp.int32, (blocks, blocks), 1)
    counts = ((earlier >> BAND_BITS) == (later >> BAND_BITS)) & (earlier < later)
    rank = dot_f32(jnp.broadcast_to(used, (8, blocks)).astype(jnp.bfloat16), counts.astype(jnp.float32).astype(jnp.bfloat16))
    return jnp.broadcast_to(used, (8, blocks)), rank


def slots_of(used, rank, band):
    lane = lax.broadcasted_iota(jnp.int32, used.shape, 1)
    slot = lax.broadcasted_iota(jnp.int32, used.shape, 0).astype(jnp.float32)
    return jnp.where(((lane >> BAND_BITS) == band) & (rank == slot), used, 0.0)


def project_kv(block_mask, tokens, w_key, w_value):
    pairs = w_key.shape[1] // LANES
    rows_in = tokens.shape[0]
    rows = KEEP * BLK
    step = 2 * BLK
    steps = rows_in // step

    def kernel(mask_any, tok_ref, wk_ref, wv_ref, *rest):
        outs, (mask_ref, tok, wk, wv, held, sems, out_sems) = rest[:pairs], rest[pairs:]
        load_mask = pltpu.make_async_copy(mask_any, mask_ref, sems.at[0])
        loads = [pltpu.make_async_copy(wk_ref, wk, sems.at[1]), pltpu.make_async_copy(wv_ref, wv, sems.at[2])]
        for c in range(steps):
            at = pl.ds(c * step, step)
            loads.append(pltpu.make_async_copy(tok_ref.at[at, :], tok.at[at, :], sems.at[3 + c]))
        for copy in [load_mask] + loads:
            copy.start()
        load_mask.wait()
        used, rank = block_ranks(mask_ref[...])
        picked = slots_of(used, rank, lax.axis_index("band"))
        place = (lax.broadcasted_iota(jnp.int32, picked.shape, 1) & (2**BAND_BITS - 1)).astype(jnp.float32)
        digit = lax.broadcasted_iota(jnp.int32, picked.shape, 0)
        scale = (1 << (BAND_BITS * jnp.minimum(digit, KEEP))).astype(jnp.float32)
        code = jnp.sum(jnp.where(digit < KEEP, picked * place * scale, 0.0)).astype(jnp.int32)
        for copy in loads[:2]:
            copy.wait()
        low = low_lanes((step, LANES))
        for c in range(steps):
            at = pl.ds(c * step, step)
            loads[2 + c].wait()
            keys = dot_f32(tok[at, :], wk[...])
            values = dot_f32(tok[at, :], wv[...])
            for p in range(pairs):
                cols = slice(p * LANES, (p + 1) * LANES)
                k, v = keys[:, cols], values[:, cols]
                held[p, 0, at, :] = jnp.where(low, k, swap_halves(v)).astype(jnp.bfloat16)
                held[p, 1, at, :] = jnp.where(low, swap_halves(k), v).astype(jnp.bfloat16)
        stores = []
        for p in range(pairs):
            for e in range(KEEP):
                begin = pl.multiple_of(((code >> (BAND_BITS * e)) & (2**BAND_BITS - 1)) * BLK, BLK)
                copy = pltpu.make_async_copy(
                    held.at[p, :, pl.ds(begin, BLK), :], outs[p].at[:, pl.ds(e * BLK, BLK), :], out_sems.at[p, e]
                )
                copy.start()
                stores.append(copy)
        for copy in stores:
            copy.wait()

    return pl.pallas_call(
        kernel,
        out_shape=[jax.ShapeDtypeStruct((2, rows, LANES), jnp.bfloat16)] * pairs,
        in_specs=[ANY] * 4,
        out_specs=[ANY] * pairs,
        scratch_shapes=[
            pltpu.VMEM(block_mask.shape, jnp.int32),
            pltpu.VMEM(tokens.shape, jnp.bfloat16),
            pltpu.VMEM(w_key.shape, jnp.bfloat16),
            pltpu.VMEM(w_value.shape, jnp.bfloat16),
            pltpu.VMEM((pairs, 2, rows_in, LANES), jnp.bfloat16),
            pltpu.SemaphoreType.DMA((3 + steps,)),
            pltpu.SemaphoreType.DMA((pairs, KEEP)),
        ],
        compiler_params=LARGE,
        cost_estimate=FREE,
        name="project_kv",
    )(block_mask, tokens, w_key, w_value)


class Tables:
    def __init__(self, landing, key_tab, value_tab, sems, refs):
        self.landing, self.key_tab, self.value_tab = landing, key_tab, value_tab
        self.copies = [
            pltpu.make_async_copy(ref, landing.at[:, pl.ds(s * HELD, HELD), :], sems.at[s]) for s, ref in enumerate(refs)
        ]
        for copy in self.copies:
            copy.start()

    def fill(self, bias_ref, first):
        low = low_lanes((BLK, LANES)).astype(jnp.float32).astype(jnp.bfloat16)
        high = (1.0 - low_lanes((BLK, LANES)).astype(jnp.float32)).astype(jnp.bfloat16)
        for s, copy in enumerate(self.copies):
            copy.wait()
            for e in range(KEEP):
                at = pl.ds((s * KEEP + e) * BLK, BLK)
                row = (first + s) * 8 + e
                add = jnp.broadcast_to(bias_ref[row : row + 1, :], (BLK, LANES)).astype(jnp.bfloat16)
                for h in range(2):
                    kv = self.landing[h, at, :]
                    self.key_tab[h, at, :] = kv * low + add
                    self.value_tab[h, at, :] = kv * high + low

    def sweep(self, q, h, peak, total_sum):
        def chunk(begin, carried):
            peak, total_sum = carried
            at = pl.ds(begin, CHUNK)
            scores = lax.dot_general(
                q, self.key_tab[h, at, :], (((1,), (1,)), ((), ())), preferred_element_type=jnp.float32
            )
            new_peak = jnp.maximum(peak, jnp.max(scores, axis=1, keepdims=True))
            weights = jnp.exp2(scores - new_peak).astype(jnp.bfloat16)
            total_sum = total_sum * jnp.exp2(peak - new_peak) + dot_f32(weights, self.value_tab[h, at, :])
            return new_peak, total_sum

        def group(g, carried):
            for c in range(GROUP):
                begin = (g * GROUP + c) * CHUNK
                carried = chunk(begin if isinstance(g, int) else pl.multiple_of(begin, CHUNK), carried)
            return carried

        groups = self.key_tab.shape[1] // (GROUP * CHUNK)
        carried = (peak, total_sum)
        if groups > 2:
            return lax.fori_loop(0, groups, group, carried)
        for g in range(groups):
            carried = group(g, carried)
        return carried


def table_scratch(sources):
    table = pltpu.VMEM((2, sources * HELD, LANES), jnp.bfloat16)
    return [table, table, table, pltpu.SemaphoreType.DMA((sources,))]


def begin_attention(block_mask, tokens, w_query, early, parts, source_bands):
    rows, width = tokens.shape
    pairs = w_query.shape[1] // LANES
    part = rows // parts
    per_band = rows // BLK
    key_blocks = block_mask.shape[1]
    sources = len(source_bands(0))

    def kernel(mask_ref, tok, w, *rest):
        early_refs, rest = rest[: len(early)], rest[len(early) :]
        outs = rest[:pairs]
        bias_ref, state_ref, held, own_rows, out_sems, *scratch = rest[pairs:]
        tables = Tables(*scratch, early_refs)
        me, band = lax.axis_index("head"), lax.axis_index("band")
        own_rows[...] = jnp.zeros(own_rows.shape, jnp.float32)
        first = pl.multiple_of(band * per_band, per_band)
        own_rows[HD : HD + per_band, :] = mask_ref[pl.ds(first, per_band), :].astype(jnp.float32)
        used, rank = block_ranks(mask_ref[...])
        lane8 = lax.broadcasted_iota(jnp.int32, (8, LANES), 1)
        for s, source in enumerate(source_bands(band)):
            allowed = lax.dot_general(
                slots_of(used, rank, source).astype(jnp.bfloat16),
                own_rows[...].astype(jnp.bfloat16),
                (((1,), (1,)), ((), ())),
                preferred_element_type=jnp.float32,
            )
            queried = (lane8 >= HD) & (lane8 < HD + per_band)
            bias_ref[s * 8 : (s + 1) * 8, :] = jnp.where(queried & (allowed < 0.5), NEG, 0.0)
        lane = lax.broadcasted_iota(jnp.int32, (part, LANES), 1)
        row = lax.broadcasted_iota(jnp.int32, (part, LANES), 0)
        stores = []
        for k in range(parts):
            at = pl.ds(k * part, part)
            begin = pl.multiple_of((me ^ k) * part, part)
            q = dot_f32(tok[pl.ds(begin, part), :], w[...]) * QUERY_SCALE
            hot = (lane - HD == ((row + begin) >> BLK_BITS)).astype(jnp.float32)
            for p in range(pairs):
                pair = q[:, p * LANES : (p + 1) * LANES]
                held[p, 0, at, :] = jnp.where(lane < HD, pair, hot).astype(jnp.bfloat16)
                held[p, 1, at, :] = jnp.where(lane < HD, swap_halves(pair), hot).astype(jnp.bfloat16)
        for p in range(pairs):
            copy = pltpu.make_async_copy(held.at[p], outs[p], out_sems.at[p])
            copy.start()
            stores.append(copy)
        tables.fill(bias_ref, 0)
        lane = lax.broadcasted_iota(jnp.int32, (rows, LANES), 1)
        for h in range(2):
            peak, total_sum = tables.sweep(
                held[0, h], h, jnp.full((rows, 1), LOWEST, jnp.float32), jnp.zeros((rows, LANES), jnp.float32)
            )
            state_ref[h] = jnp.where(lane == 1, peak, total_sum)
        for copy in stores:
            copy.wait()

    out = pl.pallas_call(
        kernel,
        out_shape=[jax.ShapeDtypeStruct((2, rows, LANES), jnp.bfloat16)] * pairs
        + [jax.ShapeDtypeStruct((sources * 8, LANES), jnp.float32), jax.ShapeDtypeStruct((2, rows, LANES), jnp.float32)],
        in_specs=[VMEM] * 3 + [ANY] * len(early),
        out_specs=[ANY] * pairs + [VMEM] * 2,
        scratch_shapes=[
            pltpu.VMEM((pairs, 2, rows, LANES), jnp.bfloat16),
            pltpu.VMEM((LANES, key_blocks), jnp.float32),
            pltpu.SemaphoreType.DMA((pairs,)),
        ]
        + table_scratch(len(early)),
        compiler_params=PARAMS,
        cost_estimate=FREE,
        name="begin_attention",
    )(block_mask, tokens, w_query, *early)
    return out[:pairs], out[pairs], out[pairs + 1]


def attend(queries, state, sources, bias, first, parts, cost):
    rows = queries.shape[1]
    part = rows // parts
    states = [] if state is None else [state]

    def kernel(q_ref, bias_ref, *rest):
        state_refs, rest = rest[: len(states)], rest[len(states) :]
        srcs, rest = rest[: len(sources)], rest[len(sources) :]
        outs, scratch = rest[:parts], rest[parts:]
        tables = Tables(*scratch, srcs)
        tables.fill(bias_ref, first)
        lane = lax.broadcasted_iota(jnp.int32, (rows, LANES), 1)
        low = lane < HD
        sums = []
        for h in range(2):
            if states:
                total_sum = state_refs[0][h]
                peak = jnp.max(jnp.where(lane == 1, total_sum, LOWEST), axis=1, keepdims=True)
                total_sum = jnp.where(lane == 1, pltpu.roll(total_sum, 1, 1), total_sum)
            else:
                peak = jnp.full((rows, 1), LOWEST, jnp.float32)
                total_sum = jnp.zeros((rows, LANES), jnp.float32)
            sums.append(tables.sweep(q_ref[h], h, peak, total_sum)[1])
        top = jnp.where(low, swap_halves(sums[0]), sums[1])
        mass = jnp.where(low, sums[0], swap_halves(sums[1]))
        out = (top / mass).astype(jnp.bfloat16)
        for k in range(parts):
            outs[k][...] = out[k * part : (k + 1) * part, :]

    return pl.pallas_call(
        kernel,
        out_shape=[jax.ShapeDtypeStruct((part, LANES), jnp.bfloat16)] * parts,
        in_specs=[VMEM, VMEM] + [VMEM] * len(states) + [ANY] * len(sources),
        out_specs=[VMEM] * parts,
        scratch_shapes=table_scratch(len(sources)),
        compiler_params=PARAMS,
        cost_estimate=pl.CostEstimate(flops=cost, bytes_accessed=0, transcendentals=0),
        name="attend",
    )(queries, bias, *states, *sources)


def assemble(w_mine, w_other, tiles):
    quarters, heads = 2 * tiles, w_mine.shape[1]
    piece, width = w_mine.shape[2:]
    order = [0]
    bit = heads // 2
    while bit:
        order += [bit ^ k for k in order]
        bit //= 2

    def kernel(mine_ref, other_ref, out_ref, sems):
        quarter = (lax.axis_index("band") & 1) * tiles + lax.axis_index("tiles")
        copies = []
        for s in range(quarters):
            ref = other_ref if s >= tiles else mine_ref
            for i, k in enumerate(order):
                begin = pl.multiple_of((quarters * k + (quarter ^ s)) * piece, piece)
                copy = pltpu.make_async_copy(ref.at[s % tiles, i], out_ref.at[pl.ds(begin, piece), :], sems.at[s, i])
                copy.start()
                copies.append(copy)
        for copy in copies:
            copy.wait()

    return pl.pallas_call(
        kernel,
        out_shape=jax.ShapeDtypeStruct((quarters * heads * piece, width), jnp.bfloat16),
        in_specs=[ANY] * 2,
        out_specs=ANY,
        scratch_shapes=[pltpu.SemaphoreType.DMA((quarters, heads))],
        compiler_params=SMALL,
        cost_estimate=FREE,
        name="assemble",
    )(w_mine, w_other)


def project_out(attended, w_full):
    pieces = [a for group in attended for a in group]
    rows, width = pieces[0].shape[0], w_full.shape[1]

    def kernel(*rest):
        w_ref, out_ref = rest[-2:]
        rows_all = jnp.concatenate([ref[...] for ref in rest[:-2]], axis=1)
        out_ref[...] = dot_f32(rows_all, w_ref[...]).astype(jnp.bfloat16)

    return pl.pallas_call(
        kernel,
        out_shape=jax.ShapeDtypeStruct((rows, width), jnp.bfloat16),
        in_specs=[VMEM] * (len(pieces) + 1),
        out_specs=VMEM,
        compiler_params=SMALL,
        cost_estimate=FREE,
        name="project_out",
    )(*pieces, w_full)


def on_device(sizes, tokens, w_query, w_key, w_value, w_out, block_mask):
    tiles, bands, heads = sizes
    hops = range(1, bands // 2)

    def along_band(array, goes_to):
        return lax.ppermute(array, "band", [(i, goes_to(i)) for i in range(bands)])

    def to_sibling(array):
        return along_band(array, lambda i: i ^ 1)

    def along_head(array, k):
        return lax.ppermute(array, "head", [(i, i ^ k) for i in range(heads)])

    def source_bands(band):
        found = [band, band ^ 1]
        for r in hops:
            far = lax.rem(band + bands - 2 * r, bands)
            found += [far, far ^ 1]
        return found

    kv = project_kv(block_mask, tokens, w_key, w_value)
    pairs = len(kv)
    far = [[along_band(one, lambda i: (i + 2 * r) % bands) for r in hops] for one in kv]
    near = [to_sibling(one) for one in kv]

    def widen(held, came, k):
        held = jnp.concatenate([held, came]) if came is not None else held
        return held, along_head(held, k)

    def other_tiles(array):
        return [lax.ppermute(array, "tiles", [(i, i ^ s) for i in range(tiles)]) for s in range(1, tiles)]

    quarter = (lax.axis_index("band") & 1) * tiles + lax.axis_index("tiles")
    piece = w_out.shape[0] // (2 * tiles)
    w_mine = lax.dynamic_slice_in_dim(w_out, quarter * piece, piece, 0)
    w_mine, kv = lax.optimization_barrier((w_mine, kv))
    bit = heads // 2
    w_mine, arriving = widen(w_mine[None], None, bit)
    queries, bias, state = begin_attention(block_mask, tokens, w_query, [kv[0], near[0]], heads, source_bands)
    far[0], queries, arriving = lax.optimization_barrier((far[0], queries, arriving))
    while bit > 1:
        bit //= 2
        w_mine, arriving = widen(w_mine, arriving, bit)

    attended = [[] for _ in range(heads)]
    for p in range(pairs):
        if p > 0:
            far[p], pieces = lax.optimization_barrier((far[p], pieces))
        late = []
        for one in far[p]:
            late += [one, to_sibling(one)]
        if p == 0:
            pieces = attend(queries[0], state, late, bias, 2, heads, 2**33)
            pieces, arriving = lax.optimization_barrier((pieces, arriving))
            w_mine = jnp.concatenate([w_mine, arriving])[None]
            arriving = other_tiles(w_mine)
        else:
            pieces = attend(queries[p], None, [kv[p], near[p]] + late, bias, 0, heads, 0)
            attended, pieces, arriving = lax.optimization_barrier((attended, pieces, arriving))
        attended[0].append(pieces[0])
        for k in range(1, heads):
            attended[k].append(along_head(pieces[k], k))
    w_mine = jnp.concatenate([w_mine] + arriving)
    w_full = assemble(w_mine, to_sibling(w_mine), tiles)
    return project_out(attended, w_full)


def solution(mesh):
    sizes = tuple(mesh.shape[axis] for axis in ("tiles", "band", "head"))
    return jax.shard_map(
        functools.partial(on_device, sizes),
        mesh=mesh,
        in_specs=(
            P(("tiles", "band"), None),
            P(None, "head"),
            P(None, "head"),
            P(None, "head"),
            P("head", None),
            P("tiles", None),
        ),
        out_specs=P(("tiles", "band", "head"), None),
        check_vma=False,
    )
```

time: 418 us -> 55.5 us (0.13)
  local copies, waits for them, and re-layouts: 120 us -> 1.02 us
  other arithmetic: 118 us -> 0.18 us
  matrix products: 89.7 us -> 0 us
  waiting for transfers between devices: 72.6 us -> 4.68 us
  Pallas kernels: 0 us -> 28.6 us
  starting transfers between devices: 0.04 us -> 20.6 us
  between operations: 14.2 us -> 0.16 us
    dot_general x10 -> x0, matrix products: 89.7 us -> none  [the longest x3 43.6 us: one_turn(): jnp.einsum('prhk,pkhd->prhd', weights, value_rows, preferred_element_type...]
    slice x9 -> x0, local copies, waits for them, and re-layouts: 56.3 us -> none  [the longest x6 37.2 us: one_turn(): pair_rows[:, :, local_cols:].reshape(per_turn, -1, head_count, head_dim)]
    gather x16 -> x0, local copies, waits for them, and re-layouts: 55.4 us -> none  [the longest x6 27.4 us: one_turn(): jnp.take(item_rows, owners, axis=0)]
    scatter-add x6 -> x0, other arithmetic: 45.5 us -> none  [the longest x3 36.8 us: one_turn(): jax.ops.segment_sum(sum_terms, owners, num_segments=item_count)]
    reduce_scatter x1 -> x0, waiting for transfers between devices: 43.1 us -> none  [on_device(): lax.psum_scatter(jnp.dot(attended, w_out, preferred_element_type=jnp.floa...]
    reduce_sum x3 -> x0, other arithmetic: 32.2 us -> none  [one_turn(): row_mass = jnp.sum(exponent, axis=3)]
    all_gather x1 -> x0, waiting for transfers between devices: 29.4 us -> none  [on_device(): lax.all_gather(key_value, 'band', axis=0, tiled=True)]
    pallas_call x0 -> x6, Pallas kernels: none -> 28.6 us  [the longest x2 13.9 us: attend(): pl.pallas_call(kernel, out_shape=[jax.ShapeDtypeStruct((part, LANES), jnp...]
  transfers between devices with their start and end apart: 2 -> 16, of which waited for: 2 -> 4; matrix products, arithmetic and copies ran while one was open for 2% -> 0% of each run, Pallas kernels for 0% -> 41%
where the time goes in v2:
time: 55.5 us; the launch traced here: 55.3 us
  Pallas kernels  28.6 us (52%)
  starting transfers between devices  20.6 us (37%)
  waiting for transfers between devices  4.68 us (8%)
  local copies, waits for them, and re-layouts  1.02 us (2%)
    pallas_call x2, Pallas kernels, attend(): pl.pallas_call(kernel, out_shape=[jax.ShapeDtypeStruct((part, LANES), jnp...  13.9 us
    ppermute x8, starting transfers between devices, along_head(): return lax.ppermute(array, 'head', [(i, i ^ k) for i in range(heads)])  13.6 us
    pallas_call x1, Pallas kernels, begin_attention(): pl.pallas_call(kernel, out_shape=[jax.ShapeDtypeStruct((2, rows, LANES),...  5.73 us
    ppermute x7, starting transfers between devices, along_band(): return lax.ppermute(array, 'band', [(i, goes_to(i)) for i in range(bands)])  5.44 us
    pallas_call x1, Pallas kernels, project_kv(): pl.pallas_call(kernel, out_shape=[jax.ShapeDtypeStruct((2, rows, LANES),...  4.6 us
    ppermute x8, waiting for transfers between devices, along_head(): return lax.ppermute(array, 'head', [(i, i ^ k) for i in range(heads)])  4.08 us
    pallas_call x1, Pallas kernels, assemble(): pl.pallas_call(kernel, out_shape=jax.ShapeDtypeStruct((quarters * heads *...  2.87 us
    ppermute x1, starting transfers between devices, other_tiles(): lax.ppermute(array, 'tiles', [(i, i ^ s) for i in range(tiles)])  1.58 us
  transfers between devices with their start and end apart: 16, of which 4 were waited for; matrix products, arithmetic and copies ran while one was open for 0% of the time, Pallas kernels for 41%

profile of v2, /device:TPU:0, one launch (start us, length us, event | category | flops | bytes accessed | tf_op | source)
XLA Modules:
  0.0 55.3 jit_solution(11447748051199368584)
XLA Ops:
  0.0 0.0 copy-start
  0.0 4.6 %project_kv.1 = (bf16[2,768,128]{2,1,0:T(8,128)(2,1)}, bf16[2,768,128]{2,1,0:T(8,128)(2,1)}) custom-call(s32[32,32]{1,0:T(8,128)} %mask_ref.1, bf16[1024,1024]{1,0:T(8,128)(2,1)} %tok.1, bf16[1024,256]{1,0:T(8,128)(2,1)} %wk_ref.1, bf16[1024,256]{1,0:T(8,128)(2,1)} %wv_ref.1), custom_call_target="tpu_custom_call" | custom-call | tf_op jit(solution)/shard_map/project_kv/pallas_call | solution.py:107
  4.6 0.0 copy-start.3
  4.6 0.5 collective-permute-start.1
  5.2 2.6 %collective-permute-start = (bf16[2,768,128]{2,1,0:T(8,128)(2,1)}, bf16[2,768,128]{2,1,0:T(8,128)(2,1)}, u32[]{:S(2)}, u32[]{:S(2)}) collective-permute-start(bf16[2,768,128]{2,1,0:T(8,128)(2,1)} %get-tuple-element.43.rest_0_), channel_id=1, source_target_pairs={{0,8},{4,12},{8,0},{12,4},{1,9},{5,13},{9,1},{13,5},{2,10},{6,14},... | collective-permute-start | bytes 1179656 | tf_op jit(solution)/shard_map/ppermute | solution.py:355
  7.7 0.0 copy-done
  7.7 2.7 %collective-permute-start.2 = (bf16[1,64,1024]{2,1,0:T(8,128)(2,1)S(1)}, bf16[1,64,1024]{2,1,0:T(8,128)(2,1)S(1)}, u32[]{:S(2)}, u32[]{:S(2)}) collective-permute-start(bf16[1,64,1024]{2,1,0:T(8,128)(2,1)S(1)} %bitcast.3), channel_id=1, source_target_pairs={{0,2},{1,3},{2,0},{3,1},{4,6},{5,7},{6,4},{7,5},{8,10},{9,11},{10,... | collective-permute-start | bytes 393224 | tf_op jit(solution)/shard_map/ppermute | solution.py:361
  10.4 0.0 collective-permute-done.1.rest_1_
  10.4 0.0 copy-done.5
  10.4 0.0 copy-done.1
  10.4 0.0 copy-done.2
  10.4 0.0 copy-start.4
  10.4 1.0 %copy-done.4 = bf16[2,768,128]{2,1,0:T(8,128)(2,1)S(1)} copy-done((bf16[2,768,128]{2,1,0:T(8,128)(2,1)S(1)}, bf16[2,768,128]{2,1,0:T(8,128)(2,1)}, u32[]{:S(2)}) %copy-start.4) | copy-done | bytes 393240
  11.4 5.7 %begin_attention.1 = (bf16[2,1024,128]{2,1,0:T(8,128)(2,1)S(1)}, bf16[2,1024,128]{2,1,0:T(8,128)(2,1)S(1)}, f32[32,128]{1,0:T(8,128)S(1)}, f32[2,1024,128]{2,1,0:T(8,128)S(1)}) custom-call(s32[32,32]{1,0:T(8,128)S(1)} %copy-done.5, bf16[1024,1024]{1,0:T(8,128)(2,1)S(1)} %copy-done.1, bf16[1024,256]{1,0:T(8,128)(2,1)S(1)} %copy-done.2, ...), custom_call_target="tpu_custom_call" | custom-call | tf_op jit(solution)/shard_map/begin_attention/pallas_call | solution.py:236
  17.2 0.0 collective-permute-done.2
  17.2 0.6 %collective-permute-done.rest_1_ = bf16[2,768,128]{2,1,0:T(8,128)(2,1)} collective-permute-done((bf16[2,768,128]{2,1,0:T(8,128)(2,1)}, bf16[2,768,128]{2,1,0:T(8,128)(2,1)}, u32[]{:S(2)}, u32[]{:S(2)}) %collective-permute-start) | collective-permute-done | bytes 393248 | tf_op jit(solution)/shard_map/ppermute | solution.py:355
  17.7 0.0 collective-permute-start.3
  17.8 1.8 %collective-permute-start.9 = (bf16[2,768,128]{2,1,0:T(8,128)(2,1)S(1)}, bf16[2,768,128]{2,1,0:T(8,128)(2,1)S(1)}, u32[]{:S(2)}, u32[]{:S(2)}) collective-permute-start(bf16[2,768,128]{2,1,0:T(8,128)(2,1)S(1)} %copy-done.3), channel_id=1, source_target_pairs={{0,8},{4,12},{8,0},{12,4},{1,9},{5,13},{9,1},{13,5},{2,10},{6,14},... | collective-permute-start | bytes 1179656 | tf_op jit(solution)/shard_map/ppermute | solution.py:355
  19.5 1.6 %collective-permute-start.4 = (bf16[2,64,1024]{2,1,0:T(8,128)(2,1)S(1)}, bf16[2,64,1024]{2,1,0:T(8,128)(2,1)S(1)}, u32[]{:S(2)}, u32[]{:S(2)}) collective-permute-start(bf16[2,64,1024]{2,1,0:T(8,128)(2,1)S(1)} %pad_maximum_fusion.1), channel_id=1, source_target_pairs={{0,1},{1,0},{2,3},{3,2},{4,5},{5,4},{6,7},{7,6},{8,9},{9,8},{10,11... | collective-permute-start | bytes 786440 | tf_op jit(solution)/shard_map/ppermute | solution.py:361
  21.2 0.0 collective-permute-done.3.rest_2_
  21.2 5.4 %attend.2 = (bf16[256,128]{1,0:T(8,128)(2,1)S(1)}, bf16[256,128]{1,0:T(8,128)(2,1)S(1)}, bf16[256,128]{1,0:T(8,128)(2,1)S(1)}, bf16[256,128]{1,0:T(8,128)(2,1)S(1)}) custom-call(bf16[2,1024,128]{2,1,0:T(8,128)(2,1)S(1)} %get-tuple-element.47.q_ref, f32[32,128]{1,0:T(8,128)S(1)} %get-tuple-element.48.bias_ref, f32[2,1024,128]{2,1,0:T(8,128)S(1)} %get-tuple-element.49.rest_0_, ...), custom_call_target="tpu_custom_call" | custom-call | flops 8589934592 | tf_op jit(solution)/shard_map/attend/pallas_call | solution.py:284
  26.6 1.5 %collective-permute-done.4 = bf16[2,64,1024]{2,1,0:T(8,128)(2,1)S(1)} collective-permute-done((bf16[2,64,1024]{2,1,0:T(8,128)(2,1)S(1)}, bf16[2,64,1024]{2,1,0:T(8,128)(2,1)S(1)}, u32[]{:S(2)}, u32[]{:S(2)}) %collective-permute-start.4) | collective-permute-done | bytes 262176 | tf_op jit(solution)/shard_map/ppermute | solution.py:361
  28.0 0.1 maximum_bitcast_fusion
  28.1 1.6 %collective-permute-start.11 = (bf16[1,4,64,1024]{3,2,1,0:T(8,128)(2,1)S(1)}, bf16[1,4,64,1024]{3,2,1,0:T(8,128)(2,1)S(1)}, u32[]{:S(2)}, u32[]{:S(2)}) collective-permute-start(bf16[1,4,64,1024]{3,2,1,0:T(8,128)(2,1)S(1)} %maximum_bitcast_fusion), channel_id=1, source_target_pairs={{0,16},{16,0},{1,17},{17,1},{2,18},{18,2},{3,19},{19,3},{4,20},{20... | collective-permute-start | bytes 1572872 | tf_op jit(solution)/shard_map/ppermute | solution.py:380
  29.7 0.0 collective-permute-start.8
  29.7 0.0 collective-permute-done.9.rest_2_
  29.7 0.5 collective-permute-start.10
  30.2 1.6 %collective-permute-start.5 = (bf16[256,128]{1,0:T(8,128)(2,1)S(1)}, bf16[256,128]{1,0:T(8,128)(2,1)S(1)}, u32[]{:S(2)}, u32[]{:S(2)}) collective-permute-start(bf16[256,128]{1,0:T(8,128)(2,1)S(1)} %get-tuple-element.57), channel_id=1, source_target_pairs={{0,1},{1,0},{2,3},{3,2},{4,5},{5,4},{6,7},{7,6},{8,9},{9,8},{10,11... | collective-permute-start | bytes 196616 | tf_op jit(solution)/shard_map/ppermute | solution.py:361
  31.8 2.6 %collective-permute-start.6 = (bf16[256,128]{1,0:T(8,128)(2,1)S(1)}, bf16[256,128]{1,0:T(8,128)(2,1)S(1)}, u32[]{:S(2)}, u32[]{:S(2)}) collective-permute-start(bf16[256,128]{1,0:T(8,128)(2,1)S(1)} %get-tuple-element.58), channel_id=1, source_target_pairs={{0,2},{1,3},{2,0},{3,1},{4,6},{5,7},{6,4},{7,5},{8,10},{9,11},{10,... | collective-permute-start | bytes 196616 | tf_op jit(solution)/shard_map/ppermute | solution.py:361
  34.4 0.0 collective-permute-done.8.rest_1_
  34.4 0.6 %collective-permute-start.7 = (bf16[256,128]{1,0:T(8,128)(2,1)S(1)}, bf16[256,128]{1,0:T(8,128)(2,1)S(1)}, u32[]{:S(2)}, u32[]{:S(2)}) collective-permute-start(bf16[256,128]{1,0:T(8,128)(2,1)S(1)} %get-tuple-element.59), channel_id=1, source_target_pairs={{0,3},{1,2},{2,1},{3,0},{4,7},{5,6},{6,5},{7,4},{8,11},{9,10},{10,... | collective-permute-start | bytes 196616 | tf_op jit(solution)/shard_map/ppermute | solution.py:361
  35.0 0.0 collective-permute-done.10.rest_3_
  35.0 8.6 %attend.3 = (bf16[256,128]{1,0:T(8,128)(2,1)S(1)}, bf16[256,128]{1,0:T(8,128)(2,1)S(1)}, bf16[256,128]{1,0:T(8,128)(2,1)S(1)}, bf16[256,128]{1,0:T(8,128)(2,1)S(1)}) custom-call(bf16[2,1024,128]{2,1,0:T(8,128)(2,1)S(1)} %get-tuple-element.60.q_ref, f32[32,128]{1,0:T(8,128)S(1)} %get-tuple-element.48.bias_ref, bf16[2,768,128]{2,1,0:T(8,128)(2,1)S(1)} %copy-done.3, ...), custom_call_target="tpu_custom_call" | custom-call | tf_op jit(solution)/shard_map/attend/pallas_call | solution.py:284
  43.6 0.0 collective-permute-done.5.rest_2_
  43.6 0.0 collective-permute-done.6.rest_4_
  43.6 0.0 collective-permute-done.7.rest_6_
  43.6 0.0 collective-permute-done.11
  43.6 0.1 pad_maximum_fusion.mine_ref
  43.7 0.1 collective-permute-start.15
  43.8 0.3 collective-permute-start.12
  44.1 3.5 %collective-permute-start.13 = (bf16[256,128]{1,0:T(8,128)(2,1)S(1)}, bf16[256,128]{1,0:T(8,128)(2,1)S(1)}, u32[]{:S(2)}, u32[]{:S(2)}) collective-permute-start(bf16[256,128]{1,0:T(8,128)(2,1)S(1)} %get-tuple-element.73), channel_id=1, source_target_pairs={{0,2},{1,3},{2,0},{3,1},{4,6},{5,7},{6,4},{7,5},{8,10},{9,11},{10,... | collective-permute-start | bytes 196616 | tf_op jit(solution)/shard_map/ppermute | solution.py:361
  47.6 0.6 %collective-permute-start.14 = (bf16[256,128]{1,0:T(8,128)(2,1)S(1)}, bf16[256,128]{1,0:T(8,128)(2,1)S(1)}, u32[]{:S(2)}, u32[]{:S(2)}) collective-permute-start(bf16[256,128]{1,0:T(8,128)(2,1)S(1)} %get-tuple-element.75), channel_id=1, source_target_pairs={{0,3},{1,2},{2,1},{3,0},{4,7},{5,6},{6,5},{7,4},{8,11},{9,10},{10,... | collective-permute-start | bytes 196616 | tf_op jit(solution)/shard_map/ppermute | solution.py:361
  48.3 0.0 collective-permute-done.15.other_ref
  48.3 2.9 %assemble.1.rest_8_ = bf16[1024,1024]{1,0:T(8,128)(2,1)S(1)} custom-call(bf16[2,4,64,1024]{3,2,1,0:T(8,128)(2,1)S(1)} %pad_maximum_fusion.mine_ref, bf16[2,4,64,1024]{3,2,1,0:T(8,128)(2,1)S(1)} %collective-permute-done.15.other_ref), custom_call_target="tpu_custom_call" | custom-call | tf_op jit(solution)/shard_map/assemble/pallas_call | solution.py:318
  51.1 0.0 collective-permute-done.12.rest_3_
  51.1 0.7 %collective-permute-done.13.rest_5_ = bf16[256,128]{1,0:T(8,128)(2,1)S(1)} collective-permute-done((bf16[256,128]{1,0:T(8,128)(2,1)S(1)}, bf16[256,128]{1,0:T(8,128)(2,1)S(1)}, u32[]{:S(2)}, u32[]{:S(2)}) %collective-permute-start.13) | collective-permute-done | bytes 65568 | tf_op jit(solution)/shard_map/ppermute | solution.py:361
  51.8 1.9 %collective-permute-done.14.rest_7_ = bf16[256,128]{1,0:T(8,128)(2,1)S(1)} collective-permute-done((bf16[256,128]{1,0:T(8,128)(2,1)S(1)}, bf16[256,128]{1,0:T(8,128)(2,1)S(1)}, u32[]{:S(2)}, u32[]{:S(2)}) %collective-permute-start.14) | collective-permute-done | bytes 65568 | tf_op jit(solution)/shard_map/ppermute | solution.py:361
  53.7 1.5 %project_out.1 = bf16[256,1024]{1,0:T(8,128)(2,1)} custom-call(bf16[256,128]{1,0:T(8,128)(2,1)S(1)} %get-tuple-element.68.rest_0_, bf16[256,128]{1,0:T(8,128)(2,1)S(1)} %get-tuple-element.69.rest_1_, bf16[256,128]{1,0:T(8,128)(2,1)S(1)} %collective-permute-done.5.rest_2_, bf16[256,128]{1,0:T(8,128)(2,1)S(1)} %collective-permute-done.12.rest_3_, ...), custom_call_target="tpu_custom_call" | custom-call | tf_op jit(solution)/shard_map/project_out/pallas_call | solution.py:339
  (6 shorter events, 0.0 us)
Async XLA Ops:
  0.0 7.7 %copy-start = (bf16[256,1024]{1,0:T(8,128)(2,1)S(1)}, bf16[256,1024]{1,0:T(8,128)(2,1)}, u32[]{:S(2)}) copy-start(bf16[256,1024]{1,0:T(8,128)(2,1)} %param.10) | copy-start | bytes 1572868
  0.0 10.4 %copy-start.5 = (s32[32,32]{1,0:T(8,128)S(1)}, s32[32,32]{1,0:T(8,128)}, u32[]{:S(2)}) copy-start(s32[32,32]{1,0:T(8,128)} %mask_ref.1) | copy-start | bytes 12292
  0.0 10.4 %copy-start.1 = (bf16[1024,1024]{1,0:T(8,128)(2,1)S(1)}, bf16[1024,1024]{1,0:T(8,128)(2,1)}, u32[]{:S(2)}) copy-start(bf16[1024,1024]{1,0:T(8,128)(2,1)} %tok.1) | copy-start | bytes 6291460
  0.0 10.4 %copy-start.2 = (bf16[1024,256]{1,0:T(8,128)(2,1)S(1)}, bf16[1024,256]{1,0:T(8,128)(2,1)}, u32[]{:S(2)}) copy-start(bf16[1024,256]{1,0:T(8,128)(2,1)} %w.1) | copy-start | bytes 1572868
  4.6 13.1 %copy-start.3 = (bf16[2,768,128]{2,1,0:T(8,128)(2,1)S(1)}, bf16[2,768,128]{2,1,0:T(8,128)(2,1)}, u32[]{:S(2)}) copy-start(bf16[2,768,128]{2,1,0:T(8,128)(2,1)} %get-tuple-element.61.rest_0_) | copy-start | bytes 1179652
  4.6 5.8 %collective-permute-start.1 = (bf16[2,768,128]{2,1,0:T(8,128)(2,1)}, bf16[2,768,128]{2,1,0:T(8,128)(2,1)}, u32[]{:S(2)}, u32[]{:S(2)}) collective-permute-start(bf16[2,768,128]{2,1,0:T(8,128)(2,1)} %get-tuple-element.43.rest_0_), channel_id=1, source_target_pairs={{0,4},{4,0},{8,12},{12,8},{1,5},{5,1},{9,13},{13,9},{2,6},{6,2},{1... | collective-permute-start | bytes 1179656 | tf_op jit(solution)/shard_map/ppermute | solution.py:355
  5.2 12.6 %collective-permute-start = (bf16[2,768,128]{2,1,0:T(8,128)(2,1)}, bf16[2,768,128]{2,1,0:T(8,128)(2,1)}, u32[]{:S(2)}, u32[]{:S(2)}) collective-permute-start(bf16[2,768,128]{2,1,0:T(8,128)(2,1)} %get-tuple-element.43.rest_0_), channel_id=1, source_target_pairs={{0,8},{4,12},{8,0},{12,4},{1,9},{5,13},{9,1},{13,5},{2,10},{6,14},... | collective-permute-start | bytes 1179656 | tf_op jit(solution)/shard_map/ppermute | solution.py:355
  7.7 9.4 %collective-permute-start.2 = (bf16[1,64,1024]{2,1,0:T(8,128)(2,1)S(1)}, bf16[1,64,1024]{2,1,0:T(8,128)(2,1)S(1)}, u32[]{:S(2)}, u32[]{:S(2)}) collective-permute-start(bf16[1,64,1024]{2,1,0:T(8,128)(2,1)S(1)} %bitcast.3), channel_id=1, source_target_pairs={{0,2},{1,3},{2,0},{3,1},{4,6},{5,7},{6,4},{7,5},{8,10},{9,11},{10,... | collective-permute-start | bytes 393224 | tf_op jit(solution)/shard_map/ppermute | solution.py:361
  10.4 1.0 %copy-start.4 = (bf16[2,768,128]{2,1,0:T(8,128)(2,1)S(1)}, bf16[2,768,128]{2,1,0:T(8,128)(2,1)}, u32[]{:S(2)}) copy-start(bf16[2,768,128]{2,1,0:T(8,128)(2,1)} %get-tuple-element.43.rest_0_) | copy-start | bytes 1179652
  17.7 3.4 %collective-permute-start.3 = (bf16[2,768,128]{2,1,0:T(8,128)(2,1)}, bf16[2,768,128]{2,1,0:T(8,128)(2,1)S(1)}, u32[]{:S(2)}, u32[]{:S(2)}) collective-permute-start(bf16[2,768,128]{2,1,0:T(8,128)(2,1)} %collective-permute-done.rest_1_), channel_id=1, source_target_pairs={{0,4},{4,0},{8,12},{12,8},{1,5},{5,1},{9,13},{13,9},{2,6},{6,2},{1... | collective-permute-start | bytes 1179656 | tf_op jit(solution)/shard_map/ppermute | solution.py:355
  17.8 11.9 %collective-permute-start.9 = (bf16[2,768,128]{2,1,0:T(8,128)(2,1)S(1)}, bf16[2,768,128]{2,1,0:T(8,128)(2,1)S(1)}, u32[]{:S(2)}, u32[]{:S(2)}) collective-permute-start(bf16[2,768,128]{2,1,0:T(8,128)(2,1)S(1)} %copy-done.3), channel_id=1, source_target_pairs={{0,8},{4,12},{8,0},{12,4},{1,9},{5,13},{9,1},{13,5},{2,10},{6,14},... | collective-permute-start | bytes 1179656 | tf_op jit(solution)/shard_map/ppermute | solution.py:355
  19.5 8.5 %collective-permute-start.4 = (bf16[2,64,1024]{2,1,0:T(8,128)(2,1)S(1)}, bf16[2,64,1024]{2,1,0:T(8,128)(2,1)S(1)}, u32[]{:S(2)}, u32[]{:S(2)}) collective-permute-start(bf16[2,64,1024]{2,1,0:T(8,128)(2,1)S(1)} %pad_maximum_fusion.1), channel_id=1, source_target_pairs={{0,1},{1,0},{2,3},{3,2},{4,5},{5,4},{6,7},{7,6},{8,9},{9,8},{10,11... | collective-permute-start | bytes 786440 | tf_op jit(solution)/shard_map/ppermute | solution.py:361
  28.1 15.5 %collective-permute-start.11 = (bf16[1,4,64,1024]{3,2,1,0:T(8,128)(2,1)S(1)}, bf16[1,4,64,1024]{3,2,1,0:T(8,128)(2,1)S(1)}, u32[]{:S(2)}, u32[]{:S(2)}) collective-permute-start(bf16[1,4,64,1024]{3,2,1,0:T(8,128)(2,1)S(1)} %maximum_bitcast_fusion), channel_id=1, source_target_pairs={{0,16},{16,0},{1,17},{17,1},{2,18},{18,2},{3,19},{19,3},{4,20},{20... | collective-permute-start | bytes 1572872 | tf_op jit(solution)/shard_map/ppermute | solution.py:380
  29.7 4.7 %collective-permute-start.8 = (bf16[2,768,128]{2,1,0:T(8,128)(2,1)S(1)}, bf16[2,768,128]{2,1,0:T(8,128)(2,1)S(1)}, u32[]{:S(2)}, u32[]{:S(2)}) collective-permute-start(bf16[2,768,128]{2,1,0:T(8,128)(2,1)S(1)} %copy-done.3), channel_id=1, source_target_pairs={{0,4},{4,0},{8,12},{12,8},{1,5},{5,1},{9,13},{13,9},{2,6},{6,2},{1... | collective-permute-start | bytes 1179656 | tf_op jit(solution)/shard_map/ppermute | solution.py:355
  29.7 5.3 %collective-permute-start.10 = (bf16[2,768,128]{2,1,0:T(8,128)(2,1)S(1)}, bf16[2,768,128]{2,1,0:T(8,128)(2,1)S(1)}, u32[]{:S(2)}, u32[]{:S(2)}) collective-permute-start(bf16[2,768,128]{2,1,0:T(8,128)(2,1)S(1)} %collective-permute-done.9.rest_2_), channel_id=1, source_target_pairs={{0,4},{4,0},{8,12},{12,8},{1,5},{5,1},{9,13},{13,9},{2,6},{6,2},{1... | collective-permute-start | bytes 1179656 | tf_op jit(solution)/shard_map/ppermute | solution.py:355
  30.2 13.4 %collective-permute-start.5 = (bf16[256,128]{1,0:T(8,128)(2,1)S(1)}, bf16[256,128]{1,0:T(8,128)(2,1)S(1)}, u32[]{:S(2)}, u32[]{:S(2)}) collective-permute-start(bf16[256,128]{1,0:T(8,128)(2,1)S(1)} %get-tuple-element.57), channel_id=1, source_target_pairs={{0,1},{1,0},{2,3},{3,2},{4,5},{5,4},{6,7},{7,6},{8,9},{9,8},{10,11... | collective-permute-start | bytes 196616 | tf_op jit(solution)/shard_map/ppermute | solution.py:361
  31.8 11.8 %collective-permute-start.6 = (bf16[256,128]{1,0:T(8,128)(2,1)S(1)}, bf16[256,128]{1,0:T(8,128)(2,1)S(1)}, u32[]{:S(2)}, u32[]{:S(2)}) collective-permute-start(bf16[256,128]{1,0:T(8,128)(2,1)S(1)} %get-tuple-element.58), channel_id=1, source_target_pairs={{0,2},{1,3},{2,0},{3,1},{4,6},{5,7},{6,4},{7,5},{8,10},{9,11},{10,... | collective-permute-start | bytes 196616 | tf_op jit(solution)/shard_map/ppermute | solution.py:361
  34.4 9.2 %collective-permute-start.7 = (bf16[256,128]{1,0:T(8,128)(2,1)S(1)}, bf16[256,128]{1,0:T(8,128)(2,1)S(1)}, u32[]{:S(2)}, u32[]{:S(2)}) collective-permute-start(bf16[256,128]{1,0:T(8,128)(2,1)S(1)} %get-tuple-element.59), channel_id=1, source_target_pairs={{0,3},{1,2},{2,1},{3,0},{4,7},{5,6},{6,5},{7,4},{8,11},{9,10},{10,... | collective-permute-start | bytes 196616 | tf_op jit(solution)/shard_map/ppermute | solution.py:361
  43.7 4.5 %collective-permute-start.15 = (bf16[2,4,64,1024]{3,2,1,0:T(8,128)(2,1)S(1)}, bf16[2,4,64,1024]{3,2,1,0:T(8,128)(2,1)S(1)}, u32[]{:S(2)}, u32[]{:S(2)}) collective-permute-start(bf16[2,4,64,1024]{3,2,1,0:T(8,128)(2,1)S(1)} %pad_maximum_fusion.mine_ref), channel_id=1, source_target_pairs={{0,4},{4,0},{8,12},{12,8},{1,5},{5,1},{9,13},{13,9},{2,6},{6,2},{1... | collective-permute-start | bytes 3145736 | tf_op jit(solution)/shard_map/ppermute | solution.py:355
  43.8 7.3 %collective-permute-start.12 = (bf16[256,128]{1,0:T(8,128)(2,1)S(1)}, bf16[256,128]{1,0:T(8,128)(2,1)S(1)}, u32[]{:S(2)}, u32[]{:S(2)}) collective-permute-start(bf16[256,128]{1,0:T(8,128)(2,1)S(1)} %get-tuple-element.71), channel_id=1, source_target_pairs={{0,1},{1,0},{2,3},{3,2},{4,5},{5,4},{6,7},{7,6},{8,9},{9,8},{10,11... | collective-permute-start | bytes 196616 | tf_op jit(solution)/shard_map/ppermute | solution.py:361
  44.1 7.7 %collective-permute-start.13 = (bf16[256,128]{1,0:T(8,128)(2,1)S(1)}, bf16[256,128]{1,0:T(8,128)(2,1)S(1)}, u32[]{:S(2)}, u32[]{:S(2)}) collective-permute-start(bf16[256,128]{1,0:T(8,128)(2,1)S(1)} %get-tuple-element.73), channel_id=1, source_target_pairs={{0,2},{1,3},{2,0},{3,1},{4,6},{5,7},{6,4},{7,5},{8,10},{9,11},{10,... | collective-permute-start | bytes 196616 | tf_op jit(solution)/shard_map/ppermute | solution.py:361
  47.6 6.1 %collective-permute-start.14 = (bf16[256,128]{1,0:T(8,128)(2,1)S(1)}, bf16[256,128]{1,0:T(8,128)(2,1)S(1)}, u32[]{:S(2)}, u32[]{:S(2)}) collective-permute-start(bf16[256,128]{1,0:T(8,128)(2,1)S(1)} %get-tuple-element.75), channel_id=1, source_target_pairs={{0,3},{1,2},{2,1},{3,0},{4,7},{5,6},{6,5},{7,4},{8,11},{9,10},{10,... | collective-permute-start | bytes 196616 | tf_op jit(solution)/shard_map/ppermute | solution.py:361

commit v3 on v2

--- a/solution.py
+++ b/solution.py
@@ -16,6 +16,7 @@
 LOWEST = -3e38
 HELD = KEEP * BLK
 CHUNK = 512
+LONG = 2**33
 GROUP = 2 * HELD // CHUNK
 QUERY_SCALE = HD**-0.5 * math.log2(math.e)
 BLK_BITS = 7
@@ -25,6 +26,7 @@
 LARGE = pltpu.CompilerParams(vmem_limit_bytes=60 * 2**20)
 PARAMS = pltpu.CompilerParams(vmem_limit_bytes=40 * 2**20)
 ANY = pl.BlockSpec(memory_space=pl.ANY)
+HBM = pl.BlockSpec(memory_space=pltpu.HBM)
 VMEM = pl.BlockSpec(memory_space=pltpu.VMEM)
 
 
@@ -61,16 +63,21 @@
     rows_in = tokens.shape[0]
     rows = KEEP * BLK
     step = 2 * BLK
-    steps = rows_in // step
+    steps = tokens.shape[1] // step
 
     def kernel(mask_any, tok_ref, wk_ref, wv_ref, *rest):
-        outs, (mask_ref, tok, wk, wv, held, sems, out_sems) = rest[:pairs], rest[pairs:]
+        outs, (mask_ref, tok, wk, wv, keys, values, held, sems, out_sems) = rest[:pairs], rest[pairs:]
         load_mask = pltpu.make_async_copy(mask_any, mask_ref, sems.at[0])
-        loads = [pltpu.make_async_copy(wk_ref, wk, sems.at[1]), pltpu.make_async_copy(wv_ref, wv, sems.at[2])]
+        load_mask.start()
+        loads = []
         for c in range(steps):
             at = pl.ds(c * step, step)
-            loads.append(pltpu.make_async_copy(tok_ref.at[at, :], tok.at[at, :], sems.at[3 + c]))
-        for copy in [load_mask] + loads:
+            loads += [
+                pltpu.make_async_copy(wk_ref.at[at, :], wk.at[at, :], sems.at[1 + 3 * c]),
+                pltpu.make_async_copy(wv_ref.at[at, :], wv.at[at, :], sems.at[2 + 3 * c]),
+                pltpu.make_async_copy(tok_ref.at[:, at], tok.at[:, at], sems.at[3 + 3 * c]),
+            ]
+        for copy in loads:
             copy.start()
         load_mask.wait()
         used, rank = block_ranks(mask_ref[...])
@@ -79,19 +86,22 @@
         digit = lax.broadcasted_iota(jnp.int32, picked.shape, 0)
         scale = (1 << (BAND_BITS * jnp.minimum(digit, KEEP))).astype(jnp.float32)
         code = jnp.sum(jnp.where(digit < KEEP, picked * place * scale, 0.0)).astype(jnp.int32)
-        for copy in loads[:2]:
-            copy.wait()
-        low = low_lanes((step, LANES))
+        low = low_lanes((rows_in, LANES))
         for c in range(steps):
             at = pl.ds(c * step, step)
-            loads[2 + c].wait()
-            keys = dot_f32(tok[at, :], wk[...])
-            values = dot_f32(tok[at, :], wv[...])
-            for p in range(pairs):
-                cols = slice(p * LANES, (p + 1) * LANES)
-                k, v = keys[:, cols], values[:, cols]
-                held[p, 0, at, :] = jnp.where(low, k, swap_halves(v)).astype(jnp.bfloat16)
-                held[p, 1, at, :] = jnp.where(low, swap_halves(k), v).astype(jnp.bfloat16)
+            for copy in loads[3 * c : 3 * c + 3]:
+                copy.wait()
+            for total, weight in ((keys, wk), (values, wv)):
+                product = dot_f32(tok[:, at], weight[at, :])
+                if c == 0:
+                    total[...] = product
+                else:
+                    total[...] += product
+        for p in range(pairs):
+            cols = slice(p * LANES, (p + 1) * LANES)
+            k, v = keys[:, cols], values[:, cols]
+            held[p, 0] = jnp.where(low, k, swap_halves(v)).astype(jnp.bfloat16)
+            held[p, 1] = jnp.where(low, swap_halves(k), v).astype(jnp.bfloat16)
         stores = []
         for p in range(pairs):
             for e in range(KEEP):
@@ -114,8 +124,10 @@
             pltpu.VMEM(tokens.shape, jnp.bfloat16),
             pltpu.VMEM(w_key.shape, jnp.bfloat16),
             pltpu.VMEM(w_value.shape, jnp.bfloat16),
+            pltpu.VMEM((rows_in, w_key.shape[1]), jnp.float32),
+            pltpu.VMEM((rows_in, w_key.shape[1]), jnp.float32),
             pltpu.VMEM((pairs, 2, rows_in, LANES), jnp.bfloat16),
-            pltpu.SemaphoreType.DMA((3 + steps,)),
+            pltpu.SemaphoreType.DMA((1 + 3 * steps,)),
             pltpu.SemaphoreType.DMA((pairs, KEEP)),
         ],
         compiler_params=LARGE,
@@ -237,7 +249,7 @@
         kernel,
         out_shape=[jax.ShapeDtypeStruct((2, rows, LANES), jnp.bfloat16)] * pairs
         + [jax.ShapeDtypeStruct((sources * 8, LANES), jnp.float32), jax.ShapeDtypeStruct((2, rows, LANES), jnp.float32)],
-        in_specs=[VMEM] * 3 + [ANY] * len(early),
+        in_specs=[VMEM] * 3 + [HBM] * len(early),
         out_specs=[ANY] * pairs + [VMEM] * 2,
         scratch_shapes=[
             pltpu.VMEM((pairs, 2, rows, LANES), jnp.bfloat16),
@@ -252,40 +264,41 @@
     return out[:pairs], out[pairs], out[pairs + 1]
 
 
-def attend(queries, state, sources, bias, first, parts, cost):
-    rows = queries.shape[1]
-    part = rows // parts
+def attend(queries, state, sources, bias, first, parts, begin, count, cost):
+    part = queries.shape[1] // parts
+    rows = count * part
     states = [] if state is None else [state]
 
     def kernel(q_ref, bias_ref, *rest):
         state_refs, rest = rest[: len(states)], rest[len(states) :]
         srcs, rest = rest[: len(sources)], rest[len(sources) :]
-        outs, scratch = rest[:parts], rest[parts:]
+        outs, scratch = rest[:count], rest[count:]
         tables = Tables(*scratch, srcs)
         tables.fill(bias_ref, first)
         lane = lax.broadcasted_iota(jnp.int32, (rows, LANES), 1)
         low = lane < HD
+        taken = slice(begin * part, begin * part + rows)
         sums = []
         for h in range(2):
             if states:
-                total_sum = state_refs[0][h]
+                total_sum = state_refs[0][h, taken]
                 peak = jnp.max(jnp.where(lane == 1, total_sum, LOWEST), axis=1, keepdims=True)
                 total_sum = jnp.where(lane == 1, pltpu.roll(total_sum, 1, 1), total_sum)
             else:
                 peak = jnp.full((rows, 1), LOWEST, jnp.float32)
                 total_sum = jnp.zeros((rows, LANES), jnp.float32)
-            sums.append(tables.sweep(q_ref[h], h, peak, total_sum)[1])
+            sums.append(tables.sweep(q_ref[h, taken], h, peak, total_sum)[1])
         top = jnp.where(low, swap_halves(sums[0]), sums[1])
         mass = jnp.where(low, sums[0], swap_halves(sums[1]))
         out = (top / mass).astype(jnp.bfloat16)
-        for k in range(parts):
+        for k in range(count):
             outs[k][...] = out[k * part : (k + 1) * part, :]
 
     return pl.pallas_call(
         kernel,
-        out_shape=[jax.ShapeDtypeStruct((part, LANES), jnp.bfloat16)] * parts,
-        in_specs=[VMEM, VMEM] + [VMEM] * len(states) + [ANY] * len(sources),
-        out_specs=[VMEM] * parts,
+        out_shape=[jax.ShapeDtypeStruct((part, LANES), jnp.bfloat16)] * count,
+        in_specs=[VMEM, VMEM] + [VMEM] * len(states) + [HBM] * len(sources),
+        out_specs=[VMEM] * count,
         scratch_shapes=table_scratch(len(sources)),
         compiler_params=PARAMS,
         cost_estimate=pl.CostEstimate(flops=cost, bytes_accessed=0, transcendentals=0),
@@ -293,58 +306,69 @@
     )(queries, bias, *states, *sources)
 
 
-def assemble(w_mine, w_other, tiles):
-    quarters, heads = 2 * tiles, w_mine.shape[1]
-    piece, width = w_mine.shape[2:]
+def project_out(attended, w_mine, w_other, tiles):
+    heads, depth, width = w_mine.shape
+    pairs = len(attended[0])
+    rows = attended[0][0].shape[0]
+    piece = depth // tiles
     order = [0]
     bit = heads // 2
     while bit:
         order += [bit ^ k for k in order]
         bit //= 2
-
-    def kernel(mine_ref, other_ref, out_ref, sems):
+    pieces = [attended[k][p] for k in order for p in range(pairs)]
+    direct = depth % LANES == 0
+
+    def kernel(*rest):
+        refs, (mine_ref, other_ref, out_ref, *scratch) = rest[: heads * pairs], rest[heads * pairs :]
         quarter = (lax.axis_index("band") & 1) * tiles + lax.axis_index("tiles")
-        copies = []
-        for s in range(quarters):
-            ref = other_ref if s >= tiles else mine_ref
-            for i, k in enumerate(order):
-                begin = pl.multiple_of((quarters * k + (quarter ^ s)) * piece, piece)
-                copy = pltpu.make_async_copy(ref.at[s % tiles, i], out_ref.at[pl.ds(begin, piece), :], sems.at[s, i])
+        lane = lax.broadcasted_iota(jnp.int32, (rows, LANES), 1)
+        groups = []
+        for i in range(heads):
+            group = [refs[i * pairs + p][...].astype(jnp.float32) for p in range(pairs)]
+            size = piece
+            while size < depth * 2:
+                flip = (quarter & (size // piece)) > 0
+                if size < LANES:
+                    moved = [
+                        jnp.where((lane & size) > 0, pltpu.roll(x, size, 1), pltpu.roll(x, LANES - size, 1)) for x in group
+                    ]
+                else:
+                    moved = [group[p ^ (size // LANES)] for p in range(pairs)]
+                group = [jnp.where(flip, m, x) for m, x in zip(moved, group)]
+                size *= 2
+            groups.append([x.astype(jnp.bfloat16) for x in group])
+        if direct:
+            half = depth // LANES
+            near_cols = jnp.concatenate([x for group in groups for x in group[:half]], axis=1)
+            far_cols = jnp.concatenate([x for group in groups for x in group[half:]], axis=1)
+            total = dot_f32(near_cols, mine_ref[...].reshape(heads * depth, width))
+            total += dot_f32(far_cols, other_ref[...].reshape(heads * depth, width))
+        else:
+            w, sems = scratch
+            copies = [
+                pltpu.make_async_copy(ref, w.at[:, pl.ds(s * depth, depth), :], sems.at[s])
+                for s, ref in enumerate((mine_ref, other_ref))
+            ]
+            for copy in copies:
                 copy.start()
-                copies.append(copy)
-        for copy in copies:
-            copy.wait()
-
-    return pl.pallas_call(
-        kernel,
-        out_shape=jax.ShapeDtypeStruct((quarters * heads * piece, width), jnp.bfloat16),
-        in_specs=[ANY] * 2,
-        out_specs=ANY,
-        scratch_shapes=[pltpu.SemaphoreType.DMA((quarters, heads))],
-        compiler_params=SMALL,
-        cost_estimate=FREE,
-        name="assemble",
-    )(w_mine, w_other)
-
-
-def project_out(attended, w_full):
-    pieces = [a for group in attended for a in group]
-    rows, width = pieces[0].shape[0], w_full.shape[1]
-
-    def kernel(*rest):
-        w_ref, out_ref = rest[-2:]
-        rows_all = jnp.concatenate([ref[...] for ref in rest[:-2]], axis=1)
-        out_ref[...] = dot_f32(rows_all, w_ref[...]).astype(jnp.bfloat16)
-
+            for copy in copies:
+                copy.wait()
+            cols = jnp.concatenate([x for group in groups for x in group], axis=1)
+            total = dot_f32(cols, w[...].reshape(heads * 2 * depth, width))
+        out_ref[...] = total.astype(jnp.bfloat16)
+
+    scratch = [] if direct else [pltpu.VMEM((heads, 2 * depth, width), jnp.bfloat16), pltpu.SemaphoreType.DMA((2,))]
     return pl.pallas_call(
         kernel,
         out_shape=jax.ShapeDtypeStruct((rows, width), jnp.bfloat16),
-        in_specs=[VMEM] * (len(pieces) + 1),
+        in_specs=[VMEM] * len(pieces) + [VMEM if direct else ANY] * 2,
         out_specs=VMEM,
+        scratch_shapes=scratch,
         compiler_params=SMALL,
         cost_estimate=FREE,
         name="project_out",
-    )(*pieces, w_full)
+    )(*pieces, w_mine, w_other)
 
 
 def on_device(sizes, tokens, w_query, w_key, w_value, w_out, block_mask):
@@ -392,26 +416,36 @@
         w_mine, arriving = widen(w_mine, arriving, bit)
 
     attended = [[] for _ in range(heads)]
+
+    def exchange(pieces, first):
+        for k, piece in enumerate(pieces, first):
+            attended[k].append(piece if k == 0 else along_head(piece, k))
+
+    last = pairs - 1
+    if last == 0:
+        w_mine = jnp.concatenate([w_mine, arriving])
+        arriving = other_tiles(w_mine)
     for p in range(pairs):
         if p > 0:
             far[p], pieces = lax.optimization_barrier((far[p], pieces))
-        late = []
+        sources = [] if p == 0 else [kv[p], near[p]]
         for one in far[p]:
-            late += [one, to_sibling(one)]
-        if p == 0:
-            pieces = attend(queries[0], state, late, bias, 2, heads, 2**33)
-            pieces, arriving = lax.optimization_barrier((pieces, arriving))
-            w_mine = jnp.concatenate([w_mine, arriving])[None]
-            arriving = other_tiles(w_mine)
+            sources += [one, to_sibling(one)]
+        held, first = (state, 2) if p == 0 else (None, 0)
+        if p < last:
+            pieces = attend(queries[p], held, sources, bias, first, heads, 0, heads, LONG)
+            if p == 0:
+                pieces, arriving = lax.optimization_barrier((pieces, arriving))
+                w_mine = jnp.concatenate([w_mine, arriving])
+                arriving = other_tiles(w_mine)
+            exchange(pieces, 0)
         else:
-            pieces = attend(queries[p], None, [kv[p], near[p]] + late, bias, 0, heads, 0)
-            attended, pieces, arriving = lax.optimization_barrier((attended, pieces, arriving))
-        attended[0].append(pieces[0])
-        for k in range(1, heads):
-            attended[k].append(along_head(pieces[k], k))
-    w_mine = jnp.concatenate([w_mine] + arriving)
-    w_full = assemble(w_mine, to_sibling(w_mine), tiles)
-    return project_out(attended, w_full)
+            pieces = attend(queries[p], held, sources, bias, first, heads, 1, heads - 1, 0)
+            pieces, attended, arriving, sources[-1] = lax.optimization_barrier((pieces, attended, arriving, sources[-1]))
+            exchange(pieces, 1)
+            exchange(attend(queries[p], held, sources, bias, first, heads, 0, 1, LONG), 0)
+    w_mine = jnp.concatenate([w_mine] + arriving, axis=1)
+    return project_out(attended, w_mine, to_sibling(w_mine), tiles)
 
 
 def solution(mesh):

time: 55.5 us -> 53.1 us (0.957)
  waiting for transfers between devices: 4.68 us -> 2.72 us
    pallas_call x2 -> x3, Pallas kernels: 13.9 us -> 17.1 us  [attend(): pl.pallas_call(kernel, out_shape=[jax.ShapeDtypeStruct((part, LANES), jnp...]
    pallas_call x1 -> x0, Pallas kernels: 2.87 us -> none  [assemble(): pl.pallas_call(kernel, out_shape=jax.ShapeDtypeStruct((quarters * heads *...]
    ppermute x8, waiting for transfers between devices: 4.08 us -> 2.13 us  [along_head(): return lax.ppermute(array, 'head', [(i, i ^ k) for i in range(heads)])]
    pallas_call x1, Pallas kernels: 4.6 us -> 3.88 us  [project_kv(): pl.pallas_call(kernel, out_shape=[jax.ShapeDtypeStruct((2, rows, LANES),...]
  transfers between devices with their start and end apart: 16 -> 16, of which waited for: 4 -> 3; matrix products, arithmetic and copies ran while one was open for 0% -> 0% of each run, Pallas kernels for 41% -> 43%
where the time goes in v3:
time: 53.1 us; the launch traced here: 52.9 us
  Pallas kernels  28.3 us (53%)
  starting transfers between devices  20.6 us (39%)
  waiting for transfers between devices  2.72 us (5%)
  local copies, waits for them, and re-layouts  1.02 us (2%)
    pallas_call x3, Pallas kernels, attend(): pl.pallas_call(kernel, out_shape=[jax.ShapeDtypeStruct((part, LANES), jnp...  17.1 us
    ppermute x8, starting transfers between devices, along_head(): return lax.ppermute(array, 'head', [(i, i ^ k) for i in range(heads)])  13.6 us
    pallas_call x1, Pallas kernels, begin_attention(): pl.pallas_call(kernel, out_shape=[jax.ShapeDtypeStruct((2, rows, LANES),...  5.73 us
    ppermute x7, starting transfers between devices, along_band(): return lax.ppermute(array, 'band', [(i, goes_to(i)) for i in range(bands)])  5.43 us
    pallas_call x1, Pallas kernels, project_kv(): pl.pallas_call(kernel, out_shape=[jax.ShapeDtypeStruct((2, rows, LANES),...  3.88 us
    ppermute x8, waiting for transfers between devices, along_head(): return lax.ppermute(array, 'head', [(i, i ^ k) for i in range(heads)])  2.13 us
    pallas_call x1, Pallas kernels, project_out(): pl.pallas_call(kernel, out_shape=jax.ShapeDtypeStruct((rows, width), jnp....  1.6 us
    ppermute x1, starting transfers between devices, other_tiles(): lax.ppermute(array, 'tiles', [(i, i ^ s) for i in range(tiles)])  1.58 us
  transfers between devices with their start and end apart: 16, of which 3 were waited for; matrix products, arithmetic and copies ran while one was open for 0% of the time, Pallas kernels for 43%

profile of v3, /device:TPU:0, one launch (start us, length us, event | category | flops | bytes accessed | tf_op | source)
XLA Modules:
  0.0 52.9 jit_solution(464790986025764341)
XLA Ops:
  0.0 0.0 copy-start
  0.0 3.9 %project_kv.1 = (bf16[2,768,128]{2,1,0:T(8,128)(2,1)}, bf16[2,768,128]{2,1,0:T(8,128)(2,1)}) custom-call(s32[32,32]{1,0:T(8,128)} %mask_ref.1, bf16[1024,1024]{1,0:T(8,128)(2,1)} %tok.1, bf16[1024,256]{1,0:T(8,128)(2,1)} %wk_ref.1, bf16[1024,256]{1,0:T(8,128)(2,1)} %wv_ref.1), custom_call_target="tpu_custom_call" | custom-call | tf_op jit(solution)/shard_map/project_kv/pallas_call | solution.py:117
  3.9 0.0 copy-start.3
  3.9 0.5 collective-permute-start.1
  4.4 2.6 %collective-permute-start = (bf16[2,768,128]{2,1,0:T(8,128)(2,1)}, bf16[2,768,128]{2,1,0:T(8,128)(2,1)}, u32[]{:S(2)}, u32[]{:S(2)}) collective-permute-start(bf16[2,768,128]{2,1,0:T(8,128)(2,1)} %get-tuple-element.42.rest_0_), channel_id=1, source_target_pairs={{0,8},{4,12},{8,0},{12,4},{1,9},{5,13},{9,1},{13,5},{2,10},{6,14},... | collective-permute-start | bytes 1179656 | tf_op jit(solution)/shard_map/ppermute | solution.py:379
  7.0 0.0 copy-done
  7.0 2.7 %collective-permute-start.2 = (bf16[1,64,1024]{2,1,0:T(8,128)(2,1)S(1)}, bf16[1,64,1024]{2,1,0:T(8,128)(2,1)S(1)}, u32[]{:S(2)}, u32[]{:S(2)}) collective-permute-start(bf16[1,64,1024]{2,1,0:T(8,128)(2,1)S(1)} %bitcast.1), channel_id=1, source_target_pairs={{0,2},{1,3},{2,0},{3,1},{4,6},{5,7},{6,4},{7,5},{8,10},{9,11},{10,... | collective-permute-start | bytes 393224 | tf_op jit(solution)/shard_map/ppermute | solution.py:385
  9.7 0.0 collective-permute-done.1.rest_1_
  9.7 0.0 copy-done.5
  9.7 0.0 copy-done.1
  9.7 0.0 copy-done.2
  9.7 0.0 copy-start.4
  9.7 1.0 %copy-done.4 = bf16[2,768,128]{2,1,0:T(8,128)(2,1)S(1)} copy-done((bf16[2,768,128]{2,1,0:T(8,128)(2,1)S(1)}, bf16[2,768,128]{2,1,0:T(8,128)(2,1)}, u32[]{:S(2)}) %copy-start.4) | copy-done | bytes 393240
  10.7 5.7 %begin_attention.1 = (bf16[2,1024,128]{2,1,0:T(8,128)(2,1)S(1)}, bf16[2,1024,128]{2,1,0:T(8,128)(2,1)S(1)}, f32[32,128]{1,0:T(8,128)S(1)}, f32[2,1024,128]{2,1,0:T(8,128)S(1)}) custom-call(s32[32,32]{1,0:T(8,128)S(1)} %copy-done.5, bf16[1024,1024]{1,0:T(8,128)(2,1)S(1)} %copy-done.1, bf16[1024,256]{1,0:T(8,128)(2,1)S(1)} %copy-done.2, ...), custom_call_target="tpu_custom_call" | custom-call | tf_op jit(solution)/shard_map/begin_attention/pallas_call | solution.py:248
  16.4 0.0 collective-permute-done.2
  16.4 0.6 %collective-permute-done.rest_1_ = bf16[2,768,128]{2,1,0:T(8,128)(2,1)} collective-permute-done((bf16[2,768,128]{2,1,0:T(8,128)(2,1)}, bf16[2,768,128]{2,1,0:T(8,128)(2,1)}, u32[]{:S(2)}, u32[]{:S(2)}) %collective-permute-start) | collective-permute-done | bytes 393248 | tf_op jit(solution)/shard_map/ppermute | solution.py:379
  17.0 0.0 collective-permute-start.5
  17.0 1.8 %collective-permute-start.4 = (bf16[2,768,128]{2,1,0:T(8,128)(2,1)S(1)}, bf16[2,768,128]{2,1,0:T(8,128)(2,1)S(1)}, u32[]{:S(2)}, u32[]{:S(2)}) collective-permute-start(bf16[2,768,128]{2,1,0:T(8,128)(2,1)S(1)} %copy-done.3), channel_id=1, source_target_pairs={{0,8},{4,12},{8,0},{12,4},{1,9},{5,13},{9,1},{13,5},{2,10},{6,14},... | collective-permute-start | bytes 1179656 | tf_op jit(solution)/shard_map/ppermute | solution.py:379
  18.8 1.6 %collective-permute-start.6 = (bf16[2,64,1024]{2,1,0:T(8,128)(2,1)S(1)}, bf16[2,64,1024]{2,1,0:T(8,128)(2,1)S(1)}, u32[]{:S(2)}, u32[]{:S(2)}) collective-permute-start(bf16[2,64,1024]{2,1,0:T(8,128)(2,1)S(1)} %pad_maximum_fusion.2), channel_id=1, source_target_pairs={{0,1},{1,0},{2,3},{3,2},{4,5},{5,4},{6,7},{7,6},{8,9},{9,8},{10,11... | collective-permute-start | bytes 786440 | tf_op jit(solution)/shard_map/ppermute | solution.py:385
  20.5 0.0 collective-permute-done.5.rest_2_
  20.5 5.4 %attend.3 = (bf16[256,128]{1,0:T(8,128)(2,1)S(1)}, bf16[256,128]{1,0:T(8,128)(2,1)S(1)}, bf16[256,128]{1,0:T(8,128)(2,1)S(1)}, bf16[256,128]{1,0:T(8,128)(2,1)S(1)}) custom-call(bf16[2,1024,128]{2,1,0:T(8,128)(2,1)S(1)} %get-tuple-element.49.q_ref, f32[32,128]{1,0:T(8,128)S(1)} %get-tuple-element.47.bias_ref, f32[2,1024,128]{2,1,0:T(8,128)S(1)} %get-tuple-element.50.rest_0_, ...), custom_call_target="tpu_custom_call" | custom-call | flops 8589934592 | tf_op jit(solution)/shard_map/attend/pallas_call | solution.py:297
  25.8 1.5 %collective-permute-done.6 = bf16[2,64,1024]{2,1,0:T(8,128)(2,1)S(1)} collective-permute-done((bf16[2,64,1024]{2,1,0:T(8,128)(2,1)S(1)}, bf16[2,64,1024]{2,1,0:T(8,128)(2,1)S(1)}, u32[]{:S(2)}, u32[]{:S(2)}) %collective-permute-start.6) | collective-permute-done | bytes 262176 | tf_op jit(solution)/shard_map/ppermute | solution.py:385
  27.3 0.1 pad_maximum_fusion.1
  27.4 1.6 %collective-permute-start.11 = (bf16[4,64,1024]{2,1,0:T(8,128)(2,1)S(1)}, bf16[4,64,1024]{2,1,0:T(8,128)(2,1)S(1)}, u32[]{:S(2)}, u32[]{:S(2)}) collective-permute-start(bf16[4,64,1024]{2,1,0:T(8,128)(2,1)S(1)} %pad_maximum_fusion.1), channel_id=1, source_target_pairs={{0,16},{16,0},{1,17},{17,1},{2,18},{18,2},{3,19},{19,3},{4,20},{20... | collective-permute-start | bytes 1572872 | tf_op jit(solution)/shard_map/ppermute | solution.py:404
  29.0 0.0 collective-permute-start.3
  29.0 0.0 collective-permute-done.4.rest_2_
  29.0 0.5 collective-permute-start.7
  29.5 1.6 %collective-permute-start.8 = (bf16[256,128]{1,0:T(8,128)(2,1)S(1)}, bf16[256,128]{1,0:T(8,128)(2,1)S(1)}, u32[]{:S(2)}, u32[]{:S(2)}) collective-permute-start(bf16[256,128]{1,0:T(8,128)(2,1)S(1)} %get-tuple-element.58), channel_id=1, source_target_pairs={{0,1},{1,0},{2,3},{3,2},{4,5},{5,4},{6,7},{7,6},{8,9},{9,8},{10,11... | collective-permute-start | bytes 196616 | tf_op jit(solution)/shard_map/ppermute | solution.py:385
  31.1 2.6 %collective-permute-start.9 = (bf16[256,128]{1,0:T(8,128)(2,1)S(1)}, bf16[256,128]{1,0:T(8,128)(2,1)S(1)}, u32[]{:S(2)}, u32[]{:S(2)}) collective-permute-start(bf16[256,128]{1,0:T(8,128)(2,1)S(1)} %get-tuple-element.59), channel_id=1, source_target_pairs={{0,2},{1,3},{2,0},{3,1},{4,6},{5,7},{6,4},{7,5},{8,10},{9,11},{10,... | collective-permute-start | bytes 196616 | tf_op jit(solution)/shard_map/ppermute | solution.py:385
  33.6 0.0 collective-permute-done.3.rest_1_
  33.6 0.6 %collective-permute-start.10 = (bf16[256,128]{1,0:T(8,128)(2,1)S(1)}, bf16[256,128]{1,0:T(8,128)(2,1)S(1)}, u32[]{:S(2)}, u32[]{:S(2)}) collective-permute-start(bf16[256,128]{1,0:T(8,128)(2,1)S(1)} %get-tuple-element.60), channel_id=1, source_target_pairs={{0,3},{1,2},{2,1},{3,0},{4,7},{5,6},{6,5},{7,4},{8,11},{9,10},{10,... | collective-permute-start | bytes 196616 | tf_op jit(solution)/shard_map/ppermute | solution.py:385
  34.3 0.0 collective-permute-done.7.rest_3_
  34.3 6.9 %attend.4 = (bf16[256,128]{1,0:T(8,128)(2,1)S(1)}, bf16[256,128]{1,0:T(8,128)(2,1)S(1)}, bf16[256,128]{1,0:T(8,128)(2,1)S(1)}) custom-call(bf16[2,1024,128]{2,1,0:T(8,128)(2,1)S(1)} %get-tuple-element.46.q_ref, f32[32,128]{1,0:T(8,128)S(1)} %get-tuple-element.47.bias_ref, bf16[2,768,128]{2,1,0:T(8,128)(2,1)S(1)} %copy-done.3, ...), custom_call_target="tpu_custom_call" | custom-call | tf_op jit(solution)/shard_map/attend/pallas_call | solution.py:297
  41.2 0.0 collective-permute-done.8.rest_4_
  41.2 0.0 collective-permute-done.9.rest_2_
  41.2 0.0 collective-permute-done.10.rest_6_
  41.3 0.0 collective-permute-done.11
  41.3 0.1 pad_maximum_fusion.rest_8_
  41.3 0.1 collective-permute-start.15
  41.4 2.1 %collective-permute-start.12 = (bf16[256,128]{1,0:T(8,128)(2,1)S(1)}, bf16[256,128]{1,0:T(8,128)(2,1)S(1)}, u32[]{:S(2)}, u32[]{:S(2)}) collective-permute-start(bf16[256,128]{1,0:T(8,128)(2,1)S(1)} %get-tuple-element.69), channel_id=1, source_target_pairs={{0,2},{1,3},{2,0},{3,1},{4,6},{5,7},{6,4},{7,5},{8,10},{9,11},{10,... | collective-permute-start | bytes 196616 | tf_op jit(solution)/shard_map/ppermute | solution.py:385
  43.5 1.7 %collective-permute-start.13 = (bf16[256,128]{1,0:T(8,128)(2,1)S(1)}, bf16[256,128]{1,0:T(8,128)(2,1)S(1)}, u32[]{:S(2)}, u32[]{:S(2)}) collective-permute-start(bf16[256,128]{1,0:T(8,128)(2,1)S(1)} %get-tuple-element.71), channel_id=1, source_target_pairs={{0,1},{1,0},{2,3},{3,2},{4,5},{5,4},{6,7},{7,6},{8,9},{9,8},{10,11... | collective-permute-start | bytes 196616 | tf_op jit(solution)/shard_map/ppermute | solution.py:385
  45.2 0.6 %collective-permute-start.14 = (bf16[256,128]{1,0:T(8,128)(2,1)S(1)}, bf16[256,128]{1,0:T(8,128)(2,1)S(1)}, u32[]{:S(2)}, u32[]{:S(2)}) collective-permute-start(bf16[256,128]{1,0:T(8,128)(2,1)S(1)} %get-tuple-element.73), channel_id=1, source_target_pairs={{0,3},{1,2},{2,1},{3,0},{4,7},{5,6},{6,5},{7,4},{8,11},{9,10},{10,... | collective-permute-start | bytes 196616 | tf_op jit(solution)/shard_map/ppermute | solution.py:385
  45.9 4.8 %attend.5.rest_1_ = bf16[256,128]{1,0:T(8,128)(2,1)S(1)} custom-call(bf16[2,1024,128]{2,1,0:T(8,128)(2,1)S(1)} %get-tuple-element.46.q_ref, f32[32,128]{1,0:T(8,128)S(1)} %get-tuple-element.47.bias_ref, bf16[2,768,128]{2,1,0:T(8,128)(2,1)S(1)} %copy-done.3, bf16[2,768,128]{2,1,0:T(8,128)(2,1)S(1)} %collective-permute-done.3.rest_1_, ...), custom_call_target="tpu_custom_call" | custom-call | flops 8589934592 | tf_op jit(solution)/shard_map/attend/pallas_call | solution.py:297
  50.6 0.0 collective-permute-done.12.rest_3_
  50.6 0.0 collective-permute-done.13.rest_5_
  50.7 0.6 %collective-permute-done.14.rest_7_ = bf16[256,128]{1,0:T(8,128)(2,1)S(1)} collective-permute-done((bf16[256,128]{1,0:T(8,128)(2,1)S(1)}, bf16[256,128]{1,0:T(8,128)(2,1)S(1)}, u32[]{:S(2)}, u32[]{:S(2)}) %collective-permute-start.14) | collective-permute-done | bytes 65568 | tf_op jit(solution)/shard_map/ppermute | solution.py:385
  51.3 0.0 collective-permute-done.15.rest_9_
  51.3 1.6 %project_out.1 = bf16[256,1024]{1,0:T(8,128)(2,1)} custom-call(bf16[256,128]{1,0:T(8,128)(2,1)S(1)} %get-tuple-element.66.rest_0_, bf16[256,128]{1,0:T(8,128)(2,1)S(1)} %attend.5.rest_1_, bf16[256,128]{1,0:T(8,128)(2,1)S(1)} %collective-permute-done.9.rest_2_, bf16[256,128]{1,0:T(8,128)(2,1)S(1)} %collective-permute-done.12.rest_3_, ...), custom_call_target="tpu_custom_call" | custom-call | tf_op jit(solution)/shard_map/project_out/pallas_call | solution.py:362
  (6 shorter events, 0.0 us)
Async XLA Ops:
  0.0 7.0 %copy-start = (bf16[256,1024]{1,0:T(8,128)(2,1)S(1)}, bf16[256,1024]{1,0:T(8,128)(2,1)}, u32[]{:S(2)}) copy-start(bf16[256,1024]{1,0:T(8,128)(2,1)} %param.10) | copy-start | bytes 1572868
  0.0 9.7 %copy-start.5 = (s32[32,32]{1,0:T(8,128)S(1)}, s32[32,32]{1,0:T(8,128)}, u32[]{:S(2)}) copy-start(s32[32,32]{1,0:T(8,128)} %mask_ref.1) | copy-start | bytes 12292
  0.0 9.7 %copy-start.1 = (bf16[1024,1024]{1,0:T(8,128)(2,1)S(1)}, bf16[1024,1024]{1,0:T(8,128)(2,1)}, u32[]{:S(2)}) copy-start(bf16[1024,1024]{1,0:T(8,128)(2,1)} %tok.1) | copy-start | bytes 6291460
  0.0 9.7 %copy-start.2 = (bf16[1024,256]{1,0:T(8,128)(2,1)S(1)}, bf16[1024,256]{1,0:T(8,128)(2,1)}, u32[]{:S(2)}) copy-start(bf16[1024,256]{1,0:T(8,128)(2,1)} %w.1) | copy-start | bytes 1572868
  3.9 13.1 %copy-start.3 = (bf16[2,768,128]{2,1,0:T(8,128)(2,1)S(1)}, bf16[2,768,128]{2,1,0:T(8,128)(2,1)}, u32[]{:S(2)}) copy-start(bf16[2,768,128]{2,1,0:T(8,128)(2,1)} %get-tuple-element.48.rest_0_) | copy-start | bytes 1179652
  3.9 5.8 %collective-permute-start.1 = (bf16[2,768,128]{2,1,0:T(8,128)(2,1)}, bf16[2,768,128]{2,1,0:T(8,128)(2,1)}, u32[]{:S(2)}, u32[]{:S(2)}) collective-permute-start(bf16[2,768,128]{2,1,0:T(8,128)(2,1)} %get-tuple-element.42.rest_0_), channel_id=1, source_target_pairs={{0,4},{4,0},{8,12},{12,8},{1,5},{5,1},{9,13},{13,9},{2,6},{6,2},{1... | collective-permute-start | bytes 1179656 | tf_op jit(solution)/shard_map/ppermute | solution.py:379
  4.4 12.6 %collective-permute-start = (bf16[2,768,128]{2,1,0:T(8,128)(2,1)}, bf16[2,768,128]{2,1,0:T(8,128)(2,1)}, u32[]{:S(2)}, u32[]{:S(2)}) collective-permute-start(bf16[2,768,128]{2,1,0:T(8,128)(2,1)} %get-tuple-element.42.rest_0_), channel_id=1, source_target_pairs={{0,8},{4,12},{8,0},{12,4},{1,9},{5,13},{9,1},{13,5},{2,10},{6,14},... | collective-permute-start | bytes 1179656 | tf_op jit(solution)/shard_map/ppermute | solution.py:379
  7.0 9.4 %collective-permute-start.2 = (bf16[1,64,1024]{2,1,0:T(8,128)(2,1)S(1)}, bf16[1,64,1024]{2,1,0:T(8,128)(2,1)S(1)}, u32[]{:S(2)}, u32[]{:S(2)}) collective-permute-start(bf16[1,64,1024]{2,1,0:T(8,128)(2,1)S(1)} %bitcast.1), channel_id=1, source_target_pairs={{0,2},{1,3},{2,0},{3,1},{4,6},{5,7},{6,4},{7,5},{8,10},{9,11},{10,... | collective-permute-start | bytes 393224 | tf_op jit(solution)/shard_map/ppermute | solution.py:385
  9.7 1.0 %copy-start.4 = (bf16[2,768,128]{2,1,0:T(8,128)(2,1)S(1)}, bf16[2,768,128]{2,1,0:T(8,128)(2,1)}, u32[]{:S(2)}) copy-start(bf16[2,768,128]{2,1,0:T(8,128)(2,1)} %get-tuple-element.42.rest_0_) | copy-start | bytes 1179652
  17.0 3.4 %collective-permute-start.5 = (bf16[2,768,128]{2,1,0:T(8,128)(2,1)}, bf16[2,768,128]{2,1,0:T(8,128)(2,1)S(1)}, u32[]{:S(2)}, u32[]{:S(2)}) collective-permute-start(bf16[2,768,128]{2,1,0:T(8,128)(2,1)} %collective-permute-done.rest_1_), channel_id=1, source_target_pairs={{0,4},{4,0},{8,12},{12,8},{1,5},{5,1},{9,13},{13,9},{2,6},{6,2},{1... | collective-permute-start | bytes 1179656 | tf_op jit(solution)/shard_map/ppermute | solution.py:379
  17.0 11.9 %collective-permute-start.4 = (bf16[2,768,128]{2,1,0:T(8,128)(2,1)S(1)}, bf16[2,768,128]{2,1,0:T(8,128)(2,1)S(1)}, u32[]{:S(2)}, u32[]{:S(2)}) collective-permute-start(bf16[2,768,128]{2,1,0:T(8,128)(2,1)S(1)} %copy-done.3), channel_id=1, source_target_pairs={{0,8},{4,12},{8,0},{12,4},{1,9},{5,13},{9,1},{13,5},{2,10},{6,14},... | collective-permute-start | bytes 1179656 | tf_op jit(solution)/shard_map/ppermute | solution.py:379
  18.8 8.5 %collective-permute-start.6 = (bf16[2,64,1024]{2,1,0:T(8,128)(2,1)S(1)}, bf16[2,64,1024]{2,1,0:T(8,128)(2,1)S(1)}, u32[]{:S(2)}, u32[]{:S(2)}) collective-permute-start(bf16[2,64,1024]{2,1,0:T(8,128)(2,1)S(1)} %pad_maximum_fusion.2), channel_id=1, source_target_pairs={{0,1},{1,0},{2,3},{3,2},{4,5},{5,4},{6,7},{7,6},{8,9},{9,8},{10,11... | collective-permute-start | bytes 786440 | tf_op jit(solution)/shard_map/ppermute | solution.py:385
  27.4 13.9 %collective-permute-start.11 = (bf16[4,64,1024]{2,1,0:T(8,128)(2,1)S(1)}, bf16[4,64,1024]{2,1,0:T(8,128)(2,1)S(1)}, u32[]{:S(2)}, u32[]{:S(2)}) collective-permute-start(bf16[4,64,1024]{2,1,0:T(8,128)(2,1)S(1)} %pad_maximum_fusion.1), channel_id=1, source_target_pairs={{0,16},{16,0},{1,17},{17,1},{2,18},{18,2},{3,19},{19,3},{4,20},{20... | collective-permute-start | bytes 1572872 | tf_op jit(solution)/shard_map/ppermute | solution.py:404
  29.0 4.7 %collective-permute-start.3 = (bf16[2,768,128]{2,1,0:T(8,128)(2,1)S(1)}, bf16[2,768,128]{2,1,0:T(8,128)(2,1)S(1)}, u32[]{:S(2)}, u32[]{:S(2)}) collective-permute-start(bf16[2,768,128]{2,1,0:T(8,128)(2,1)S(1)} %copy-done.3), channel_id=1, source_target_pairs={{0,4},{4,0},{8,12},{12,8},{1,5},{5,1},{9,13},{13,9},{2,6},{6,2},{1... | collective-permute-start | bytes 1179656 | tf_op jit(solution)/shard_map/ppermute | solution.py:379
  29.0 5.3 %collective-permute-start.7 = (bf16[2,768,128]{2,1,0:T(8,128)(2,1)S(1)}, bf16[2,768,128]{2,1,0:T(8,128)(2,1)S(1)}, u32[]{:S(2)}, u32[]{:S(2)}) collective-permute-start(bf16[2,768,128]{2,1,0:T(8,128)(2,1)S(1)} %collective-permute-done.4.rest_2_), channel_id=1, source_target_pairs={{0,4},{4,0},{8,12},{12,8},{1,5},{5,1},{9,13},{13,9},{2,6},{6,2},{1... | collective-permute-start | bytes 1179656 | tf_op jit(solution)/shard_map/ppermute | solution.py:379
  29.5 11.8 %collective-permute-start.8 = (bf16[256,128]{1,0:T(8,128)(2,1)S(1)}, bf16[256,128]{1,0:T(8,128)(2,1)S(1)}, u32[]{:S(2)}, u32[]{:S(2)}) collective-permute-start(bf16[256,128]{1,0:T(8,128)(2,1)S(1)} %get-tuple-element.58), channel_id=1, source_target_pairs={{0,1},{1,0},{2,3},{3,2},{4,5},{5,4},{6,7},{7,6},{8,9},{9,8},{10,11... | collective-permute-start | bytes 196616 | tf_op jit(solution)/shard_map/ppermute | solution.py:385
  31.1 10.2 %collective-permute-start.9 = (bf16[256,128]{1,0:T(8,128)(2,1)S(1)}, bf16[256,128]{1,0:T(8,128)(2,1)S(1)}, u32[]{:S(2)}, u32[]{:S(2)}) collective-permute-start(bf16[256,128]{1,0:T(8,128)(2,1)S(1)} %get-tuple-element.59), channel_id=1, source_target_pairs={{0,2},{1,3},{2,0},{3,1},{4,6},{5,7},{6,4},{7,5},{8,10},{9,11},{10,... | collective-permute-start | bytes 196616 | tf_op jit(solution)/shard_map/ppermute | solution.py:385
  33.6 7.6 %collective-permute-start.10 = (bf16[256,128]{1,0:T(8,128)(2,1)S(1)}, bf16[256,128]{1,0:T(8,128)(2,1)S(1)}, u32[]{:S(2)}, u32[]{:S(2)}) collective-permute-start(bf16[256,128]{1,0:T(8,128)(2,1)S(1)} %get-tuple-element.60), channel_id=1, source_target_pairs={{0,3},{1,2},{2,1},{3,0},{4,7},{5,6},{6,5},{7,4},{8,11},{9,10},{10,... | collective-permute-start | bytes 196616 | tf_op jit(solution)/shard_map/ppermute | solution.py:385
  41.3 10.0 %collective-permute-start.15 = (bf16[4,128,1024]{2,1,0:T(8,128)(2,1)S(1)}, bf16[4,128,1024]{2,1,0:T(8,128)(2,1)S(1)}, u32[]{:S(2)}, u32[]{:S(2)}) collective-permute-start(bf16[4,128,1024]{2,1,0:T(8,128)(2,1)S(1)} %pad_maximum_fusion.rest_8_), channel_id=1, source_target_pairs={{0,4},{4,0},{8,12},{12,8},{1,5},{5,1},{9,13},{13,9},{2,6},{6,2},{1... | collective-permute-start | bytes 3145736 | tf_op jit(solution)/shard_map/ppermute | solution.py:379
  41.4 9.2 %collective-permute-start.12 = (bf16[256,128]{1,0:T(8,128)(2,1)S(1)}, bf16[256,128]{1,0:T(8,128)(2,1)S(1)}, u32[]{:S(2)}, u32[]{:S(2)}) collective-permute-start(bf16[256,128]{1,0:T(8,128)(2,1)S(1)} %get-tuple-element.69), channel_id=1, source_target_pairs={{0,2},{1,3},{2,0},{3,1},{4,6},{5,7},{6,4},{7,5},{8,10},{9,11},{10,... | collective-permute-start | bytes 196616 | tf_op jit(solution)/shard_map/ppermute | solution.py:385
  43.5 7.2 %collective-permute-start.13 = (bf16[256,128]{1,0:T(8,128)(2,1)S(1)}, bf16[256,128]{1,0:T(8,128)(2,1)S(1)}, u32[]{:S(2)}, u32[]{:S(2)}) collective-permute-start(bf16[256,128]{1,0:T(8,128)(2,1)S(1)} %get-tuple-element.71), channel_id=1, source_target_pairs={{0,1},{1,0},{2,3},{3,2},{4,5},{5,4},{6,7},{7,6},{8,9},{9,8},{10,11... | collective-permute-start | bytes 196616 | tf_op jit(solution)/shard_map/ppermute | solution.py:385
  45.2 6.1 %collective-permute-start.14 = (bf16[256,128]{1,0:T(8,128)(2,1)S(1)}, bf16[256,128]{1,0:T(8,128)(2,1)S(1)}, u32[]{:S(2)}, u32[]{:S(2)}) collective-permute-start(bf16[256,128]{1,0:T(8,128)(2,1)S(1)} %get-tuple-element.73), channel_id=1, source_target_pairs={{0,3},{1,2},{2,1},{3,0},{4,7},{5,6},{6,5},{7,4},{8,11},{9,10},{10,... | collective-permute-start | bytes 196616 | tf_op jit(solution)/shard_map/ppermute | solution.py:385

commit v4 on v3

--- a/solution.py
+++ b/solution.py
@@ -15,7 +15,7 @@
 NEG = -1e30
 LOWEST = -3e38
 HELD = KEEP * BLK
-CHUNK = 512
+CHUNK = 1536
 LONG = 2**33
 GROUP = 2 * HELD // CHUNK
 QUERY_SCALE = HD**-0.5 * math.log2(math.e)
@@ -24,7 +24,7 @@
 SMALL = pltpu.CompilerParams(vmem_limit_bytes=16 * 2**20)
 FREE = pl.CostEstimate(flops=0, bytes_accessed=0, transcendentals=0)
 LARGE = pltpu.CompilerParams(vmem_limit_bytes=60 * 2**20)
-PARAMS = pltpu.CompilerParams(vmem_limit_bytes=40 * 2**20)
+PARAMS = pltpu.CompilerParams(vmem_limit_bytes=32 * 2**20)
 ANY = pl.BlockSpec(memory_space=pl.ANY)
 HBM = pl.BlockSpec(memory_space=pltpu.HBM)
 VMEM = pl.BlockSpec(memory_space=pltpu.VMEM)
@@ -66,7 +66,8 @@
     steps = tokens.shape[1] // step
 
     def kernel(mask_any, tok_ref, wk_ref, wv_ref, *rest):
-        outs, (mask_ref, tok, wk, wv, keys, values, held, sems, out_sems) = rest[:pairs], rest[pairs:]
+        outs, rest = rest[: pairs + 1], rest[pairs + 1 :]
+        (mask_ref, tok, wk, wv, keys, values, held, sems, out_sems) = rest
         load_mask = pltpu.make_async_copy(mask_any, mask_ref, sems.at[0])
         load_mask.start()
         loads = []
@@ -106,19 +107,24 @@
         for p in range(pairs):
             for e in range(KEEP):
                 begin = pl.multiple_of(((code >> (BAND_BITS * e)) & (2**BAND_BITS - 1)) * BLK, BLK)
-                copy = pltpu.make_async_copy(
-                    held.at[p, :, pl.ds(begin, BLK), :], outs[p].at[:, pl.ds(e * BLK, BLK), :], out_sems.at[p, e]
-                )
-                copy.start()
-                stores.append(copy)
+                block, at = pl.ds(begin, BLK), pl.ds(e * BLK, BLK)
+                if p == 0:
+                    moves = [(held.at[0, h, block, :], outs[h].at[at, :]) for h in range(2)]
+                else:
+                    moves = [(held.at[p, :, block, :], outs[p + 1].at[:, at, :])]
+                for i, (source, to) in enumerate(moves):
+                    copy = pltpu.make_async_copy(source, to, out_sems.at[p, e, i])
+                    copy.start()
+                    stores.append(copy)
         for copy in stores:
             copy.wait()
 
     return pl.pallas_call(
         kernel,
-        out_shape=[jax.ShapeDtypeStruct((2, rows, LANES), jnp.bfloat16)] * pairs,
+        out_shape=[jax.ShapeDtypeStruct((rows, LANES), jnp.bfloat16)] * 2
+        + [jax.ShapeDtypeStruct((2, rows, LANES), jnp.bfloat16)] * (pairs - 1),
         in_specs=[ANY] * 4,
-        out_specs=[ANY] * pairs,
+        out_specs=[ANY] * (pairs + 1),
         scratch_shapes=[
             pltpu.VMEM(block_mask.shape, jnp.int32),
             pltpu.VMEM(tokens.shape, jnp.bfloat16),
@@ -128,7 +134,7 @@
             pltpu.VMEM((rows_in, w_key.shape[1]), jnp.float32),
             pltpu.VMEM((pairs, 2, rows_in, LANES), jnp.bfloat16),
             pltpu.SemaphoreType.DMA((1 + 3 * steps,)),
-            pltpu.SemaphoreType.DMA((pairs, KEEP)),
+            pltpu.SemaphoreType.DMA((pairs, KEEP, 2)),
         ],
         compiler_params=LARGE,
         cost_estimate=FREE,
@@ -139,17 +145,22 @@
 class Tables:
     def __init__(self, landing, key_tab, value_tab, sems, refs):
         self.landing, self.key_tab, self.value_tab = landing, key_tab, value_tab
-        self.copies = [
-            pltpu.make_async_copy(ref, landing.at[:, pl.ds(s * HELD, HELD), :], sems.at[s]) for s, ref in enumerate(refs)
-        ]
+        self.copies = []
+        for s, ref in enumerate(refs):
+            at = pl.ds(s // 2 * HELD, HELD) if len(ref.shape) == 2 else pl.ds(s * HELD, HELD)
+            to = landing.at[s % 2, at, :] if len(ref.shape) == 2 else landing.at[:, at, :]
+            self.copies.append(pltpu.make_async_copy(ref, to, sems.at[s]))
         for copy in self.copies:
             copy.start()
 
     def fill(self, bias_ref, first):
         low = low_lanes((BLK, LANES)).astype(jnp.float32).astype(jnp.bfloat16)
         high = (1.0 - low_lanes((BLK, LANES)).astype(jnp.float32)).astype(jnp.bfloat16)
-        for s, copy in enumerate(self.copies):
-            copy.wait()
+        sources = self.landing.shape[1] // HELD
+        split = len(self.copies) // sources
+        for s in range(sources):
+            for copy in self.copies[s * split : (s + 1) * split]:
+                copy.wait()
             for e in range(KEEP):
                 at = pl.ds((s * KEEP + e) * BLK, BLK)
                 row = (first + s) * 8 + e
@@ -186,9 +197,10 @@
         return carried
 
 
-def table_scratch(sources):
+def table_scratch(arrays):
+    sources = sum(array.ndim - 1 for array in arrays) // 2
     table = pltpu.VMEM((2, sources * HELD, LANES), jnp.bfloat16)
-    return [table, table, table, pltpu.SemaphoreType.DMA((sources,))]
+    return [table, table, table, pltpu.SemaphoreType.DMA((len(arrays),))]
 
 
 def begin_attention(block_mask, tokens, w_query, early, parts, source_bands):
@@ -199,10 +211,12 @@
     key_blocks = block_mask.shape[1]
     sources = len(source_bands(0))
 
-    def kernel(mask_ref, tok, w, *rest):
+    def kernel(mask_ref, tok, w_any, *rest):
         early_refs, rest = rest[: len(early)], rest[len(early) :]
         outs = rest[:pairs]
-        bias_ref, state_ref, held, own_rows, out_sems, *scratch = rest[pairs:]
+        bias_ref, state_ref, held, own_rows, w, w_sem, out_sems, *scratch = rest[pairs:]
+        load_w = pltpu.make_async_copy(w_any, w, w_sem)
+        load_w.start()
         tables = Tables(*scratch, early_refs)
         me, band = lax.axis_index("head"), lax.axis_index("band")
         own_rows[...] = jnp.zeros(own_rows.shape, jnp.float32)
@@ -219,6 +233,7 @@
             )
             queried = (lane8 >= HD) & (lane8 < HD + per_band)
             bias_ref[s * 8 : (s + 1) * 8, :] = jnp.where(queried & (allowed < 0.5), NEG, 0.0)
+        load_w.wait()
         lane = lax.broadcasted_iota(jnp.int32, (part, LANES), 1)
         row = lax.broadcasted_iota(jnp.int32, (part, LANES), 0)
         stores = []
@@ -249,14 +264,16 @@
         kernel,
         out_shape=[jax.ShapeDtypeStruct((2, rows, LANES), jnp.bfloat16)] * pairs
         + [jax.ShapeDtypeStruct((sources * 8, LANES), jnp.float32), jax.ShapeDtypeStruct((2, rows, LANES), jnp.float32)],
-        in_specs=[VMEM] * 3 + [HBM] * len(early),
+        in_specs=[VMEM] * 2 + [HBM] * (1 + len(early)),
         out_specs=[ANY] * pairs + [VMEM] * 2,
         scratch_shapes=[
             pltpu.VMEM((pairs, 2, rows, LANES), jnp.bfloat16),
             pltpu.VMEM((LANES, key_blocks), jnp.float32),
+            pltpu.VMEM(w_query.shape, jnp.bfloat16),
+            pltpu.SemaphoreType.DMA(()),
             pltpu.SemaphoreType.DMA((pairs,)),
         ]
-        + table_scratch(len(early)),
+        + table_scratch(early),
         compiler_params=PARAMS,
         cost_estimate=FREE,
         name="begin_attention",
@@ -299,7 +316,7 @@
         out_shape=[jax.ShapeDtypeStruct((part, LANES), jnp.bfloat16)] * count,
         in_specs=[VMEM, VMEM] + [VMEM] * len(states) + [HBM] * len(sources),
         out_specs=[VMEM] * count,
-        scratch_shapes=table_scratch(len(sources)),
+        scratch_shapes=table_scratch(sources),
         compiler_params=PARAMS,
         cost_estimate=pl.CostEstimate(flops=cost, bytes_accessed=0, transcendentals=0),
         name="attend",
@@ -392,9 +409,10 @@
         return found
 
     kv = project_kv(block_mask, tokens, w_key, w_value)
+    kv = [list(kv[:2])] + [[one] for one in kv[2:]]
     pairs = len(kv)
-    far = [[along_band(one, lambda i: (i + 2 * r) % bands) for r in hops] for one in kv]
-    near = [to_sibling(one) for one in kv]
+    far = [[[along_band(one, lambda i: (i + 2 * r) % bands) for one in arrays] for r in hops] for arrays in kv]
+    near = [[to_sibling(one) for one in arrays] for arrays in kv]
 
     def widen(held, came, k):
         held = jnp.concatenate([held, came]) if came is not None else held
@@ -409,7 +427,7 @@
     w_mine, kv = lax.optimization_barrier((w_mine, kv))
     bit = heads // 2
     w_mine, arriving = widen(w_mine[None], None, bit)
-    queries, bias, state = begin_attention(block_mask, tokens, w_query, [kv[0], near[0]], heads, source_bands)
+    queries, bias, state = begin_attention(block_mask, tokens, w_query, kv[0] + near[0], heads, source_bands)
     far[0], queries, arriving = lax.optimization_barrier((far[0], queries, arriving))
     while bit > 1:
         bit //= 2
@@ -428,12 +446,12 @@
     for p in range(pairs):
         if p > 0:
             far[p], pieces = lax.optimization_barrier((far[p], pieces))
-        sources = [] if p == 0 else [kv[p], near[p]]
-        for one in far[p]:
-            sources += [one, to_sibling(one)]
+        sources = [] if p == 0 else kv[p] + near[p]
+        for arrays in far[p]:
+            sources += arrays + [to_sibling(one) for one in arrays]
         held, first = (state, 2) if p == 0 else (None, 0)
         if p < last:
-            pieces = attend(queries[p], held, sources, bias, first, heads, 0, heads, LONG)
+            pieces = attend(queries[p], held, sources, bias, first, heads, 0, heads, 0)
             if p == 0:
                 pieces, arriving = lax.optimization_barrier((pieces, arriving))
                 w_mine = jnp.concatenate([w_mine, arriving])
@@ -441,8 +459,9 @@
             exchange(pieces, 0)
         else:
             pieces = attend(queries[p], held, sources, bias, first, heads, 1, heads - 1, 0)
-            pieces, attended, arriving, sources[-1] = lax.optimization_barrier((pieces, attended, arriving, sources[-1]))
+            pieces, attended, sources[-1] = lax.optimization_barrier((pieces, attended, sources[-1]))
             exchange(pieces, 1)
+            arriving, sources[-1] = lax.optimization_barrier((arriving, sources[-1]))
             exchange(attend(queries[p], held, sources, bias, first, heads, 0, 1, LONG), 0)
     w_mine = jnp.concatenate([w_mine] + arriving, axis=1)
     return project_out(attended, w_mine, to_sibling(w_mine), tiles)

time: 53.1 us -> 52.4 us (0.987)
  Pallas kernels: 28.3 us -> 26.4 us
  local copies, waits for them, and re-layouts: 1.02 us -> 1.87 us
    ppermute x7 -> x10, waiting for transfers between devices: 0.59 us -> 2.63 us  [along_band(): return lax.ppermute(array, 'band', [(i, goes_to(i)) for i in range(bands)])]
    pallas_call x3, Pallas kernels: 17.1 us -> 15.2 us  [attend(): pl.pallas_call(kernel, out_shape=[jax.ShapeDtypeStruct((part, LANES), jnp...]
    ppermute x8, waiting for transfers between devices: 2.13 us -> 0.33 us  [along_head(): return lax.ppermute(array, 'head', [(i, i ^ k) for i in range(heads)])]
    unnamed x12 -> x14, local copies, waits for them, and re-layouts: 1.01 us -> 1.87 us
    ppermute x7 -> x10, starting transfers between devices: 5.43 us -> 5.6 us  [along_band(): return lax.ppermute(array, 'band', [(i, goes_to(i)) for i in range(bands)])]
  transfers between devices with their start and end apart: 16 -> 19, of which waited for: 3 -> 2; matrix products, arithmetic and copies ran while one was open for 0% -> 0% of each run, Pallas kernels for 43% -> 40%
where the time goes in v4:
time: 52.4 us; the launch traced here: 52.2 us
  Pallas kernels  26.4 us (50%)
  starting transfers between devices  20.6 us (39%)
  waiting for transfers between devices  2.97 us (6%)
  local copies, waits for them, and re-layouts  1.87 us (4%)
    pallas_call x3, Pallas kernels, attend(): pl.pallas_call(kernel, out_shape=[jax.ShapeDtypeStruct((part, LANES), jnp...  15.2 us
    ppermute x8, starting transfers between devices, along_head(): return lax.ppermute(array, 'head', [(i, i ^ k) for i in range(heads)])  13.4 us
    pallas_call x1, Pallas kernels, begin_attention(): pl.pallas_call(kernel, out_shape=[jax.ShapeDtypeStruct((2, rows, LANES),...  5.66 us
    ppermute x10, starting transfers between devices, along_band(): return lax.ppermute(array, 'band', [(i, goes_to(i)) for i in range(bands)])  5.6 us
    pallas_call x1, Pallas kernels, project_kv(): pl.pallas_call(kernel, out_shape=[jax.ShapeDtypeStruct((rows, LANES), jnp...  4 us
    ppermute x10, waiting for transfers between devices, along_band(): return lax.ppermute(array, 'band', [(i, goes_to(i)) for i in range(bands)])  2.63 us
    unnamed x14, local copies, waits for them, and re-layouts  1.87 us
    pallas_call x1, Pallas kernels, project_out(): pl.pallas_call(kernel, out_shape=jax.ShapeDtypeStruct((rows, width), jnp....  1.6 us
  transfers between devices with their start and end apart: 19, of which 2 were waited for; matrix products, arithmetic and copies ran while one was open for 0% of the time, Pallas kernels for 40%

profile of v4, /device:TPU:0, one launch (start us, length us, event | category | flops | bytes accessed | tf_op | source)
XLA Modules:
  0.0 52.2 jit_solution(499319424496136593)
XLA Ops:
  0.0 4.0 %project_kv.1 = (bf16[768,128]{1,0:T(8,128)(2,1)}, bf16[768,128]{1,0:T(8,128)(2,1)}, bf16[2,768,128]{2,1,0:T(8,128)(2,1)}) custom-call(s32[32,32]{1,0:T(8,128)} %mask_ref.1, bf16[1024,1024]{1,0:T(8,128)(2,1)} %tok.1, bf16[1024,256]{1,0:T(8,128)(2,1)} %wk_ref.1, bf16[1024,256]{1,0:T(8,128)(2,1)} %wv_ref.1), custom_call_target="tpu_custom_call" | custom-call | tf_op jit(solution)/shard_map/project_kv/pallas_call | solution.py:122
  4.0 3.0 %collective-permute-start = (bf16[768,128]{1,0:T(8,128)(2,1)}, bf16[768,128]{1,0:T(8,128)(2,1)S(1)}, u32[]{:S(2)}, u32[]{:S(2)}) collective-permute-start(bf16[768,128]{1,0:T(8,128)(2,1)} %get-tuple-element.47.rest_0_), channel_id=1, source_target_pairs={{0,8},{4,12},{8,0},{12,4},{1,9},{5,13},{9,1},{13,5},{2,10},{6,14},... | collective-permute-start | bytes 589832 | tf_op jit(solution)/shard_map/ppermute | solution.py:396
  7.0 0.0 collective-permute-start.2
  7.0 0.2 collective-permute-start.1
  7.2 0.4 collective-permute-start.3
  7.6 2.9 %collective-permute-start.4 = (bf16[1,64,1024]{2,1,0:T(8,128)(2,1)S(1)}, bf16[1,64,1024]{2,1,0:T(8,128)(2,1)S(1)}, u32[]{:S(2)}, u32[]{:S(2)}) collective-permute-start(bf16[1,64,1024]{2,1,0:T(8,128)(2,1)S(1)} %bitcast.1), channel_id=1, source_target_pairs={{0,2},{1,3},{2,0},{3,1},{4,6},{5,7},{6,4},{7,5},{8,10},{9,11},{10,... | collective-permute-start | bytes 393224 | tf_op jit(solution)/shard_map/ppermute | solution.py:402
  10.5 0.0 collective-permute-done.2.rest_2_
  10.5 0.0 collective-permute-done.3.rest_3_
  10.5 0.9 %copy-done.4 = bf16[768,128]{1,0:T(8,128)(2,1)S(1)} copy-done((bf16[768,128]{1,0:T(8,128)(2,1)S(1)}, bf16[768,128]{1,0:T(8,128)(2,1)}, u32[]{:S(2)}) %copy-start.4) | copy-done | bytes 196632
  11.4 0.9 %copy-done.5 = bf16[768,128]{1,0:T(8,128)(2,1)S(1)} copy-done((bf16[768,128]{1,0:T(8,128)(2,1)S(1)}, bf16[768,128]{1,0:T(8,128)(2,1)}, u32[]{:S(2)}) %copy-start.5) | copy-done | bytes 196632
  12.4 5.7 %begin_attention.1 = (bf16[2,1024,128]{2,1,0:T(8,128)(2,1)S(1)}, bf16[2,1024,128]{2,1,0:T(8,128)(2,1)S(1)}, f32[32,128]{1,0:T(8,128)S(1)}, f32[2,1024,128]{2,1,0:T(8,128)S(1)}) custom-call(s32[32,32]{1,0:T(8,128)S(1)} %copy-done.6, bf16[1024,1024]{1,0:T(8,128)(2,1)S(1)} %copy-done.1, bf16[1024,256]{1,0:T(8,128)(2,1)S(1)} %copy-done.2, ...), custom_call_target="tpu_custom_call" | custom-call | tf_op jit(solution)/shard_map/begin_attention/pallas_call | solution.py:263
  18.0 0.0 collective-permute-done.4
  18.0 0.0 collective-permute-done.rest_1_
  18.1 0.0 collective-permute-done.1.rest_2_
  18.1 1.6 %collective-permute-start.9 = (bf16[2,64,1024]{2,1,0:T(8,128)(2,1)S(1)}, bf16[2,64,1024]{2,1,0:T(8,128)(2,1)S(1)}, u32[]{:S(2)}, u32[]{:S(2)}) collective-permute-start(bf16[2,64,1024]{2,1,0:T(8,128)(2,1)S(1)} %pad_maximum_fusion.2), channel_id=1, source_target_pairs={{0,1},{1,0},{2,3},{3,2},{4,5},{5,4},{6,7},{7,6},{8,9},{9,8},{10,11... | collective-permute-start | bytes 786440 | tf_op jit(solution)/shard_map/ppermute | solution.py:402
  19.7 0.0 collective-permute-start.7
  19.7 0.5 collective-permute-start.8
  20.3 1.5 %collective-permute-start.6 = (bf16[2,768,128]{2,1,0:T(8,128)(2,1)S(1)}, bf16[2,768,128]{2,1,0:T(8,128)(2,1)S(1)}, u32[]{:S(2)}, u32[]{:S(2)}) collective-permute-start(bf16[2,768,128]{2,1,0:T(8,128)(2,1)S(1)} %copy-done.3), channel_id=1, source_target_pairs={{0,8},{4,12},{8,0},{12,4},{1,9},{5,13},{9,1},{13,5},{2,10},{6,14},... | collective-permute-start | bytes 1179656 | tf_op jit(solution)/shard_map/ppermute | solution.py:396
  21.7 0.0 collective-permute-done.7.rest_3_
  21.7 0.0 collective-permute-done.8.rest_4_
  21.8 5.3 %attend.3 = (bf16[256,128]{1,0:T(8,128)(2,1)S(1)}, bf16[256,128]{1,0:T(8,128)(2,1)S(1)}, bf16[256,128]{1,0:T(8,128)(2,1)S(1)}, bf16[256,128]{1,0:T(8,128)(2,1)S(1)}) custom-call(bf16[2,1024,128]{2,1,0:T(8,128)(2,1)S(1)} %get-tuple-element.55.q_ref, f32[32,128]{1,0:T(8,128)S(1)} %get-tuple-element.53.bias_ref, f32[2,1024,128]{2,1,0:T(8,128)S(1)} %get-tuple-element.56.rest_0_, ...), custom_call_target="tpu_custom_call" | custom-call | tf_op jit(solution)/shard_map/attend/pallas_call | solution.py:314
  27.0 0.0 collective-permute-done.9
  27.0 0.1 pad_maximum_fusion.1
  27.1 1.6 %collective-permute-start.14 = (bf16[4,64,1024]{2,1,0:T(8,128)(2,1)S(1)}, bf16[4,64,1024]{2,1,0:T(8,128)(2,1)S(1)}, u32[]{:S(2)}, u32[]{:S(2)}) collective-permute-start(bf16[4,64,1024]{2,1,0:T(8,128)(2,1)S(1)} %pad_maximum_fusion.1), channel_id=1, source_target_pairs={{0,16},{16,0},{1,17},{17,1},{2,18},{18,2},{3,19},{19,3},{4,20},{20... | collective-permute-start | bytes 1572872 | tf_op jit(solution)/shard_map/ppermute | solution.py:422
  28.7 0.0 collective-permute-start.5
  28.7 2.6 %collective-permute-done.6.rest_2_ = bf16[2,768,128]{2,1,0:T(8,128)(2,1)S(1)} collective-permute-done((bf16[2,768,128]{2,1,0:T(8,128)(2,1)S(1)}, bf16[2,768,128]{2,1,0:T(8,128)(2,1)S(1)}, u32[]{:S(2)}, u32[]{:S(2)}) %collective-permute-start.6) | collective-permute-done | bytes 393248 | tf_op jit(solution)/shard_map/ppermute | solution.py:396
  31.3 0.0 collective-permute-start.10
  31.3 0.4 collective-permute-start.11
  31.7 1.4 %collective-permute-start.12 = (bf16[256,128]{1,0:T(8,128)(2,1)S(1)}, bf16[256,128]{1,0:T(8,128)(2,1)S(1)}, u32[]{:S(2)}, u32[]{:S(2)}) collective-permute-start(bf16[256,128]{1,0:T(8,128)(2,1)S(1)} %get-tuple-element.66), channel_id=1, source_target_pairs={{0,2},{1,3},{2,0},{3,1},{4,6},{5,7},{6,4},{7,5},{8,10},{9,11},{10,... | collective-permute-start | bytes 196616 | tf_op jit(solution)/shard_map/ppermute | solution.py:402
  33.2 0.0 collective-permute-done.5.rest_1_
  33.2 2.5 %collective-permute-start.13 = (bf16[256,128]{1,0:T(8,128)(2,1)S(1)}, bf16[256,128]{1,0:T(8,128)(2,1)S(1)}, u32[]{:S(2)}, u32[]{:S(2)}) collective-permute-start(bf16[256,128]{1,0:T(8,128)(2,1)S(1)} %get-tuple-element.67), channel_id=1, source_target_pairs={{0,3},{1,2},{2,1},{3,0},{4,7},{5,6},{6,5},{7,4},{8,11},{9,10},{10,... | collective-permute-start | bytes 196616 | tf_op jit(solution)/shard_map/ppermute | solution.py:402
  35.7 0.0 collective-permute-done.10.rest_3_
  35.7 6.5 %attend.4 = (bf16[256,128]{1,0:T(8,128)(2,1)S(1)}, bf16[256,128]{1,0:T(8,128)(2,1)S(1)}, bf16[256,128]{1,0:T(8,128)(2,1)S(1)}) custom-call(bf16[2,1024,128]{2,1,0:T(8,128)(2,1)S(1)} %get-tuple-element.52.q_ref, f32[32,128]{1,0:T(8,128)S(1)} %get-tuple-element.53.bias_ref, bf16[2,768,128]{2,1,0:T(8,128)(2,1)S(1)} %copy-done.3, ...), custom_call_target="tpu_custom_call" | custom-call | tf_op jit(solution)/shard_map/attend/pallas_call | solution.py:314
  42.2 0.0 collective-permute-done.11.rest_4_
  42.2 0.0 collective-permute-done.12.rest_2_
  42.2 0.0 collective-permute-done.13.rest_6_
  42.2 0.0 collective-permute-done.14
  42.3 0.1 pad_maximum_fusion.rest_8_
  42.3 0.1 collective-permute-start.18
  42.4 0.9 %collective-permute-start.15 = (bf16[256,128]{1,0:T(8,128)(2,1)S(1)}, bf16[256,128]{1,0:T(8,128)(2,1)S(1)}, u32[]{:S(2)}, u32[]{:S(2)}) collective-permute-start(bf16[256,128]{1,0:T(8,128)(2,1)S(1)} %get-tuple-element.77), channel_id=1, source_target_pairs={{0,2},{1,3},{2,0},{3,1},{4,6},{5,7},{6,4},{7,5},{8,10},{9,11},{10,... | collective-permute-start | bytes 196616 | tf_op jit(solution)/shard_map/ppermute | solution.py:402
  43.3 1.1 %collective-permute-start.16 = (bf16[256,128]{1,0:T(8,128)(2,1)S(1)}, bf16[256,128]{1,0:T(8,128)(2,1)S(1)}, u32[]{:S(2)}, u32[]{:S(2)}) collective-permute-start(bf16[256,128]{1,0:T(8,128)(2,1)S(1)} %get-tuple-element.79), channel_id=1, source_target_pairs={{0,1},{1,0},{2,3},{3,2},{4,5},{5,4},{6,7},{7,6},{8,9},{9,8},{10,11... | collective-permute-start | bytes 196616 | tf_op jit(solution)/shard_map/ppermute | solution.py:402
  44.4 2.5 %collective-permute-start.17 = (bf16[256,128]{1,0:T(8,128)(2,1)S(1)}, bf16[256,128]{1,0:T(8,128)(2,1)S(1)}, u32[]{:S(2)}, u32[]{:S(2)}) collective-permute-start(bf16[256,128]{1,0:T(8,128)(2,1)S(1)} %get-tuple-element.81), channel_id=1, source_target_pairs={{0,3},{1,2},{2,1},{3,0},{4,7},{5,6},{6,5},{7,4},{8,11},{9,10},{10,... | collective-permute-start | bytes 196616 | tf_op jit(solution)/shard_map/ppermute | solution.py:402
  46.9 3.4 %attend.5.rest_1_ = bf16[256,128]{1,0:T(8,128)(2,1)S(1)} custom-call(bf16[2,1024,128]{2,1,0:T(8,128)(2,1)S(1)} %get-tuple-element.52.q_ref, f32[32,128]{1,0:T(8,128)S(1)} %get-tuple-element.53.bias_ref, bf16[2,768,128]{2,1,0:T(8,128)(2,1)S(1)} %copy-done.3, bf16[2,768,128]{2,1,0:T(8,128)(2,1)S(1)} %collective-permute-done.5.rest_1_, ...), custom_call_target="tpu_custom_call" | custom-call | flops 8589934592 | tf_op jit(solution)/shard_map/attend/pallas_call | solution.py:314
  50.3 0.0 collective-permute-done.15.rest_3_
  50.3 0.0 collective-permute-done.16.rest_5_
  50.3 0.3 collective-permute-done.17.rest_7_
  50.6 0.0 collective-permute-done.18.rest_9_
  50.6 1.6 %project_out.1 = bf16[256,1024]{1,0:T(8,128)(2,1)} custom-call(bf16[256,128]{1,0:T(8,128)(2,1)S(1)} %get-tuple-element.72.rest_0_, bf16[256,128]{1,0:T(8,128)(2,1)S(1)} %attend.5.rest_1_, bf16[256,128]{1,0:T(8,128)(2,1)S(1)} %collective-permute-done.12.rest_2_, bf16[256,128]{1,0:T(8,128)(2,1)S(1)} %collective-permute-done.15.rest_3_, ...), custom_call_target="tpu_custom_call" | custom-call | tf_op jit(solution)/shard_map/project_out/pallas_call | solution.py:379
  (14 shorter events, 0.1 us)
Async XLA Ops:
  0.0 7.5 %copy-start = (bf16[256,1024]{1,0:T(8,128)(2,1)S(1)}, bf16[256,1024]{1,0:T(8,128)(2,1)}, u32[]{:S(2)}) copy-start(bf16[256,1024]{1,0:T(8,128)(2,1)} %param.10) | copy-start | bytes 1572868
  0.0 10.5 %copy-start.6 = (s32[32,32]{1,0:T(8,128)S(1)}, s32[32,32]{1,0:T(8,128)}, u32[]{:S(2)}) copy-start(s32[32,32]{1,0:T(8,128)} %mask_ref.1) | copy-start | bytes 12292
  0.0 10.5 %copy-start.1 = (bf16[1024,1024]{1,0:T(8,128)(2,1)S(1)}, bf16[1024,1024]{1,0:T(8,128)(2,1)}, u32[]{:S(2)}) copy-start(bf16[1024,1024]{1,0:T(8,128)(2,1)} %tok.1) | copy-start | bytes 6291460
  0.0 10.5 %copy-start.2 = (bf16[1024,256]{1,0:T(8,128)(2,1)S(1)}, bf16[1024,256]{1,0:T(8,128)(2,1)}, u32[]{:S(2)}) copy-start(bf16[1024,256]{1,0:T(8,128)(2,1)} %w_any.1) | copy-start | bytes 1572868
  4.0 14.0 %collective-permute-start = (bf16[768,128]{1,0:T(8,128)(2,1)}, bf16[768,128]{1,0:T(8,128)(2,1)S(1)}, u32[]{:S(2)}, u32[]{:S(2)}) collective-permute-start(bf16[768,128]{1,0:T(8,128)(2,1)} %get-tuple-element.47.rest_0_), channel_id=1, source_target_pairs={{0,8},{4,12},{8,0},{12,4},{1,9},{5,13},{9,1},{13,5},{2,10},{6,14},... | collective-permute-start | bytes 589832 | tf_op jit(solution)/shard_map/ppermute | solution.py:396
  7.0 3.4 %collective-permute-start.2 = (bf16[768,128]{1,0:T(8,128)(2,1)}, bf16[768,128]{1,0:T(8,128)(2,1)}, u32[]{:S(2)}, u32[]{:S(2)}) collective-permute-start(bf16[768,128]{1,0:T(8,128)(2,1)} %get-tuple-element.47.rest_0_), channel_id=1, source_target_pairs={{0,4},{4,0},{8,12},{12,8},{1,5},{5,1},{9,13},{13,9},{2,6},{6,2},{1... | collective-permute-start | bytes 589832 | tf_op jit(solution)/shard_map/ppermute | solution.py:396
  7.0 11.0 %collective-permute-start.1 = (bf16[768,128]{1,0:T(8,128)(2,1)}, bf16[768,128]{1,0:T(8,128)(2,1)S(1)}, u32[]{:S(2)}, u32[]{:S(2)}) collective-permute-start(bf16[768,128]{1,0:T(8,128)(2,1)} %get-tuple-element.48.rest_1_), channel_id=1, source_target_pairs={{0,8},{4,12},{8,0},{12,4},{1,9},{5,13},{9,1},{13,5},{2,10},{6,14},... | collective-permute-start | bytes 589832 | tf_op jit(solution)/shard_map/ppermute | solution.py:396
  7.2 3.3 %collective-permute-start.3 = (bf16[768,128]{1,0:T(8,128)(2,1)}, bf16[768,128]{1,0:T(8,128)(2,1)}, u32[]{:S(2)}, u32[]{:S(2)}) collective-permute-start(bf16[768,128]{1,0:T(8,128)(2,1)} %get-tuple-element.48.rest_1_), channel_id=1, source_target_pairs={{0,4},{4,0},{8,12},{12,8},{1,5},{5,1},{9,13},{13,9},{2,6},{6,2},{1... | collective-permute-start | bytes 589832 | tf_op jit(solution)/shard_map/ppermute | solution.py:396
  7.5 12.7 %copy-start.3 = (bf16[2,768,128]{2,1,0:T(8,128)(2,1)S(1)}, bf16[2,768,128]{2,1,0:T(8,128)(2,1)}, u32[]{:S(2)}) copy-start(bf16[2,768,128]{2,1,0:T(8,128)(2,1)} %get-tuple-element.54.rest_0_) | copy-start | bytes 1179652
  7.6 10.5 %collective-permute-start.4 = (bf16[1,64,1024]{2,1,0:T(8,128)(2,1)S(1)}, bf16[1,64,1024]{2,1,0:T(8,128)(2,1)S(1)}, u32[]{:S(2)}, u32[]{:S(2)}) collective-permute-start(bf16[1,64,1024]{2,1,0:T(8,128)(2,1)S(1)} %bitcast.1), channel_id=1, source_target_pairs={{0,2},{1,3},{2,0},{3,1},{4,6},{5,7},{6,4},{7,5},{8,10},{9,11},{10,... | collective-permute-start | bytes 393224 | tf_op jit(solution)/shard_map/ppermute | solution.py:402
  10.5 0.9 %copy-start.4 = (bf16[768,128]{1,0:T(8,128)(2,1)S(1)}, bf16[768,128]{1,0:T(8,128)(2,1)}, u32[]{:S(2)}) copy-start(bf16[768,128]{1,0:T(8,128)(2,1)} %get-tuple-element.48.rest_1_) | copy-start | bytes 589828
  11.4 0.9 %copy-start.5 = (bf16[768,128]{1,0:T(8,128)(2,1)S(1)}, bf16[768,128]{1,0:T(8,128)(2,1)}, u32[]{:S(2)}) copy-start(bf16[768,128]{1,0:T(8,128)(2,1)} %get-tuple-element.47.rest_0_) | copy-start | bytes 589828
  18.1 8.9 %collective-permute-start.9 = (bf16[2,64,1024]{2,1,0:T(8,128)(2,1)S(1)}, bf16[2,64,1024]{2,1,0:T(8,128)(2,1)S(1)}, u32[]{:S(2)}, u32[]{:S(2)}) collective-permute-start(bf16[2,64,1024]{2,1,0:T(8,128)(2,1)S(1)} %pad_maximum_fusion.2), channel_id=1, source_target_pairs={{0,1},{1,0},{2,3},{3,2},{4,5},{5,4},{6,7},{7,6},{8,9},{9,8},{10,11... | collective-permute-start | bytes 786440 | tf_op jit(solution)/shard_map/ppermute | solution.py:402
  19.7 2.0 %collective-permute-start.7 = (bf16[768,128]{1,0:T(8,128)(2,1)S(1)}, bf16[768,128]{1,0:T(8,128)(2,1)S(1)}, u32[]{:S(2)}, u32[]{:S(2)}) collective-permute-start(bf16[768,128]{1,0:T(8,128)(2,1)S(1)} %collective-permute-done.rest_1_), channel_id=1, source_target_pairs={{0,4},{4,0},{8,12},{12,8},{1,5},{5,1},{9,13},{13,9},{2,6},{6,2},{1... | collective-permute-start | bytes 589832 | tf_op jit(solution)/shard_map/ppermute | solution.py:396
  19.7 2.0 %collective-permute-start.8 = (bf16[768,128]{1,0:T(8,128)(2,1)S(1)}, bf16[768,128]{1,0:T(8,128)(2,1)S(1)}, u32[]{:S(2)}, u32[]{:S(2)}) collective-permute-start(bf16[768,128]{1,0:T(8,128)(2,1)S(1)} %collective-permute-done.1.rest_2_), channel_id=1, source_target_pairs={{0,4},{4,0},{8,12},{12,8},{1,5},{5,1},{9,13},{13,9},{2,6},{6,2},{1... | collective-permute-start | bytes 589832 | tf_op jit(solution)/shard_map/ppermute | solution.py:396
  20.3 11.0 %collective-permute-start.6 = (bf16[2,768,128]{2,1,0:T(8,128)(2,1)S(1)}, bf16[2,768,128]{2,1,0:T(8,128)(2,1)S(1)}, u32[]{:S(2)}, u32[]{:S(2)}) collective-permute-start(bf16[2,768,128]{2,1,0:T(8,128)(2,1)S(1)} %copy-done.3), channel_id=1, source_target_pairs={{0,8},{4,12},{8,0},{12,4},{1,9},{5,13},{9,1},{13,5},{2,10},{6,14},... | collective-permute-start | bytes 1179656 | tf_op jit(solution)/shard_map/ppermute | solution.py:396
  27.1 15.2 %collective-permute-start.14 = (bf16[4,64,1024]{2,1,0:T(8,128)(2,1)S(1)}, bf16[4,64,1024]{2,1,0:T(8,128)(2,1)S(1)}, u32[]{:S(2)}, u32[]{:S(2)}) collective-permute-start(bf16[4,64,1024]{2,1,0:T(8,128)(2,1)S(1)} %pad_maximum_fusion.1), channel_id=1, source_target_pairs={{0,16},{16,0},{1,17},{17,1},{2,18},{18,2},{3,19},{19,3},{4,20},{20... | collective-permute-start | bytes 1572872 | tf_op jit(solution)/shard_map/ppermute | solution.py:422
  28.7 4.5 %collective-permute-start.5 = (bf16[2,768,128]{2,1,0:T(8,128)(2,1)S(1)}, bf16[2,768,128]{2,1,0:T(8,128)(2,1)S(1)}, u32[]{:S(2)}, u32[]{:S(2)}) collective-permute-start(bf16[2,768,128]{2,1,0:T(8,128)(2,1)S(1)} %copy-done.3), channel_id=1, source_target_pairs={{0,4},{4,0},{8,12},{12,8},{1,5},{5,1},{9,13},{13,9},{2,6},{6,2},{1... | collective-permute-start | bytes 1179656 | tf_op jit(solution)/shard_map/ppermute | solution.py:396
  31.3 4.4 %collective-permute-start.10 = (bf16[2,768,128]{2,1,0:T(8,128)(2,1)S(1)}, bf16[2,768,128]{2,1,0:T(8,128)(2,1)S(1)}, u32[]{:S(2)}, u32[]{:S(2)}) collective-permute-start(bf16[2,768,128]{2,1,0:T(8,128)(2,1)S(1)} %collective-permute-done.6.rest_2_), channel_id=1, source_target_pairs={{0,4},{4,0},{8,12},{12,8},{1,5},{5,1},{9,13},{13,9},{2,6},{6,2},{1... | collective-permute-start | bytes 1179656 | tf_op jit(solution)/shard_map/ppermute | solution.py:396
  31.3 10.9 %collective-permute-start.11 = (bf16[256,128]{1,0:T(8,128)(2,1)S(1)}, bf16[256,128]{1,0:T(8,128)(2,1)S(1)}, u32[]{:S(2)}, u32[]{:S(2)}) collective-permute-start(bf16[256,128]{1,0:T(8,128)(2,1)S(1)} %get-tuple-element.65), channel_id=1, source_target_pairs={{0,1},{1,0},{2,3},{3,2},{4,5},{5,4},{6,7},{7,6},{8,9},{9,8},{10,11... | collective-permute-start | bytes 196616 | tf_op jit(solution)/shard_map/ppermute | solution.py:402
  31.7 10.5 %collective-permute-start.12 = (bf16[256,128]{1,0:T(8,128)(2,1)S(1)}, bf16[256,128]{1,0:T(8,128)(2,1)S(1)}, u32[]{:S(2)}, u32[]{:S(2)}) collective-permute-start(bf16[256,128]{1,0:T(8,128)(2,1)S(1)} %get-tuple-element.66), channel_id=1, source_target_pairs={{0,2},{1,3},{2,0},{3,1},{4,6},{5,7},{6,4},{7,5},{8,10},{9,11},{10,... | collective-permute-start | bytes 196616 | tf_op jit(solution)/shard_map/ppermute | solution.py:402
  33.2 9.1 %collective-permute-start.13 = (bf16[256,128]{1,0:T(8,128)(2,1)S(1)}, bf16[256,128]{1,0:T(8,128)(2,1)S(1)}, u32[]{:S(2)}, u32[]{:S(2)}) collective-permute-start(bf16[256,128]{1,0:T(8,128)(2,1)S(1)} %get-tuple-element.67), channel_id=1, source_target_pairs={{0,3},{1,2},{2,1},{3,0},{4,7},{5,6},{6,5},{7,4},{8,11},{9,10},{10,... | collective-permute-start | bytes 196616 | tf_op jit(solution)/shard_map/ppermute | solution.py:402
  42.3 8.3 %collective-permute-start.18 = (bf16[4,128,1024]{2,1,0:T(8,128)(2,1)S(1)}, bf16[4,128,1024]{2,1,0:T(8,128)(2,1)S(1)}, u32[]{:S(2)}, u32[]{:S(2)}) collective-permute-start(bf16[4,128,1024]{2,1,0:T(8,128)(2,1)S(1)} %pad_maximum_fusion.rest_8_), channel_id=1, source_target_pairs={{0,4},{4,0},{8,12},{12,8},{1,5},{5,1},{9,13},{13,9},{2,6},{6,2},{1... | collective-permute-start | bytes 3145736 | tf_op jit(solution)/shard_map/ppermute | solution.py:396
  42.4 7.9 %collective-permute-start.15 = (bf16[256,128]{1,0:T(8,128)(2,1)S(1)}, bf16[256,128]{1,0:T(8,128)(2,1)S(1)}, u32[]{:S(2)}, u32[]{:S(2)}) collective-permute-start(bf16[256,128]{1,0:T(8,128)(2,1)S(1)} %get-tuple-element.77), channel_id=1, source_target_pairs={{0,2},{1,3},{2,0},{3,1},{4,6},{5,7},{6,4},{7,5},{8,10},{9,11},{10,... | collective-permute-start | bytes 196616 | tf_op jit(solution)/shard_map/ppermute | solution.py:402
  43.3 7.0 %collective-permute-start.16 = (bf16[256,128]{1,0:T(8,128)(2,1)S(1)}, bf16[256,128]{1,0:T(8,128)(2,1)S(1)}, u32[]{:S(2)}, u32[]{:S(2)}) collective-permute-start(bf16[256,128]{1,0:T(8,128)(2,1)S(1)} %get-tuple-element.79), channel_id=1, source_target_pairs={{0,1},{1,0},{2,3},{3,2},{4,5},{5,4},{6,7},{7,6},{8,9},{9,8},{10,11... | collective-permute-start | bytes 196616 | tf_op jit(solution)/shard_map/ppermute | solution.py:402
  44.4 6.2 %collective-permute-start.17 = (bf16[256,128]{1,0:T(8,128)(2,1)S(1)}, bf16[256,128]{1,0:T(8,128)(2,1)S(1)}, u32[]{:S(2)}, u32[]{:S(2)}) collective-permute-start(bf16[256,128]{1,0:T(8,128)(2,1)S(1)} %get-tuple-element.81), channel_id=1, source_target_pairs={{0,3},{1,2},{2,1},{3,0},{4,7},{5,6},{6,5},{7,4},{8,11},{9,10},{10,... | collective-permute-start | bytes 196616 | tf_op jit(solution)/shard_map/ppermute | solution.py:402

commit v5 on v4

--- a/solution.py
+++ b/solution.py
@@ -66,7 +66,7 @@
     steps = tokens.shape[1] // step
 
     def kernel(mask_any, tok_ref, wk_ref, wv_ref, *rest):
-        outs, rest = rest[: pairs + 1], rest[pairs + 1 :]
+        outs, own_ref, rest = rest[: pairs + 1], rest[pairs + 1], rest[pairs + 2 :]
         (mask_ref, tok, wk, wv, keys, values, held, sems, out_sems) = rest
         load_mask = pltpu.make_async_copy(mask_any, mask_ref, sems.at[0])
         load_mask.start()
@@ -110,6 +110,7 @@
                 block, at = pl.ds(begin, BLK), pl.ds(e * BLK, BLK)
                 if p == 0:
                     moves = [(held.at[0, h, block, :], outs[h].at[at, :]) for h in range(2)]
+                    moves.append((held.at[0, :, block, :], own_ref.at[:, at, :]))
                 else:
                     moves = [(held.at[p, :, block, :], outs[p + 1].at[:, at, :])]
                 for i, (source, to) in enumerate(moves):
@@ -122,9 +123,9 @@
     return pl.pallas_call(
         kernel,
         out_shape=[jax.ShapeDtypeStruct((rows, LANES), jnp.bfloat16)] * 2
-        + [jax.ShapeDtypeStruct((2, rows, LANES), jnp.bfloat16)] * (pairs - 1),
+        + [jax.ShapeDtypeStruct((2, rows, LANES), jnp.bfloat16)] * pairs,
         in_specs=[ANY] * 4,
-        out_specs=[ANY] * (pairs + 1),
+        out_specs=[ANY] * (pairs + 2),
         scratch_shapes=[
             pltpu.VMEM(block_mask.shape, jnp.int32),
             pltpu.VMEM(tokens.shape, jnp.bfloat16),
@@ -134,7 +135,7 @@
             pltpu.VMEM((rows_in, w_key.shape[1]), jnp.float32),
             pltpu.VMEM((pairs, 2, rows_in, LANES), jnp.bfloat16),
             pltpu.SemaphoreType.DMA((1 + 3 * steps,)),
-            pltpu.SemaphoreType.DMA((pairs, KEEP, 2)),
+            pltpu.SemaphoreType.DMA((pairs, KEEP, 3)),
         ],
         compiler_params=LARGE,
         cost_estimate=FREE,
@@ -145,22 +146,23 @@
 class Tables:
     def __init__(self, landing, key_tab, value_tab, sems, refs):
         self.landing, self.key_tab, self.value_tab = landing, key_tab, value_tab
-        self.copies = []
+        self.copies, taken = [], 0
         for s, ref in enumerate(refs):
-            at = pl.ds(s // 2 * HELD, HELD) if len(ref.shape) == 2 else pl.ds(s * HELD, HELD)
-            to = landing.at[s % 2, at, :] if len(ref.shape) == 2 else landing.at[:, at, :]
-            self.copies.append(pltpu.make_async_copy(ref, to, sems.at[s]))
-        for copy in self.copies:
+            at = pl.ds(taken // 2 * HELD, HELD)
+            to = landing.at[taken % 2, at, :] if len(ref.shape) == 2 else landing.at[:, at, :]
+            taken += len(ref.shape) - 1
+            self.copies.append((taken, pltpu.make_async_copy(ref, to, sems.at[s])))
+        for _, copy in self.copies:
             copy.start()
 
     def fill(self, bias_ref, first):
         low = low_lanes((BLK, LANES)).astype(jnp.float32).astype(jnp.bfloat16)
         high = (1.0 - low_lanes((BLK, LANES)).astype(jnp.float32)).astype(jnp.bfloat16)
         sources = self.landing.shape[1] // HELD
-        split = len(self.copies) // sources
         for s in range(sources):
-            for copy in self.copies[s * split : (s + 1) * split]:
-                copy.wait()
+            for taken, copy in self.copies:
+                if 2 * s < taken <= 2 * s + 2:
+                    copy.wait()
             for e in range(KEEP):
                 at = pl.ds((s * KEEP + e) * BLK, BLK)
                 row = (first + s) * 8 + e
@@ -323,9 +325,9 @@
     )(queries, bias, *states, *sources)
 
 
-def project_out(attended, w_mine, w_other, tiles):
-    heads, depth, width = w_mine.shape
-    pairs = len(attended[0])
+def project_out(attended, w_out, w_mine, w_other, tiles):
+    depth, width = w_mine.shape[1:]
+    heads, pairs = len(attended), len(attended[0])
     rows = attended[0][0].shape[0]
     piece = depth // tiles
     order = [0]
@@ -337,11 +339,19 @@
     direct = depth % LANES == 0
 
     def kernel(*rest):
-        refs, (mine_ref, other_ref, out_ref, *scratch) = rest[: heads * pairs], rest[heads * pairs :]
+        refs, (own_ref, mine_ref, other_ref, out_ref, *scratch) = rest[: heads * pairs], rest[heads * pairs :]
+        if not direct:
+            w, sems = scratch
+            copies = [
+                pltpu.make_async_copy(ref, w.at[:, pl.ds(s * depth, depth), :], sems.at[s])
+                for s, ref in enumerate((mine_ref, other_ref))
+            ]
+            for copy in copies:
+                copy.start()
         quarter = (lax.axis_index("band") & 1) * tiles + lax.axis_index("tiles")
         lane = lax.broadcasted_iota(jnp.int32, (rows, LANES), 1)
         groups = []
-        for i in range(heads):
+        for i in range(1, heads):
             group = [refs[i * pairs + p][...].astype(jnp.float32) for p in range(pairs)]
             size = piece
             while size < depth * 2:
@@ -355,37 +365,31 @@
                 group = [jnp.where(flip, m, x) for m, x in zip(moved, group)]
                 size *= 2
             groups.append([x.astype(jnp.bfloat16) for x in group])
+        total = dot_f32(jnp.concatenate([ref[...] for ref in refs[:pairs]], axis=1), own_ref[...])
         if direct:
             half = depth // LANES
             near_cols = jnp.concatenate([x for group in groups for x in group[:half]], axis=1)
             far_cols = jnp.concatenate([x for group in groups for x in group[half:]], axis=1)
-            total = dot_f32(near_cols, mine_ref[...].reshape(heads * depth, width))
-            total += dot_f32(far_cols, other_ref[...].reshape(heads * depth, width))
+            total += dot_f32(near_cols, mine_ref[...].reshape((heads - 1) * depth, width))
+            total += dot_f32(far_cols, other_ref[...].reshape((heads - 1) * depth, width))
         else:
-            w, sems = scratch
-            copies = [
-                pltpu.make_async_copy(ref, w.at[:, pl.ds(s * depth, depth), :], sems.at[s])
-                for s, ref in enumerate((mine_ref, other_ref))
-            ]
-            for copy in copies:
-                copy.start()
             for copy in copies:
                 copy.wait()
             cols = jnp.concatenate([x for group in groups for x in group], axis=1)
-            total = dot_f32(cols, w[...].reshape(heads * 2 * depth, width))
+            total += dot_f32(cols, w[...].reshape((heads - 1) * 2 * depth, width))
         out_ref[...] = total.astype(jnp.bfloat16)
 
-    scratch = [] if direct else [pltpu.VMEM((heads, 2 * depth, width), jnp.bfloat16), pltpu.SemaphoreType.DMA((2,))]
+    scratch = [pltpu.VMEM((heads - 1, 2 * depth, width), jnp.bfloat16), pltpu.SemaphoreType.DMA((2,))]
     return pl.pallas_call(
         kernel,
         out_shape=jax.ShapeDtypeStruct((rows, width), jnp.bfloat16),
-        in_specs=[VMEM] * len(pieces) + [VMEM if direct else ANY] * 2,
+        in_specs=[VMEM] * (len(pieces) + 1) + [VMEM if direct else ANY] * 2,
         out_specs=VMEM,
-        scratch_shapes=scratch,
+        scratch_shapes=[] if direct else scratch,
         compiler_params=SMALL,
         cost_estimate=FREE,
         name="project_out",
-    )(*pieces, w_mine, w_other)
+    )(*pieces, w_out, w_mine, w_other)
 
 
 def on_device(sizes, tokens, w_query, w_key, w_value, w_out, block_mask):
@@ -409,6 +413,7 @@
         return found
 
     kv = project_kv(block_mask, tokens, w_key, w_value)
+    *kv, own = kv
     kv = [list(kv[:2])] + [[one] for one in kv[2:]]
     pairs = len(kv)
     far = [[[along_band(one, lambda i: (i + 2 * r) % bands) for one in arrays] for r in hops] for arrays in kv]
@@ -427,7 +432,7 @@
     w_mine, kv = lax.optimization_barrier((w_mine, kv))
     bit = heads // 2
     w_mine, arriving = widen(w_mine[None], None, bit)
-    queries, bias, state = begin_attention(block_mask, tokens, w_query, kv[0] + near[0], heads, source_bands)
+    queries, bias, state = begin_attention(block_mask, tokens, w_query, [own] + near[0], heads, source_bands)
     far[0], queries, arriving = lax.optimization_barrier((far[0], queries, arriving))
     while bit > 1:
         bit //= 2
@@ -441,7 +446,7 @@
 
     last = pairs - 1
     if last == 0:
-        w_mine = jnp.concatenate([w_mine, arriving])
+        w_mine = jnp.concatenate([w_mine, arriving])[1:]
         arriving = other_tiles(w_mine)
     for p in range(pairs):
         if p > 0:
@@ -454,17 +459,17 @@
             pieces = attend(queries[p], held, sources, bias, first, heads, 0, heads, 0)
             if p == 0:
                 pieces, arriving = lax.optimization_barrier((pieces, arriving))
-                w_mine = jnp.concatenate([w_mine, arriving])
+                w_mine = jnp.concatenate([w_mine, arriving])[1:]
                 arriving = other_tiles(w_mine)
             exchange(pieces, 0)
         else:
-            pieces = attend(queries[p], held, sources, bias, first, heads, 1, heads - 1, 0)
+            pieces = attend(queries[p], held, sources, bias, first, heads, 1, heads - 1, 2**31)
             pieces, attended, sources[-1] = lax.optimization_barrier((pieces, attended, sources[-1]))
             exchange(pieces, 1)
             arriving, sources[-1] = lax.optimization_barrier((arriving, sources[-1]))
             exchange(attend(queries[p], held, sources, bias, first, heads, 0, 1, LONG), 0)
     w_mine = jnp.concatenate([w_mine] + arriving, axis=1)
-    return project_out(attended, w_mine, to_sibling(w_mine), tiles)
+    return project_out(attended, w_out, w_mine, to_sibling(w_mine), tiles)
 
 
 def solution(mesh):

time: 52.4 us -> 50.9 us (0.971)
  local copies, waits for them, and re-layouts: 1.87 us -> 1.05 us
  waiting for transfers between devices: 2.97 us -> 2.19 us
    ppermute x10, waiting for transfers between devices: 2.63 us -> 1.23 us  [along_band(): return lax.ppermute(array, 'band', [(i, goes_to(i)) for i in range(bands)])]
    unnamed x14 -> x13, local copies, waits for them, and re-layouts: 1.87 us -> 1.02 us
    ppermute x8, waiting for transfers between devices: 0.33 us -> 0.96 us  [along_head(): return lax.ppermute(array, 'head', [(i, i ^ k) for i in range(heads)])]
  transfers between devices with their start and end apart: 19 -> 19, of which waited for: 2 -> 3; matrix products, arithmetic and copies ran while one was open for 0% -> 0% of each run, Pallas kernels for 40% -> 40%
where the time goes in v5:
time: 50.9 us; the launch traced here: 50.8 us
  Pallas kernels  26.4 us (52%)
  starting transfers between devices  20.9 us (41%)
  waiting for transfers between devices  2.19 us (4%)
  local copies, waits for them, and re-layouts  1.05 us (2%)
    pallas_call x3, Pallas kernels, attend(): pl.pallas_call(kernel, out_shape=[jax.ShapeDtypeStruct((part, LANES), jnp...  15.2 us
    ppermute x8, starting transfers between devices, along_head(): return lax.ppermute(array, 'head', [(i, i ^ k) for i in range(heads)])  13.4 us
    ppermute x10, starting transfers between devices, along_band(): return lax.ppermute(array, 'band', [(i, goes_to(i)) for i in range(bands)])  5.92 us
    pallas_call x1, Pallas kernels, begin_attention(): pl.pallas_call(kernel, out_shape=[jax.ShapeDtypeStruct((2, rows, LANES),...  5.25 us
    pallas_call x1, Pallas kernels, project_kv(): pl.pallas_call(kernel, out_shape=[jax.ShapeDtypeStruct((rows, LANES), jnp...  4.24 us
    pallas_call x1, Pallas kernels, project_out(): pl.pallas_call(kernel, out_shape=jax.ShapeDtypeStruct((rows, width), jnp....  1.72 us
    ppermute x1, starting transfers between devices, other_tiles(): lax.ppermute(array, 'tiles', [(i, i ^ s) for i in range(tiles)])  1.58 us
    ppermute x10, waiting for transfers between devices, along_band(): return lax.ppermute(array, 'band', [(i, goes_to(i)) for i in range(bands)])  1.23 us
  transfers between devices with their start and end apart: 19, of which 3 were waited for; matrix products, arithmetic and copies ran while one was open for 0% of the time, Pallas kernels for 40%

profile of v5, /device:TPU:0, one launch (start us, length us, event | category | flops | bytes accessed | tf_op | source)
XLA Modules:
  0.0 50.8 jit_solution(18384990725448843220)
XLA Ops:
  0.0 4.2 %project_kv.1 = (bf16[768,128]{1,0:T(8,128)(2,1)}, bf16[768,128]{1,0:T(8,128)(2,1)}, bf16[2,768,128]{2,1,0:T(8,128)(2,1)}, bf16[2,768,128]{2,1,0:T(8,128)(2,1)}) custom-call(s32[32,32]{1,0:T(8,128)} %mask_ref.1, bf16[1024,1024]{1,0:T(8,128)(2,1)} %tok.1, bf16[1024,256]{1,0:T(8,128)(2,1)} %wk_ref.1, bf16[1024,256]{1,0:T(8,128)(2,1)} %wv_ref.1), custom_call_target="tpu_custom_call" | custom-call | tf_op jit(solution)/shard_map/project_kv/pallas_call | solution.py:123
  4.3 0.5 %collective-permute-start.2 = (bf16[768,128]{1,0:T(8,128)(2,1)}, bf16[768,128]{1,0:T(8,128)(2,1)}, u32[]{:S(2)}, u32[]{:S(2)}) collective-permute-start(bf16[768,128]{1,0:T(8,128)(2,1)} %get-tuple-element.43), channel_id=1, source_target_pairs={{0,4},{4,0},{8,12},{12,8},{1,5},{5,1},{9,13},{13,9},{2,6},{6,2},{1... | collective-permute-start | bytes 589832 | tf_op jit(solution)/shard_map/ppermute | solution.py:400
  4.8 2.6 %collective-permute-start = (bf16[768,128]{1,0:T(8,128)(2,1)}, bf16[768,128]{1,0:T(8,128)(2,1)S(1)}, u32[]{:S(2)}, u32[]{:S(2)}) collective-permute-start(bf16[768,128]{1,0:T(8,128)(2,1)} %get-tuple-element.43), channel_id=1, source_target_pairs={{0,8},{4,12},{8,0},{12,4},{1,9},{5,13},{9,1},{13,5},{2,10},{6,14},... | collective-permute-start | bytes 589832 | tf_op jit(solution)/shard_map/ppermute | solution.py:400
  7.4 0.2 collective-permute-start.3
  7.5 0.3 collective-permute-start.1
  7.8 0.0 copy-done.1
  7.8 2.9 %collective-permute-start.4 = (bf16[1,64,1024]{2,1,0:T(8,128)(2,1)S(1)}, bf16[1,64,1024]{2,1,0:T(8,128)(2,1)S(1)}, u32[]{:S(2)}, u32[]{:S(2)}) collective-permute-start(bf16[1,64,1024]{2,1,0:T(8,128)(2,1)S(1)} %bitcast.1), channel_id=1, source_target_pairs={{0,2},{1,3},{2,0},{3,1},{4,6},{5,7},{6,4},{7,5},{8,10},{9,11},{10,... | collective-permute-start | bytes 393224 | tf_op jit(solution)/shard_map/ppermute | solution.py:406
  10.7 0.0 collective-permute-done.2.rest_1_
  10.7 1.5 %collective-permute-start.6 = (bf16[2,768,128]{2,1,0:T(8,128)(2,1)}, bf16[2,768,128]{2,1,0:T(8,128)(2,1)S(1)}, u32[]{:S(2)}, u32[]{:S(2)}) collective-permute-start(bf16[2,768,128]{2,1,0:T(8,128)(2,1)} %get-tuple-element.52.rest_0_), channel_id=1, source_target_pairs={{0,8},{4,12},{8,0},{12,4},{1,9},{5,13},{9,1},{13,5},{2,10},{6,14},... | collective-permute-start | bytes 1179656 | tf_op jit(solution)/shard_map/ppermute | solution.py:400
  12.2 0.0 collective-permute-done.3.rest_2_
  12.2 0.0 copy-done.4
  12.3 1.0 %copy-done.3 = bf16[2,768,128]{2,1,0:T(8,128)(2,1)S(1)} copy-done((bf16[2,768,128]{2,1,0:T(8,128)(2,1)S(1)}, bf16[2,768,128]{2,1,0:T(8,128)(2,1)}, u32[]{:S(2)}) %copy-start.3) | copy-done | bytes 393240
  13.2 5.2 %begin_attention.1 = (bf16[2,1024,128]{2,1,0:T(8,128)(2,1)S(1)}, bf16[2,1024,128]{2,1,0:T(8,128)(2,1)S(1)}, f32[32,128]{1,0:T(8,128)S(1)}, f32[2,1024,128]{2,1,0:T(8,128)S(1)}) custom-call(s32[32,32]{1,0:T(8,128)S(1)} %copy-done.4, bf16[1024,1024]{1,0:T(8,128)(2,1)S(1)} %copy-done, bf16[1024,256]{1,0:T(8,128)(2,1)S(1)} %copy-done.2, ...), custom_call_target="tpu_custom_call" | custom-call | tf_op jit(solution)/shard_map/begin_attention/pallas_call | solution.py:265
  18.5 0.0 collective-permute-done.4
  18.5 0.0 collective-permute-done.rest_1_
  18.5 0.0 collective-permute-done.1.rest_2_
  18.6 1.6 %collective-permute-start.9 = (bf16[2,64,1024]{2,1,0:T(8,128)(2,1)S(1)}, bf16[2,64,1024]{2,1,0:T(8,128)(2,1)S(1)}, u32[]{:S(2)}, u32[]{:S(2)}) collective-permute-start(bf16[2,64,1024]{2,1,0:T(8,128)(2,1)S(1)} %pad_maximum_fusion.1), channel_id=1, source_target_pairs={{0,1},{1,0},{2,3},{3,2},{4,5},{5,4},{6,7},{7,6},{8,9},{9,8},{10,11... | collective-permute-start | bytes 786440 | tf_op jit(solution)/shard_map/ppermute | solution.py:406
  20.2 0.0 collective-permute-start.7
  20.2 0.5 collective-permute-start.8
  20.7 0.0 collective-permute-start.5
  20.7 0.9 %collective-permute-done.7.rest_3_ = bf16[768,128]{1,0:T(8,128)(2,1)S(1)} collective-permute-done((bf16[768,128]{1,0:T(8,128)(2,1)S(1)}, bf16[768,128]{1,0:T(8,128)(2,1)S(1)}, u32[]{:S(2)}, u32[]{:S(2)}) %collective-permute-start.7) | collective-permute-done | bytes 196640 | tf_op jit(solution)/shard_map/ppermute | solution.py:400
  21.7 0.3 collective-permute-done.8.rest_4_
  21.9 5.2 %attend.3 = (bf16[256,128]{1,0:T(8,128)(2,1)S(1)}, bf16[256,128]{1,0:T(8,128)(2,1)S(1)}, bf16[256,128]{1,0:T(8,128)(2,1)S(1)}, bf16[256,128]{1,0:T(8,128)(2,1)S(1)}) custom-call(bf16[2,1024,128]{2,1,0:T(8,128)(2,1)S(1)} %get-tuple-element.53.q_ref, f32[32,128]{1,0:T(8,128)S(1)} %get-tuple-element.51.bias_ref, f32[2,1024,128]{2,1,0:T(8,128)S(1)} %get-tuple-element.54.rest_0_, ...), custom_call_target="tpu_custom_call" | custom-call | tf_op jit(solution)/shard_map/attend/pallas_call | solution.py:316
  27.2 0.0 collective-permute-done.9
  27.2 0.0 collective-permute-done.6.rest_2_
  27.2 0.3 collective-permute-start.10
  27.5 1.6 %collective-permute-start.14 = (bf16[3,64,1024]{2,1,0:T(8,128)(2,1)S(1)}, bf16[3,64,1024]{2,1,0:T(8,128)(2,1)S(1)}, u32[]{:S(2)}, u32[]{:S(2)}) collective-permute-start(bf16[3,64,1024]{2,1,0:T(8,128)(2,1)S(1)} %constant_dynamic-update-slice_fusion), channel_id=1, source_target_pairs={{0,16},{16,0},{1,17},{17,1},{2,18},{18,2},{3,19},{19,3},{4,20},{20... | collective-permute-start | bytes 1179656 | tf_op jit(solution)/shard_map/ppermute | solution.py:427
  29.1 0.4 collective-permute-start.11
  29.6 2.2 %collective-permute-start.12 = (bf16[256,128]{1,0:T(8,128)(2,1)S(1)}, bf16[256,128]{1,0:T(8,128)(2,1)S(1)}, u32[]{:S(2)}, u32[]{:S(2)}) collective-permute-start(bf16[256,128]{1,0:T(8,128)(2,1)S(1)} %get-tuple-element.64), channel_id=1, source_target_pairs={{0,2},{1,3},{2,0},{3,1},{4,6},{5,7},{6,4},{7,5},{8,10},{9,11},{10,... | collective-permute-start | bytes 196616 | tf_op jit(solution)/shard_map/ppermute | solution.py:406
  31.8 0.0 collective-permute-done.5.rest_1_
  31.8 1.7 %collective-permute-start.13 = (bf16[256,128]{1,0:T(8,128)(2,1)S(1)}, bf16[256,128]{1,0:T(8,128)(2,1)S(1)}, u32[]{:S(2)}, u32[]{:S(2)}) collective-permute-start(bf16[256,128]{1,0:T(8,128)(2,1)S(1)} %get-tuple-element.65), channel_id=1, source_target_pairs={{0,3},{1,2},{2,1},{3,0},{4,7},{5,6},{6,5},{7,4},{8,11},{9,10},{10,... | collective-permute-start | bytes 196616 | tf_op jit(solution)/shard_map/ppermute | solution.py:406
  33.5 0.0 collective-permute-done.10.rest_3_
  33.5 6.5 %attend.4 = (bf16[256,128]{1,0:T(8,128)(2,1)S(1)}, bf16[256,128]{1,0:T(8,128)(2,1)S(1)}, bf16[256,128]{1,0:T(8,128)(2,1)S(1)}) custom-call(bf16[2,1024,128]{2,1,0:T(8,128)(2,1)S(1)} %get-tuple-element.50.q_ref, f32[32,128]{1,0:T(8,128)S(1)} %get-tuple-element.51.bias_ref, bf16[2,768,128]{2,1,0:T(8,128)(2,1)S(1)} %copy-done.5, ...), custom_call_target="tpu_custom_call" | custom-call | flops 2147483648 | tf_op jit(solution)/shard_map/attend/pallas_call | solution.py:316
  40.1 0.0 collective-permute-done.11.rest_4_
  40.1 0.0 collective-permute-done.12.rest_2_
  40.1 0.0 collective-permute-done.13.rest_6_
  40.1 0.0 collective-permute-done.14
  40.1 0.1 pad_maximum_fusion.rest_9_
  40.2 0.1 collective-permute-start.18
  40.2 1.2 %collective-permute-start.15 = (bf16[256,128]{1,0:T(8,128)(2,1)S(1)}, bf16[256,128]{1,0:T(8,128)(2,1)S(1)}, u32[]{:S(2)}, u32[]{:S(2)}) collective-permute-start(bf16[256,128]{1,0:T(8,128)(2,1)S(1)} %get-tuple-element.75), channel_id=1, source_target_pairs={{0,2},{1,3},{2,0},{3,1},{4,6},{5,7},{6,4},{7,5},{8,10},{9,11},{10,... | collective-permute-start | bytes 196616 | tf_op jit(solution)/shard_map/ppermute | solution.py:406
  41.4 1.5 %collective-permute-start.16 = (bf16[256,128]{1,0:T(8,128)(2,1)S(1)}, bf16[256,128]{1,0:T(8,128)(2,1)S(1)}, u32[]{:S(2)}, u32[]{:S(2)}) collective-permute-start(bf16[256,128]{1,0:T(8,128)(2,1)S(1)} %get-tuple-element.77), channel_id=1, source_target_pairs={{0,1},{1,0},{2,3},{3,2},{4,5},{5,4},{6,7},{7,6},{8,9},{9,8},{10,11... | collective-permute-start | bytes 196616 | tf_op jit(solution)/shard_map/ppermute | solution.py:406
  42.9 1.7 %collective-permute-start.17 = (bf16[256,128]{1,0:T(8,128)(2,1)S(1)}, bf16[256,128]{1,0:T(8,128)(2,1)S(1)}, u32[]{:S(2)}, u32[]{:S(2)}) collective-permute-start(bf16[256,128]{1,0:T(8,128)(2,1)S(1)} %get-tuple-element.79), channel_id=1, source_target_pairs={{0,3},{1,2},{2,1},{3,0},{4,7},{5,6},{6,5},{7,4},{8,11},{9,10},{10,... | collective-permute-start | bytes 196616 | tf_op jit(solution)/shard_map/ppermute | solution.py:406
  44.7 3.4 %attend.5.rest_1_ = bf16[256,128]{1,0:T(8,128)(2,1)S(1)} custom-call(bf16[2,1024,128]{2,1,0:T(8,128)(2,1)S(1)} %get-tuple-element.50.q_ref, f32[32,128]{1,0:T(8,128)S(1)} %get-tuple-element.51.bias_ref, bf16[2,768,128]{2,1,0:T(8,128)(2,1)S(1)} %copy-done.5, bf16[2,768,128]{2,1,0:T(8,128)(2,1)S(1)} %collective-permute-done.5.rest_1_, ...), custom_call_target="tpu_custom_call" | custom-call | flops 8589934592 | tf_op jit(solution)/shard_map/attend/pallas_call | solution.py:316
  48.1 0.0 collective-permute-done.15.rest_3_
  48.1 0.0 collective-permute-done.16.rest_5_
  48.1 0.9 %collective-permute-done.17.rest_7_ = bf16[256,128]{1,0:T(8,128)(2,1)S(1)} collective-permute-done((bf16[256,128]{1,0:T(8,128)(2,1)S(1)}, bf16[256,128]{1,0:T(8,128)(2,1)S(1)}, u32[]{:S(2)}, u32[]{:S(2)}) %collective-permute-start.17) | collective-permute-done | bytes 65568 | tf_op jit(solution)/shard_map/ppermute | solution.py:406
  49.1 0.0 collective-permute-done.18.rest_10_
  49.1 1.7 %project_out.1 = bf16[256,1024]{1,0:T(8,128)(2,1)} custom-call(bf16[256,128]{1,0:T(8,128)(2,1)S(1)} %get-tuple-element.70.rest_0_, bf16[256,128]{1,0:T(8,128)(2,1)S(1)} %attend.5.rest_1_, bf16[256,128]{1,0:T(8,128)(2,1)S(1)} %collective-permute-done.12.rest_2_, bf16[256,128]{1,0:T(8,128)(2,1)S(1)} %collective-permute-done.15.rest_3_, ...), custom_call_target="tpu_custom_call" | custom-call | tf_op jit(solution)/shard_map/project_out/pallas_call | solution.py:383
  (13 shorter events, 0.1 us)
Async XLA Ops:
  0.0 12.2 %copy-start.4 = (s32[32,32]{1,0:T(8,128)S(1)}, s32[32,32]{1,0:T(8,128)}, u32[]{:S(2)}) copy-start(s32[32,32]{1,0:T(8,128)} %mask_ref.1) | copy-start | bytes 12292
  0.0 12.2 %copy-start = (bf16[1024,1024]{1,0:T(8,128)(2,1)S(1)}, bf16[1024,1024]{1,0:T(8,128)(2,1)}, u32[]{:S(2)}) copy-start(bf16[1024,1024]{1,0:T(8,128)(2,1)} %tok.1) | copy-start | bytes 6291460
  0.0 7.8 %copy-start.1 = (bf16[256,1024]{1,0:T(8,128)(2,1)S(1)}, bf16[256,1024]{1,0:T(8,128)(2,1)}, u32[]{:S(2)}) copy-start(bf16[256,1024]{1,0:T(8,128)(2,1)} %rest_8_.1) | copy-start | bytes 1572868
  0.0 12.2 %copy-start.2 = (bf16[1024,256]{1,0:T(8,128)(2,1)S(1)}, bf16[1024,256]{1,0:T(8,128)(2,1)}, u32[]{:S(2)}) copy-start(bf16[1024,256]{1,0:T(8,128)(2,1)} %w_any.1) | copy-start | bytes 1572868
  4.3 6.5 %collective-permute-start.2 = (bf16[768,128]{1,0:T(8,128)(2,1)}, bf16[768,128]{1,0:T(8,128)(2,1)}, u32[]{:S(2)}, u32[]{:S(2)}) collective-permute-start(bf16[768,128]{1,0:T(8,128)(2,1)} %get-tuple-element.43), channel_id=1, source_target_pairs={{0,4},{4,0},{8,12},{12,8},{1,5},{5,1},{9,13},{13,9},{2,6},{6,2},{1... | collective-permute-start | bytes 589832 | tf_op jit(solution)/shard_map/ppermute | solution.py:400
  4.8 13.7 %collective-permute-start = (bf16[768,128]{1,0:T(8,128)(2,1)}, bf16[768,128]{1,0:T(8,128)(2,1)S(1)}, u32[]{:S(2)}, u32[]{:S(2)}) collective-permute-start(bf16[768,128]{1,0:T(8,128)(2,1)} %get-tuple-element.43), channel_id=1, source_target_pairs={{0,8},{4,12},{8,0},{12,4},{1,9},{5,13},{9,1},{13,5},{2,10},{6,14},... | collective-permute-start | bytes 589832 | tf_op jit(solution)/shard_map/ppermute | solution.py:400
  7.4 4.9 %collective-permute-start.3 = (bf16[768,128]{1,0:T(8,128)(2,1)}, bf16[768,128]{1,0:T(8,128)(2,1)}, u32[]{:S(2)}, u32[]{:S(2)}) collective-permute-start(bf16[768,128]{1,0:T(8,128)(2,1)} %get-tuple-element.44), channel_id=1, source_target_pairs={{0,4},{4,0},{8,12},{12,8},{1,5},{5,1},{9,13},{13,9},{2,6},{6,2},{1... | collective-permute-start | bytes 589832 | tf_op jit(solution)/shard_map/ppermute | solution.py:400
  7.5 11.0 %collective-permute-start.1 = (bf16[768,128]{1,0:T(8,128)(2,1)}, bf16[768,128]{1,0:T(8,128)(2,1)S(1)}, u32[]{:S(2)}, u32[]{:S(2)}) collective-permute-start(bf16[768,128]{1,0:T(8,128)(2,1)} %get-tuple-element.44), channel_id=1, source_target_pairs={{0,8},{4,12},{8,0},{12,4},{1,9},{5,13},{9,1},{13,5},{2,10},{6,14},... | collective-permute-start | bytes 589832 | tf_op jit(solution)/shard_map/ppermute | solution.py:400
  7.8 10.7 %collective-permute-start.4 = (bf16[1,64,1024]{2,1,0:T(8,128)(2,1)S(1)}, bf16[1,64,1024]{2,1,0:T(8,128)(2,1)S(1)}, u32[]{:S(2)}, u32[]{:S(2)}) collective-permute-start(bf16[1,64,1024]{2,1,0:T(8,128)(2,1)S(1)} %bitcast.1), channel_id=1, source_target_pairs={{0,2},{1,3},{2,0},{3,1},{4,6},{5,7},{6,4},{7,5},{8,10},{9,11},{10,... | collective-permute-start | bytes 393224 | tf_op jit(solution)/shard_map/ppermute | solution.py:406
  10.7 16.5 %collective-permute-start.6 = (bf16[2,768,128]{2,1,0:T(8,128)(2,1)}, bf16[2,768,128]{2,1,0:T(8,128)(2,1)S(1)}, u32[]{:S(2)}, u32[]{:S(2)}) collective-permute-start(bf16[2,768,128]{2,1,0:T(8,128)(2,1)} %get-tuple-element.52.rest_0_), channel_id=1, source_target_pairs={{0,8},{4,12},{8,0},{12,4},{1,9},{5,13},{9,1},{13,5},{2,10},{6,14},... | collective-permute-start | bytes 1179656 | tf_op jit(solution)/shard_map/ppermute | solution.py:400
  12.2 1.0 %copy-start.3 = (bf16[2,768,128]{2,1,0:T(8,128)(2,1)S(1)}, bf16[2,768,128]{2,1,0:T(8,128)(2,1)}, u32[]{:S(2)}) copy-start(bf16[2,768,128]{2,1,0:T(8,128)(2,1)} %get-tuple-element.45.rest_0_) | copy-start | bytes 1179652
  13.2 7.5 %copy-start.5 = (bf16[2,768,128]{2,1,0:T(8,128)(2,1)S(1)}, bf16[2,768,128]{2,1,0:T(8,128)(2,1)}, u32[]{:S(2)}) copy-start(bf16[2,768,128]{2,1,0:T(8,128)(2,1)} %get-tuple-element.52.rest_0_) | copy-start | bytes 1179652
  18.6 8.6 %collective-permute-start.9 = (bf16[2,64,1024]{2,1,0:T(8,128)(2,1)S(1)}, bf16[2,64,1024]{2,1,0:T(8,128)(2,1)S(1)}, u32[]{:S(2)}, u32[]{:S(2)}) collective-permute-start(bf16[2,64,1024]{2,1,0:T(8,128)(2,1)S(1)} %pad_maximum_fusion.1), channel_id=1, source_target_pairs={{0,1},{1,0},{2,3},{3,2},{4,5},{5,4},{6,7},{7,6},{8,9},{9,8},{10,11... | collective-permute-start | bytes 786440 | tf_op jit(solution)/shard_map/ppermute | solution.py:406
  20.2 1.4 %collective-permute-start.7 = (bf16[768,128]{1,0:T(8,128)(2,1)S(1)}, bf16[768,128]{1,0:T(8,128)(2,1)S(1)}, u32[]{:S(2)}, u32[]{:S(2)}) collective-permute-start(bf16[768,128]{1,0:T(8,128)(2,1)S(1)} %collective-permute-done.rest_1_), channel_id=1, source_target_pairs={{0,4},{4,0},{8,12},{12,8},{1,5},{5,1},{9,13},{13,9},{2,6},{6,2},{1... | collective-permute-start | bytes 589832 | tf_op jit(solution)/shard_map/ppermute | solution.py:400
  20.2 1.7 %collective-permute-start.8 = (bf16[768,128]{1,0:T(8,128)(2,1)S(1)}, bf16[768,128]{1,0:T(8,128)(2,1)S(1)}, u32[]{:S(2)}, u32[]{:S(2)}) collective-permute-start(bf16[768,128]{1,0:T(8,128)(2,1)S(1)} %collective-permute-done.1.rest_2_), channel_id=1, source_target_pairs={{0,4},{4,0},{8,12},{12,8},{1,5},{5,1},{9,13},{13,9},{2,6},{6,2},{1... | collective-permute-start | bytes 589832 | tf_op jit(solution)/shard_map/ppermute | solution.py:400
  20.7 11.0 %collective-permute-start.5 = (bf16[2,768,128]{2,1,0:T(8,128)(2,1)S(1)}, bf16[2,768,128]{2,1,0:T(8,128)(2,1)S(1)}, u32[]{:S(2)}, u32[]{:S(2)}) collective-permute-start(bf16[2,768,128]{2,1,0:T(8,128)(2,1)S(1)} %copy-done.5), channel_id=1, source_target_pairs={{0,4},{4,0},{8,12},{12,8},{1,5},{5,1},{9,13},{13,9},{2,6},{6,2},{1... | collective-permute-start | bytes 1179656 | tf_op jit(solution)/shard_map/ppermute | solution.py:400
  27.2 6.3 %collective-permute-start.10 = (bf16[2,768,128]{2,1,0:T(8,128)(2,1)S(1)}, bf16[2,768,128]{2,1,0:T(8,128)(2,1)S(1)}, u32[]{:S(2)}, u32[]{:S(2)}) collective-permute-start(bf16[2,768,128]{2,1,0:T(8,128)(2,1)S(1)} %collective-permute-done.6.rest_2_), channel_id=1, source_target_pairs={{0,4},{4,0},{8,12},{12,8},{1,5},{5,1},{9,13},{13,9},{2,6},{6,2},{1... | collective-permute-start | bytes 1179656 | tf_op jit(solution)/shard_map/ppermute | solution.py:400
  27.5 12.6 %collective-permute-start.14 = (bf16[3,64,1024]{2,1,0:T(8,128)(2,1)S(1)}, bf16[3,64,1024]{2,1,0:T(8,128)(2,1)S(1)}, u32[]{:S(2)}, u32[]{:S(2)}) collective-permute-start(bf16[3,64,1024]{2,1,0:T(8,128)(2,1)S(1)} %constant_dynamic-update-slice_fusion), channel_id=1, source_target_pairs={{0,16},{16,0},{1,17},{17,1},{2,18},{18,2},{3,19},{19,3},{4,20},{20... | collective-permute-start | bytes 1179656 | tf_op jit(solution)/shard_map/ppermute | solution.py:427
  29.1 10.9 %collective-permute-start.11 = (bf16[256,128]{1,0:T(8,128)(2,1)S(1)}, bf16[256,128]{1,0:T(8,128)(2,1)S(1)}, u32[]{:S(2)}, u32[]{:S(2)}) collective-permute-start(bf16[256,128]{1,0:T(8,128)(2,1)S(1)} %get-tuple-element.63), channel_id=1, source_target_pairs={{0,1},{1,0},{2,3},{3,2},{4,5},{5,4},{6,7},{7,6},{8,9},{9,8},{10,11... | collective-permute-start | bytes 196616 | tf_op jit(solution)/shard_map/ppermute | solution.py:406
  29.6 10.5 %collective-permute-start.12 = (bf16[256,128]{1,0:T(8,128)(2,1)S(1)}, bf16[256,128]{1,0:T(8,128)(2,1)S(1)}, u32[]{:S(2)}, u32[]{:S(2)}) collective-permute-start(bf16[256,128]{1,0:T(8,128)(2,1)S(1)} %get-tuple-element.64), channel_id=1, source_target_pairs={{0,2},{1,3},{2,0},{3,1},{4,6},{5,7},{6,4},{7,5},{8,10},{9,11},{10,... | collective-permute-start | bytes 196616 | tf_op jit(solution)/shard_map/ppermute | solution.py:406
  31.8 8.3 %collective-permute-start.13 = (bf16[256,128]{1,0:T(8,128)(2,1)S(1)}, bf16[256,128]{1,0:T(8,128)(2,1)S(1)}, u32[]{:S(2)}, u32[]{:S(2)}) collective-permute-start(bf16[256,128]{1,0:T(8,128)(2,1)S(1)} %get-tuple-element.65), channel_id=1, source_target_pairs={{0,3},{1,2},{2,1},{3,0},{4,7},{5,6},{6,5},{7,4},{8,11},{9,10},{10,... | collective-permute-start | bytes 196616 | tf_op jit(solution)/shard_map/ppermute | solution.py:406
  40.2 8.9 %collective-permute-start.18 = (bf16[3,128,1024]{2,1,0:T(8,128)(2,1)S(1)}, bf16[3,128,1024]{2,1,0:T(8,128)(2,1)S(1)}, u32[]{:S(2)}, u32[]{:S(2)}) collective-permute-start(bf16[3,128,1024]{2,1,0:T(8,128)(2,1)S(1)} %pad_maximum_fusion.rest_9_), channel_id=1, source_target_pairs={{0,4},{4,0},{8,12},{12,8},{1,5},{5,1},{9,13},{13,9},{2,6},{6,2},{1... | collective-permute-start | bytes 2359304 | tf_op jit(solution)/shard_map/ppermute | solution.py:400
  40.2 7.9 %collective-permute-start.15 = (bf16[256,128]{1,0:T(8,128)(2,1)S(1)}, bf16[256,128]{1,0:T(8,128)(2,1)S(1)}, u32[]{:S(2)}, u32[]{:S(2)}) collective-permute-start(bf16[256,128]{1,0:T(8,128)(2,1)S(1)} %get-tuple-element.75), channel_id=1, source_target_pairs={{0,2},{1,3},{2,0},{3,1},{4,6},{5,7},{6,4},{7,5},{8,10},{9,11},{10,... | collective-permute-start | bytes 196616 | tf_op jit(solution)/shard_map/ppermute | solution.py:406
  41.4 6.7 %collective-permute-start.16 = (bf16[256,128]{1,0:T(8,128)(2,1)S(1)}, bf16[256,128]{1,0:T(8,128)(2,1)S(1)}, u32[]{:S(2)}, u32[]{:S(2)}) collective-permute-start(bf16[256,128]{1,0:T(8,128)(2,1)S(1)} %get-tuple-element.77), channel_id=1, source_target_pairs={{0,1},{1,0},{2,3},{3,2},{4,5},{5,4},{6,7},{7,6},{8,9},{9,8},{10,11... | collective-permute-start | bytes 196616 | tf_op jit(solution)/shard_map/ppermute | solution.py:406
  42.9 6.1 %collective-permute-start.17 = (bf16[256,128]{1,0:T(8,128)(2,1)S(1)}, bf16[256,128]{1,0:T(8,128)(2,1)S(1)}, u32[]{:S(2)}, u32[]{:S(2)}) collective-permute-start(bf16[256,128]{1,0:T(8,128)(2,1)S(1)} %get-tuple-element.79), channel_id=1, source_target_pairs={{0,3},{1,2},{2,1},{3,0},{4,7},{5,6},{6,5},{7,4},{8,11},{9,10},{10,... | collective-permute-start | bytes 196616 | tf_op jit(solution)/shard_map/ppermute | solution.py:406

commit v6 on v5

--- a/solution.py
+++ b/solution.py
@@ -60,7 +60,6 @@
 
 def project_kv(block_mask, tokens, w_key, w_value):
     pairs = w_key.shape[1] // LANES
-    rows_in = tokens.shape[0]
     rows = KEEP * BLK
     step = 2 * BLK
     steps = tokens.shape[1] // step
@@ -87,13 +86,15 @@
         digit = lax.broadcasted_iota(jnp.int32, picked.shape, 0)
         scale = (1 << (BAND_BITS * jnp.minimum(digit, KEEP))).astype(jnp.float32)
         code = jnp.sum(jnp.where(digit < KEEP, picked * place * scale, 0.0)).astype(jnp.int32)
-        low = low_lanes((rows_in, LANES))
+        low = low_lanes((rows, LANES))
+        begins = [pl.multiple_of(((code >> (BAND_BITS * e)) & (2**BAND_BITS - 1)) * BLK, BLK) for e in range(KEEP)]
         for c in range(steps):
             at = pl.ds(c * step, step)
             for copy in loads[3 * c : 3 * c + 3]:
                 copy.wait()
+            chosen = jnp.concatenate([tok[pl.ds(begin, BLK), at] for begin in begins], axis=0)
             for total, weight in ((keys, wk), (values, wv)):
-                product = dot_f32(tok[:, at], weight[at, :])
+                product = dot_f32(chosen, weight[at, :])
                 if c == 0:
                     total[...] = product
                 else:
@@ -103,20 +104,11 @@
             k, v = keys[:, cols], values[:, cols]
             held[p, 0] = jnp.where(low, k, swap_halves(v)).astype(jnp.bfloat16)
             held[p, 1] = jnp.where(low, swap_halves(k), v).astype(jnp.bfloat16)
-        stores = []
-        for p in range(pairs):
-            for e in range(KEEP):
-                begin = pl.multiple_of(((code >> (BAND_BITS * e)) & (2**BAND_BITS - 1)) * BLK, BLK)
-                block, at = pl.ds(begin, BLK), pl.ds(e * BLK, BLK)
-                if p == 0:
-                    moves = [(held.at[0, h, block, :], outs[h].at[at, :]) for h in range(2)]
-                    moves.append((held.at[0, :, block, :], own_ref.at[:, at, :]))
-                else:
-                    moves = [(held.at[p, :, block, :], outs[p + 1].at[:, at, :])]
-                for i, (source, to) in enumerate(moves):
-                    copy = pltpu.make_async_copy(source, to, out_sems.at[p, e, i])
-                    copy.start()
-                    stores.append(copy)
+        moves = [(held.at[0, 0], outs[0]), (held.at[0, 1], outs[1]), (held.at[0], own_ref)]
+        moves += [(held.at[p], outs[p + 1]) for p in range(1, pairs)]
+        stores = [pltpu.make_async_copy(source, to, out_sems.at[i]) for i, (source, to) in enumerate(moves)]
+        for copy in stores:
+            copy.start()
         for copy in stores:
             copy.wait()
 
@@ -131,11 +123,11 @@
             pltpu.VMEM(tokens.shape, jnp.bfloat16),
             pltpu.VMEM(w_key.shape, jnp.bfloat16),
             pltpu.VMEM(w_value.shape, jnp.bfloat16),
-            pltpu.VMEM((rows_in, w_key.shape[1]), jnp.float32),
-            pltpu.VMEM((rows_in, w_key.shape[1]), jnp.float32),
-            pltpu.VMEM((pairs, 2, rows_in, LANES), jnp.bfloat16),
+            pltpu.VMEM((rows, w_key.shape[1]), jnp.float32),
+            pltpu.VMEM((rows, w_key.shape[1]), jnp.float32),
+            pltpu.VMEM((pairs, 2, rows, LANES), jnp.bfloat16),
             pltpu.SemaphoreType.DMA((1 + 3 * steps,)),
-            pltpu.SemaphoreType.DMA((pairs, KEEP, 3)),
+            pltpu.SemaphoreType.DMA((pairs + 2,)),
         ],
         compiler_params=LARGE,
         cost_estimate=FREE,

time: 50.9 us -> 50.4 us (level)
  Pallas kernels: 26.4 us -> 25.8 us
    pallas_call x1, Pallas kernels: 4.24 us -> 3.69 us  [project_kv(): pl.pallas_call(kernel, out_shape=[jax.ShapeDtypeStruct((rows, LANES), jnp...]
  transfers between devices with their start and end apart: 19 -> 19, of which waited for: 3 -> 3; matrix products, arithmetic and copies ran while one was open for 0% -> 0% of each run, Pallas kernels for 40% -> 41%
where the time goes in v6:
time: 50.4 us; the launch traced here: 50.2 us
  Pallas kernels  25.8 us (51%)
  starting transfers between devices  20.9 us (41%)
  waiting for transfers between devices  2.18 us (4%)
  local copies, waits for them, and re-layouts  1.05 us (2%)
    pallas_call x3, Pallas kernels, attend(): pl.pallas_call(kernel, out_shape=[jax.ShapeDtypeStruct((part, LANES), jnp...  15.2 us
    ppermute x8, starting transfers between devices, along_head(): return lax.ppermute(array, 'head', [(i, i ^ k) for i in range(heads)])  13.4 us
    ppermute x10, starting transfers between devices, along_band(): return lax.ppermute(array, 'band', [(i, goes_to(i)) for i in range(bands)])  5.91 us
    pallas_call x1, Pallas kernels, begin_attention(): pl.pallas_call(kernel, out_shape=[jax.ShapeDtypeStruct((2, rows, LANES),...  5.25 us
    pallas_call x1, Pallas kernels, project_kv(): pl.pallas_call(kernel, out_shape=[jax.ShapeDtypeStruct((rows, LANES), jnp...  3.69 us
    pallas_call x1, Pallas kernels, project_out(): pl.pallas_call(kernel, out_shape=jax.ShapeDtypeStruct((rows, width), jnp....  1.72 us
    ppermute x1, starting transfers between devices, other_tiles(): lax.ppermute(array, 'tiles', [(i, i ^ s) for i in range(tiles)])  1.58 us
    ppermute x10, waiting for transfers between devices, along_band(): return lax.ppermute(array, 'band', [(i, goes_to(i)) for i in range(bands)])  1.23 us
  transfers between devices with their start and end apart: 19, of which 3 were waited for; matrix products, arithmetic and copies ran while one was open for 0% of the time, Pallas kernels for 41%

profile of v6, /device:TPU:0, one launch (start us, length us, event | category | flops | bytes accessed | tf_op | source)
XLA Modules:
  0.0 50.2 jit_solution(8108397041032833331)
XLA Ops:
  0.0 3.7 %project_kv.1 = (bf16[768,128]{1,0:T(8,128)(2,1)}, bf16[768,128]{1,0:T(8,128)(2,1)}, bf16[2,768,128]{2,1,0:T(8,128)(2,1)}, bf16[2,768,128]{2,1,0:T(8,128)(2,1)}) custom-call(s32[32,32]{1,0:T(8,128)} %mask_ref.1, bf16[1024,1024]{1,0:T(8,128)(2,1)} %tok.1, bf16[1024,256]{1,0:T(8,128)(2,1)} %wk_ref.1, bf16[1024,256]{1,0:T(8,128)(2,1)} %wv_ref.1), custom_call_target="tpu_custom_call" | custom-call | tf_op jit(solution)/shard_map/project_kv/pallas_call | solution.py:115
  3.7 0.5 %collective-permute-start.2 = (bf16[768,128]{1,0:T(8,128)(2,1)}, bf16[768,128]{1,0:T(8,128)(2,1)}, u32[]{:S(2)}, u32[]{:S(2)}) collective-permute-start(bf16[768,128]{1,0:T(8,128)(2,1)} %get-tuple-element.43), channel_id=1, source_target_pairs={{0,4},{4,0},{8,12},{12,8},{1,5},{5,1},{9,13},{13,9},{2,6},{6,2},{1... | collective-permute-start | bytes 589832 | tf_op jit(solution)/shard_map/ppermute | solution.py:392
  4.2 2.6 %collective-permute-start = (bf16[768,128]{1,0:T(8,128)(2,1)}, bf16[768,128]{1,0:T(8,128)(2,1)S(1)}, u32[]{:S(2)}, u32[]{:S(2)}) collective-permute-start(bf16[768,128]{1,0:T(8,128)(2,1)} %get-tuple-element.43), channel_id=1, source_target_pairs={{0,8},{4,12},{8,0},{12,4},{1,9},{5,13},{9,1},{13,5},{2,10},{6,14},... | collective-permute-start | bytes 589832 | tf_op jit(solution)/shard_map/ppermute | solution.py:392
  6.8 0.2 collective-permute-start.3
  7.0 0.3 collective-permute-start.1
  7.2 0.0 copy-done.1
  7.3 2.9 %collective-permute-start.4 = (bf16[1,64,1024]{2,1,0:T(8,128)(2,1)S(1)}, bf16[1,64,1024]{2,1,0:T(8,128)(2,1)S(1)}, u32[]{:S(2)}, u32[]{:S(2)}) collective-permute-start(bf16[1,64,1024]{2,1,0:T(8,128)(2,1)S(1)} %bitcast.1), channel_id=1, source_target_pairs={{0,2},{1,3},{2,0},{3,1},{4,6},{5,7},{6,4},{7,5},{8,10},{9,11},{10,... | collective-permute-start | bytes 393224 | tf_op jit(solution)/shard_map/ppermute | solution.py:398
  10.2 0.0 collective-permute-done.2.rest_1_
  10.2 1.5 %collective-permute-start.6 = (bf16[2,768,128]{2,1,0:T(8,128)(2,1)}, bf16[2,768,128]{2,1,0:T(8,128)(2,1)S(1)}, u32[]{:S(2)}, u32[]{:S(2)}) collective-permute-start(bf16[2,768,128]{2,1,0:T(8,128)(2,1)} %get-tuple-element.52.rest_0_), channel_id=1, source_target_pairs={{0,8},{4,12},{8,0},{12,4},{1,9},{5,13},{9,1},{13,5},{2,10},{6,14},... | collective-permute-start | bytes 1179656 | tf_op jit(solution)/shard_map/ppermute | solution.py:392
  11.7 0.0 collective-permute-done.3.rest_2_
  11.7 1.0 %copy-done.3 = bf16[2,768,128]{2,1,0:T(8,128)(2,1)S(1)} copy-done((bf16[2,768,128]{2,1,0:T(8,128)(2,1)S(1)}, bf16[2,768,128]{2,1,0:T(8,128)(2,1)}, u32[]{:S(2)}) %copy-start.3) | copy-done | bytes 393240
  12.7 5.2 %begin_attention.1 = (bf16[2,1024,128]{2,1,0:T(8,128)(2,1)S(1)}, bf16[2,1024,128]{2,1,0:T(8,128)(2,1)S(1)}, f32[32,128]{1,0:T(8,128)S(1)}, f32[2,1024,128]{2,1,0:T(8,128)S(1)}) custom-call(s32[32,32]{1,0:T(8,128)S(1)} %copy-done.4, bf16[1024,1024]{1,0:T(8,128)(2,1)S(1)} %copy-done, bf16[1024,256]{1,0:T(8,128)(2,1)S(1)} %copy-done.2, ...), custom_call_target="tpu_custom_call" | custom-call | tf_op jit(solution)/shard_map/begin_attention/pallas_call | solution.py:257
  18.0 0.0 collective-permute-done.4
  18.0 0.0 collective-permute-done.rest_1_
  18.0 0.0 collective-permute-done.1.rest_2_
  18.0 1.6 %collective-permute-start.9 = (bf16[2,64,1024]{2,1,0:T(8,128)(2,1)S(1)}, bf16[2,64,1024]{2,1,0:T(8,128)(2,1)S(1)}, u32[]{:S(2)}, u32[]{:S(2)}) collective-permute-start(bf16[2,64,1024]{2,1,0:T(8,128)(2,1)S(1)} %pad_maximum_fusion.1), channel_id=1, source_target_pairs={{0,1},{1,0},{2,3},{3,2},{4,5},{5,4},{6,7},{7,6},{8,9},{9,8},{10,11... | collective-permute-start | bytes 786440 | tf_op jit(solution)/shard_map/ppermute | solution.py:398
  19.7 0.0 collective-permute-start.7
  19.7 0.5 %collective-permute-start.8 = (bf16[768,128]{1,0:T(8,128)(2,1)S(1)}, bf16[768,128]{1,0:T(8,128)(2,1)S(1)}, u32[]{:S(2)}, u32[]{:S(2)}) collective-permute-start(bf16[768,128]{1,0:T(8,128)(2,1)S(1)} %collective-permute-done.1.rest_2_), channel_id=1, source_target_pairs={{0,4},{4,0},{8,12},{12,8},{1,5},{5,1},{9,13},{13,9},{2,6},{6,2},{1... | collective-permute-start | bytes 589832 | tf_op jit(solution)/shard_map/ppermute | solution.py:392
  20.2 0.0 copy-done.5
  20.2 0.0 collective-permute-start.5
  20.2 0.9 %collective-permute-done.7.rest_3_ = bf16[768,128]{1,0:T(8,128)(2,1)S(1)} collective-permute-done((bf16[768,128]{1,0:T(8,128)(2,1)S(1)}, bf16[768,128]{1,0:T(8,128)(2,1)S(1)}, u32[]{:S(2)}, u32[]{:S(2)}) %collective-permute-start.7) | collective-permute-done | bytes 196640 | tf_op jit(solution)/shard_map/ppermute | solution.py:392
  21.1 0.3 collective-permute-done.8.rest_4_
  21.4 5.2 %attend.3 = (bf16[256,128]{1,0:T(8,128)(2,1)S(1)}, bf16[256,128]{1,0:T(8,128)(2,1)S(1)}, bf16[256,128]{1,0:T(8,128)(2,1)S(1)}, bf16[256,128]{1,0:T(8,128)(2,1)S(1)}) custom-call(bf16[2,1024,128]{2,1,0:T(8,128)(2,1)S(1)} %get-tuple-element.53.q_ref, f32[32,128]{1,0:T(8,128)S(1)} %get-tuple-element.51.bias_ref, f32[2,1024,128]{2,1,0:T(8,128)S(1)} %get-tuple-element.54.rest_0_, ...), custom_call_target="tpu_custom_call" | custom-call | tf_op jit(solution)/shard_map/attend/pallas_call | solution.py:308
  26.6 0.0 collective-permute-done.9
  26.6 0.0 collective-permute-done.6.rest_2_
  26.6 0.3 collective-permute-start.10
  27.0 1.6 %collective-permute-start.14 = (bf16[3,64,1024]{2,1,0:T(8,128)(2,1)S(1)}, bf16[3,64,1024]{2,1,0:T(8,128)(2,1)S(1)}, u32[]{:S(2)}, u32[]{:S(2)}) collective-permute-start(bf16[3,64,1024]{2,1,0:T(8,128)(2,1)S(1)} %constant_dynamic-update-slice_fusion), channel_id=1, source_target_pairs={{0,16},{16,0},{1,17},{17,1},{2,18},{18,2},{3,19},{19,3},{4,20},{20... | collective-permute-start | bytes 1179656 | tf_op jit(solution)/shard_map/ppermute | solution.py:419
  28.6 0.4 collective-permute-start.11
  29.0 2.2 %collective-permute-start.12 = (bf16[256,128]{1,0:T(8,128)(2,1)S(1)}, bf16[256,128]{1,0:T(8,128)(2,1)S(1)}, u32[]{:S(2)}, u32[]{:S(2)}) collective-permute-start(bf16[256,128]{1,0:T(8,128)(2,1)S(1)} %get-tuple-element.64), channel_id=1, source_target_pairs={{0,2},{1,3},{2,0},{3,1},{4,6},{5,7},{6,4},{7,5},{8,10},{9,11},{10,... | collective-permute-start | bytes 196616 | tf_op jit(solution)/shard_map/ppermute | solution.py:398
  31.2 0.0 collective-permute-done.5.rest_1_
  31.2 1.7 %collective-permute-start.13 = (bf16[256,128]{1,0:T(8,128)(2,1)S(1)}, bf16[256,128]{1,0:T(8,128)(2,1)S(1)}, u32[]{:S(2)}, u32[]{:S(2)}) collective-permute-start(bf16[256,128]{1,0:T(8,128)(2,1)S(1)} %get-tuple-element.65), channel_id=1, source_target_pairs={{0,3},{1,2},{2,1},{3,0},{4,7},{5,6},{6,5},{7,4},{8,11},{9,10},{10,... | collective-permute-start | bytes 196616 | tf_op jit(solution)/shard_map/ppermute | solution.py:398
  33.0 0.0 collective-permute-done.10.rest_3_
  33.0 6.5 %attend.4 = (bf16[256,128]{1,0:T(8,128)(2,1)S(1)}, bf16[256,128]{1,0:T(8,128)(2,1)S(1)}, bf16[256,128]{1,0:T(8,128)(2,1)S(1)}) custom-call(bf16[2,1024,128]{2,1,0:T(8,128)(2,1)S(1)} %get-tuple-element.50.q_ref, f32[32,128]{1,0:T(8,128)S(1)} %get-tuple-element.51.bias_ref, bf16[2,768,128]{2,1,0:T(8,128)(2,1)S(1)} %copy-done.5, ...), custom_call_target="tpu_custom_call" | custom-call | flops 2147483648 | tf_op jit(solution)/shard_map/attend/pallas_call | solution.py:308
  39.5 0.0 collective-permute-done.11.rest_4_
  39.5 0.0 collective-permute-done.12.rest_2_
  39.5 0.0 collective-permute-done.13.rest_6_
  39.5 0.0 collective-permute-done.14
  39.5 0.1 pad_maximum_fusion.rest_9_
  39.6 0.1 collective-permute-start.18
  39.7 1.2 %collective-permute-start.15 = (bf16[256,128]{1,0:T(8,128)(2,1)S(1)}, bf16[256,128]{1,0:T(8,128)(2,1)S(1)}, u32[]{:S(2)}, u32[]{:S(2)}) collective-permute-start(bf16[256,128]{1,0:T(8,128)(2,1)S(1)} %get-tuple-element.75), channel_id=1, source_target_pairs={{0,2},{1,3},{2,0},{3,1},{4,6},{5,7},{6,4},{7,5},{8,10},{9,11},{10,... | collective-permute-start | bytes 196616 | tf_op jit(solution)/shard_map/ppermute | solution.py:398
  40.9 1.5 %collective-permute-start.16 = (bf16[256,128]{1,0:T(8,128)(2,1)S(1)}, bf16[256,128]{1,0:T(8,128)(2,1)S(1)}, u32[]{:S(2)}, u32[]{:S(2)}) collective-permute-start(bf16[256,128]{1,0:T(8,128)(2,1)S(1)} %get-tuple-element.77), channel_id=1, source_target_pairs={{0,1},{1,0},{2,3},{3,2},{4,5},{5,4},{6,7},{7,6},{8,9},{9,8},{10,11... | collective-permute-start | bytes 196616 | tf_op jit(solution)/shard_map/ppermute | solution.py:398
  42.4 1.7 %collective-permute-start.17 = (bf16[256,128]{1,0:T(8,128)(2,1)S(1)}, bf16[256,128]{1,0:T(8,128)(2,1)S(1)}, u32[]{:S(2)}, u32[]{:S(2)}) collective-permute-start(bf16[256,128]{1,0:T(8,128)(2,1)S(1)} %get-tuple-element.79), channel_id=1, source_target_pairs={{0,3},{1,2},{2,1},{3,0},{4,7},{5,6},{6,5},{7,4},{8,11},{9,10},{10,... | collective-permute-start | bytes 196616 | tf_op jit(solution)/shard_map/ppermute | solution.py:398
  44.1 3.4 %attend.5.rest_1_ = bf16[256,128]{1,0:T(8,128)(2,1)S(1)} custom-call(bf16[2,1024,128]{2,1,0:T(8,128)(2,1)S(1)} %get-tuple-element.50.q_ref, f32[32,128]{1,0:T(8,128)S(1)} %get-tuple-element.51.bias_ref, bf16[2,768,128]{2,1,0:T(8,128)(2,1)S(1)} %copy-done.5, bf16[2,768,128]{2,1,0:T(8,128)(2,1)S(1)} %collective-permute-done.5.rest_1_, ...), custom_call_target="tpu_custom_call" | custom-call | flops 8589934592 | tf_op jit(solution)/shard_map/attend/pallas_call | solution.py:308
  47.6 0.0 collective-permute-done.15.rest_3_
  47.6 0.0 collective-permute-done.16.rest_5_
  47.6 0.9 %collective-permute-done.17.rest_7_ = bf16[256,128]{1,0:T(8,128)(2,1)S(1)} collective-permute-done((bf16[256,128]{1,0:T(8,128)(2,1)S(1)}, bf16[256,128]{1,0:T(8,128)(2,1)S(1)}, u32[]{:S(2)}, u32[]{:S(2)}) %collective-permute-start.17) | collective-permute-done | bytes 65568 | tf_op jit(solution)/shard_map/ppermute | solution.py:398
  48.5 0.0 collective-permute-done.18.rest_10_
  48.5 1.7 %project_out.1 = bf16[256,1024]{1,0:T(8,128)(2,1)} custom-call(bf16[256,128]{1,0:T(8,128)(2,1)S(1)} %get-tuple-element.70.rest_0_, bf16[256,128]{1,0:T(8,128)(2,1)S(1)} %attend.5.rest_1_, bf16[256,128]{1,0:T(8,128)(2,1)S(1)} %collective-permute-done.12.rest_2_, bf16[256,128]{1,0:T(8,128)(2,1)S(1)} %collective-permute-done.15.rest_3_, ...), custom_call_target="tpu_custom_call" | custom-call | tf_op jit(solution)/shard_map/project_out/pallas_call | solution.py:375
  (13 shorter events, 0.1 us)
Async XLA Ops:
  0.0 11.7 %copy-start.4 = (s32[32,32]{1,0:T(8,128)S(1)}, s32[32,32]{1,0:T(8,128)}, u32[]{:S(2)}) copy-start(s32[32,32]{1,0:T(8,128)} %mask_ref.1) | copy-start | bytes 12292
  0.0 11.7 %copy-start = (bf16[1024,1024]{1,0:T(8,128)(2,1)S(1)}, bf16[1024,1024]{1,0:T(8,128)(2,1)}, u32[]{:S(2)}) copy-start(bf16[1024,1024]{1,0:T(8,128)(2,1)} %tok.1) | copy-start | bytes 6291460
  0.0 7.2 %copy-start.1 = (bf16[256,1024]{1,0:T(8,128)(2,1)S(1)}, bf16[256,1024]{1,0:T(8,128)(2,1)}, u32[]{:S(2)}) copy-start(bf16[256,1024]{1,0:T(8,128)(2,1)} %rest_8_.1) | copy-start | bytes 1572868
  0.0 11.7 %copy-start.2 = (bf16[1024,256]{1,0:T(8,128)(2,1)S(1)}, bf16[1024,256]{1,0:T(8,128)(2,1)}, u32[]{:S(2)}) copy-start(bf16[1024,256]{1,0:T(8,128)(2,1)} %w_any.1) | copy-start | bytes 1572868
  3.7 6.5 %collective-permute-start.2 = (bf16[768,128]{1,0:T(8,128)(2,1)}, bf16[768,128]{1,0:T(8,128)(2,1)}, u32[]{:S(2)}, u32[]{:S(2)}) collective-permute-start(bf16[768,128]{1,0:T(8,128)(2,1)} %get-tuple-element.43), channel_id=1, source_target_pairs={{0,4},{4,0},{8,12},{12,8},{1,5},{5,1},{9,13},{13,9},{2,6},{6,2},{1... | collective-permute-start | bytes 589832 | tf_op jit(solution)/shard_map/ppermute | solution.py:392
  4.2 13.7 %collective-permute-start = (bf16[768,128]{1,0:T(8,128)(2,1)}, bf16[768,128]{1,0:T(8,128)(2,1)S(1)}, u32[]{:S(2)}, u32[]{:S(2)}) collective-permute-start(bf16[768,128]{1,0:T(8,128)(2,1)} %get-tuple-element.43), channel_id=1, source_target_pairs={{0,8},{4,12},{8,0},{12,4},{1,9},{5,13},{9,1},{13,5},{2,10},{6,14},... | collective-permute-start | bytes 589832 | tf_op jit(solution)/shard_map/ppermute | solution.py:392
  6.8 4.9 %collective-permute-start.3 = (bf16[768,128]{1,0:T(8,128)(2,1)}, bf16[768,128]{1,0:T(8,128)(2,1)}, u32[]{:S(2)}, u32[]{:S(2)}) collective-permute-start(bf16[768,128]{1,0:T(8,128)(2,1)} %get-tuple-element.44), channel_id=1, source_target_pairs={{0,4},{4,0},{8,12},{12,8},{1,5},{5,1},{9,13},{13,9},{2,6},{6,2},{1... | collective-permute-start | bytes 589832 | tf_op jit(solution)/shard_map/ppermute | solution.py:392
  7.0 11.0 %collective-permute-start.1 = (bf16[768,128]{1,0:T(8,128)(2,1)}, bf16[768,128]{1,0:T(8,128)(2,1)S(1)}, u32[]{:S(2)}, u32[]{:S(2)}) collective-permute-start(bf16[768,128]{1,0:T(8,128)(2,1)} %get-tuple-element.44), channel_id=1, source_target_pairs={{0,8},{4,12},{8,0},{12,4},{1,9},{5,13},{9,1},{13,5},{2,10},{6,14},... | collective-permute-start | bytes 589832 | tf_op jit(solution)/shard_map/ppermute | solution.py:392
  7.3 10.7 %collective-permute-start.4 = (bf16[1,64,1024]{2,1,0:T(8,128)(2,1)S(1)}, bf16[1,64,1024]{2,1,0:T(8,128)(2,1)S(1)}, u32[]{:S(2)}, u32[]{:S(2)}) collective-permute-start(bf16[1,64,1024]{2,1,0:T(8,128)(2,1)S(1)} %bitcast.1), channel_id=1, source_target_pairs={{0,2},{1,3},{2,0},{3,1},{4,6},{5,7},{6,4},{7,5},{8,10},{9,11},{10,... | collective-permute-start | bytes 393224 | tf_op jit(solution)/shard_map/ppermute | solution.py:398
  10.2 16.5 %collective-permute-start.6 = (bf16[2,768,128]{2,1,0:T(8,128)(2,1)}, bf16[2,768,128]{2,1,0:T(8,128)(2,1)S(1)}, u32[]{:S(2)}, u32[]{:S(2)}) collective-permute-start(bf16[2,768,128]{2,1,0:T(8,128)(2,1)} %get-tuple-element.52.rest_0_), channel_id=1, source_target_pairs={{0,8},{4,12},{8,0},{12,4},{1,9},{5,13},{9,1},{13,5},{2,10},{6,14},... | collective-permute-start | bytes 1179656 | tf_op jit(solution)/shard_map/ppermute | solution.py:392
  11.7 1.0 %copy-start.3 = (bf16[2,768,128]{2,1,0:T(8,128)(2,1)S(1)}, bf16[2,768,128]{2,1,0:T(8,128)(2,1)}, u32[]{:S(2)}) copy-start(bf16[2,768,128]{2,1,0:T(8,128)(2,1)} %get-tuple-element.45.rest_0_) | copy-start | bytes 1179652
  12.7 7.5 %copy-start.5 = (bf16[2,768,128]{2,1,0:T(8,128)(2,1)S(1)}, bf16[2,768,128]{2,1,0:T(8,128)(2,1)}, u32[]{:S(2)}) copy-start(bf16[2,768,128]{2,1,0:T(8,128)(2,1)} %get-tuple-element.52.rest_0_) | copy-start | bytes 1179652
  18.0 8.6 %collective-permute-start.9 = (bf16[2,64,1024]{2,1,0:T(8,128)(2,1)S(1)}, bf16[2,64,1024]{2,1,0:T(8,128)(2,1)S(1)}, u32[]{:S(2)}, u32[]{:S(2)}) collective-permute-start(bf16[2,64,1024]{2,1,0:T(8,128)(2,1)S(1)} %pad_maximum_fusion.1), channel_id=1, source_target_pairs={{0,1},{1,0},{2,3},{3,2},{4,5},{5,4},{6,7},{7,6},{8,9},{9,8},{10,11... | collective-permute-start | bytes 786440 | tf_op jit(solution)/shard_map/ppermute | solution.py:398
  19.7 1.4 %collective-permute-start.7 = (bf16[768,128]{1,0:T(8,128)(2,1)S(1)}, bf16[768,128]{1,0:T(8,128)(2,1)S(1)}, u32[]{:S(2)}, u32[]{:S(2)}) collective-permute-start(bf16[768,128]{1,0:T(8,128)(2,1)S(1)} %collective-permute-done.rest_1_), channel_id=1, source_target_pairs={{0,4},{4,0},{8,12},{12,8},{1,5},{5,1},{9,13},{13,9},{2,6},{6,2},{1... | collective-permute-start | bytes 589832 | tf_op jit(solution)/shard_map/ppermute | solution.py:392
  19.7 1.7 %collective-permute-start.8 = (bf16[768,128]{1,0:T(8,128)(2,1)S(1)}, bf16[768,128]{1,0:T(8,128)(2,1)S(1)}, u32[]{:S(2)}, u32[]{:S(2)}) collective-permute-start(bf16[768,128]{1,0:T(8,128)(2,1)S(1)} %collective-permute-done.1.rest_2_), channel_id=1, source_target_pairs={{0,4},{4,0},{8,12},{12,8},{1,5},{5,1},{9,13},{13,9},{2,6},{6,2},{1... | collective-permute-start | bytes 589832 | tf_op jit(solution)/shard_map/ppermute | solution.py:392
  20.2 11.0 %collective-permute-start.5 = (bf16[2,768,128]{2,1,0:T(8,128)(2,1)S(1)}, bf16[2,768,128]{2,1,0:T(8,128)(2,1)S(1)}, u32[]{:S(2)}, u32[]{:S(2)}) collective-permute-start(bf16[2,768,128]{2,1,0:T(8,128)(2,1)S(1)} %copy-done.5), channel_id=1, source_target_pairs={{0,4},{4,0},{8,12},{12,8},{1,5},{5,1},{9,13},{13,9},{2,6},{6,2},{1... | collective-permute-start | bytes 1179656 | tf_op jit(solution)/shard_map/ppermute | solution.py:392
  26.6 6.3 %collective-permute-start.10 = (bf16[2,768,128]{2,1,0:T(8,128)(2,1)S(1)}, bf16[2,768,128]{2,1,0:T(8,128)(2,1)S(1)}, u32[]{:S(2)}, u32[]{:S(2)}) collective-permute-start(bf16[2,768,128]{2,1,0:T(8,128)(2,1)S(1)} %collective-permute-done.6.rest_2_), channel_id=1, source_target_pairs={{0,4},{4,0},{8,12},{12,8},{1,5},{5,1},{9,13},{13,9},{2,6},{6,2},{1... | collective-permute-start | bytes 1179656 | tf_op jit(solution)/shard_map/ppermute | solution.py:392
  27.0 12.5 %collective-permute-start.14 = (bf16[3,64,1024]{2,1,0:T(8,128)(2,1)S(1)}, bf16[3,64,1024]{2,1,0:T(8,128)(2,1)S(1)}, u32[]{:S(2)}, u32[]{:S(2)}) collective-permute-start(bf16[3,64,1024]{2,1,0:T(8,128)(2,1)S(1)} %constant_dynamic-update-slice_fusion), channel_id=1, source_target_pairs={{0,16},{16,0},{1,17},{17,1},{2,18},{18,2},{3,19},{19,3},{4,20},{20... | collective-permute-start | bytes 1179656 | tf_op jit(solution)/shard_map/ppermute | solution.py:419
  28.6 10.9 %collective-permute-start.11 = (bf16[256,128]{1,0:T(8,128)(2,1)S(1)}, bf16[256,128]{1,0:T(8,128)(2,1)S(1)}, u32[]{:S(2)}, u32[]{:S(2)}) collective-permute-start(bf16[256,128]{1,0:T(8,128)(2,1)S(1)} %get-tuple-element.63), channel_id=1, source_target_pairs={{0,1},{1,0},{2,3},{3,2},{4,5},{5,4},{6,7},{7,6},{8,9},{9,8},{10,11... | collective-permute-start | bytes 196616 | tf_op jit(solution)/shard_map/ppermute | solution.py:398
  29.0 10.5 %collective-permute-start.12 = (bf16[256,128]{1,0:T(8,128)(2,1)S(1)}, bf16[256,128]{1,0:T(8,128)(2,1)S(1)}, u32[]{:S(2)}, u32[]{:S(2)}) collective-permute-start(bf16[256,128]{1,0:T(8,128)(2,1)S(1)} %get-tuple-element.64), channel_id=1, source_target_pairs={{0,2},{1,3},{2,0},{3,1},{4,6},{5,7},{6,4},{7,5},{8,10},{9,11},{10,... | collective-permute-start | bytes 196616 | tf_op jit(solution)/shard_map/ppermute | solution.py:398
  31.2 8.3 %collective-permute-start.13 = (bf16[256,128]{1,0:T(8,128)(2,1)S(1)}, bf16[256,128]{1,0:T(8,128)(2,1)S(1)}, u32[]{:S(2)}, u32[]{:S(2)}) collective-permute-start(bf16[256,128]{1,0:T(8,128)(2,1)S(1)} %get-tuple-element.65), channel_id=1, source_target_pairs={{0,3},{1,2},{2,1},{3,0},{4,7},{5,6},{6,5},{7,4},{8,11},{9,10},{10,... | collective-permute-start | bytes 196616 | tf_op jit(solution)/shard_map/ppermute | solution.py:398
  39.6 8.9 %collective-permute-start.18 = (bf16[3,128,1024]{2,1,0:T(8,128)(2,1)S(1)}, bf16[3,128,1024]{2,1,0:T(8,128)(2,1)S(1)}, u32[]{:S(2)}, u32[]{:S(2)}) collective-permute-start(bf16[3,128,1024]{2,1,0:T(8,128)(2,1)S(1)} %pad_maximum_fusion.rest_9_), channel_id=1, source_target_pairs={{0,4},{4,0},{8,12},{12,8},{1,5},{5,1},{9,13},{13,9},{2,6},{6,2},{1... | collective-permute-start | bytes 2359304 | tf_op jit(solution)/shard_map/ppermute | solution.py:392
  39.7 7.9 %collective-permute-start.15 = (bf16[256,128]{1,0:T(8,128)(2,1)S(1)}, bf16[256,128]{1,0:T(8,128)(2,1)S(1)}, u32[]{:S(2)}, u32[]{:S(2)}) collective-permute-start(bf16[256,128]{1,0:T(8,128)(2,1)S(1)} %get-tuple-element.75), channel_id=1, source_target_pairs={{0,2},{1,3},{2,0},{3,1},{4,6},{5,7},{6,4},{7,5},{8,10},{9,11},{10,... | collective-permute-start | bytes 196616 | tf_op jit(solution)/shard_map/ppermute | solution.py:398
  40.9 6.7 %collective-permute-start.16 = (bf16[256,128]{1,0:T(8,128)(2,1)S(1)}, bf16[256,128]{1,0:T(8,128)(2,1)S(1)}, u32[]{:S(2)}, u32[]{:S(2)}) collective-permute-start(bf16[256,128]{1,0:T(8,128)(2,1)S(1)} %get-tuple-element.77), channel_id=1, source_target_pairs={{0,1},{1,0},{2,3},{3,2},{4,5},{5,4},{6,7},{7,6},{8,9},{9,8},{10,11... | collective-permute-start | bytes 196616 | tf_op jit(solution)/shard_map/ppermute | solution.py:398
  42.4 6.1 %collective-permute-start.17 = (bf16[256,128]{1,0:T(8,128)(2,1)S(1)}, bf16[256,128]{1,0:T(8,128)(2,1)S(1)}, u32[]{:S(2)}, u32[]{:S(2)}) collective-permute-start(bf16[256,128]{1,0:T(8,128)(2,1)S(1)} %get-tuple-element.79), channel_id=1, source_target_pairs={{0,3},{1,2},{2,1},{3,0},{4,7},{5,6},{6,5},{7,4},{8,11},{9,10},{10,... | collective-permute-start | bytes 196616 | tf_op jit(solution)/shard_map/ppermute | solution.py:398

commit v7 on v6

--- a/solution.py
+++ b/solution.py
@@ -448,7 +448,7 @@
             sources += arrays + [to_sibling(one) for one in arrays]
         held, first = (state, 2) if p == 0 else (None, 0)
         if p < last:
-            pieces = attend(queries[p], held, sources, bias, first, heads, 0, heads, 0)
+            pieces = attend(queries[p], held, sources, bias, first, heads, 0, heads, 2**29)
             if p == 0:
                 pieces, arriving = lax.optimization_barrier((pieces, arriving))
                 w_mine = jnp.concatenate([w_mine, arriving])[1:]

time: 50.4 us -> 50.4 us (level)
  no operation moved by 1% of the time
where the time goes in v7:
time: 50.4 us; the launch traced here: 50.2 us
  Pallas kernels  25.8 us (51%)
  starting transfers between devices  20.9 us (41%)
  waiting for transfers between devices  2.18 us (4%)
  local copies, waits for them, and re-layouts  1.05 us (2%)
    pallas_call x3, Pallas kernels, attend(): pl.pallas_call(kernel, out_shape=[jax.ShapeDtypeStruct((part, LANES), jnp...  15.2 us
    ppermute x8, starting transfers between devices, along_head(): return lax.ppermute(array, 'head', [(i, i ^ k) for i in range(heads)])  13.4 us
    ppermute x10, starting transfers between devices, along_band(): return lax.ppermute(array, 'band', [(i, goes_to(i)) for i in range(bands)])  5.91 us
    pallas_call x1, Pallas kernels, begin_attention(): pl.pallas_call(kernel, out_shape=[jax.ShapeDtypeStruct((2, rows, LANES),...  5.25 us
    pallas_call x1, Pallas kernels, project_kv(): pl.pallas_call(kernel, out_shape=[jax.ShapeDtypeStruct((rows, LANES), jnp...  3.69 us
    pallas_call x1, Pallas kernels, project_out(): pl.pallas_call(kernel, out_shape=jax.ShapeDtypeStruct((rows, width), jnp....  1.72 us
    ppermute x1, starting transfers between devices, other_tiles(): lax.ppermute(array, 'tiles', [(i, i ^ s) for i in range(tiles)])  1.58 us
    ppermute x10, waiting for transfers between devices, along_band(): return lax.ppermute(array, 'band', [(i, goes_to(i)) for i in range(bands)])  1.23 us
  transfers between devices with their start and end apart: 19, of which 3 were waited for; matrix products, arithmetic and copies ran while one was open for 0% of the time, Pallas kernels for 41%

profile of v7, /device:TPU:0, one launch (start us, length us, event | category | flops | bytes accessed | tf_op | source)
XLA Modules:
  0.0 50.2 jit_solution(8108397041032833331)
XLA Ops:
  0.0 3.7 %project_kv.1 = (bf16[768,128]{1,0:T(8,128)(2,1)}, bf16[768,128]{1,0:T(8,128)(2,1)}, bf16[2,768,128]{2,1,0:T(8,128)(2,1)}, bf16[2,768,128]{2,1,0:T(8,128)(2,1)}) custom-call(s32[32,32]{1,0:T(8,128)} %mask_ref.1, bf16[1024,1024]{1,0:T(8,128)(2,1)} %tok.1, bf16[1024,256]{1,0:T(8,128)(2,1)} %wk_ref.1, bf16[1024,256]{1,0:T(8,128)(2,1)} %wv_ref.1), custom_call_target="tpu_custom_call" | custom-call | tf_op jit(solution)/shard_map/project_kv/pallas_call | solution.py:115
  3.7 0.5 %collective-permute-start.2 = (bf16[768,128]{1,0:T(8,128)(2,1)}, bf16[768,128]{1,0:T(8,128)(2,1)}, u32[]{:S(2)}, u32[]{:S(2)}) collective-permute-start(bf16[768,128]{1,0:T(8,128)(2,1)} %get-tuple-element.43), channel_id=1, source_target_pairs={{0,4},{4,0},{8,12},{12,8},{1,5},{5,1},{9,13},{13,9},{2,6},{6,2},{1... | collective-permute-start | bytes 589832 | tf_op jit(solution)/shard_map/ppermute | solution.py:392
  4.2 2.6 %collective-permute-start = (bf16[768,128]{1,0:T(8,128)(2,1)}, bf16[768,128]{1,0:T(8,128)(2,1)S(1)}, u32[]{:S(2)}, u32[]{:S(2)}) collective-permute-start(bf16[768,128]{1,0:T(8,128)(2,1)} %get-tuple-element.43), channel_id=1, source_target_pairs={{0,8},{4,12},{8,0},{12,4},{1,9},{5,13},{9,1},{13,5},{2,10},{6,14},... | collective-permute-start | bytes 589832 | tf_op jit(solution)/shard_map/ppermute | solution.py:392
  6.8 0.2 collective-permute-start.3
  7.0 0.3 collective-permute-start.1
  7.2 0.0 copy-done.1
  7.3 2.9 %collective-permute-start.4 = (bf16[1,64,1024]{2,1,0:T(8,128)(2,1)S(1)}, bf16[1,64,1024]{2,1,0:T(8,128)(2,1)S(1)}, u32[]{:S(2)}, u32[]{:S(2)}) collective-permute-start(bf16[1,64,1024]{2,1,0:T(8,128)(2,1)S(1)} %bitcast.1), channel_id=1, source_target_pairs={{0,2},{1,3},{2,0},{3,1},{4,6},{5,7},{6,4},{7,5},{8,10},{9,11},{10,... | collective-permute-start | bytes 393224 | tf_op jit(solution)/shard_map/ppermute | solution.py:398
  10.2 0.0 collective-permute-done.2.rest_1_
  10.2 1.5 %collective-permute-start.6 = (bf16[2,768,128]{2,1,0:T(8,128)(2,1)}, bf16[2,768,128]{2,1,0:T(8,128)(2,1)S(1)}, u32[]{:S(2)}, u32[]{:S(2)}) collective-permute-start(bf16[2,768,128]{2,1,0:T(8,128)(2,1)} %get-tuple-element.52.rest_0_), channel_id=1, source_target_pairs={{0,8},{4,12},{8,0},{12,4},{1,9},{5,13},{9,1},{13,5},{2,10},{6,14},... | collective-permute-start | bytes 1179656 | tf_op jit(solution)/shard_map/ppermute | solution.py:392
  11.7 0.0 collective-permute-done.3.rest_2_
  11.7 1.0 %copy-done.3 = bf16[2,768,128]{2,1,0:T(8,128)(2,1)S(1)} copy-done((bf16[2,768,128]{2,1,0:T(8,128)(2,1)S(1)}, bf16[2,768,128]{2,1,0:T(8,128)(2,1)}, u32[]{:S(2)}) %copy-start.3) | copy-done | bytes 393240
  12.7 5.2 %begin_attention.1 = (bf16[2,1024,128]{2,1,0:T(8,128)(2,1)S(1)}, bf16[2,1024,128]{2,1,0:T(8,128)(2,1)S(1)}, f32[32,128]{1,0:T(8,128)S(1)}, f32[2,1024,128]{2,1,0:T(8,128)S(1)}) custom-call(s32[32,32]{1,0:T(8,128)S(1)} %copy-done.4, bf16[1024,1024]{1,0:T(8,128)(2,1)S(1)} %copy-done, bf16[1024,256]{1,0:T(8,128)(2,1)S(1)} %copy-done.2, ...), custom_call_target="tpu_custom_call" | custom-call | tf_op jit(solution)/shard_map/begin_attention/pallas_call | solution.py:257
  18.0 0.0 collective-permute-done.4
  18.0 0.0 collective-permute-done.rest_1_
  18.0 0.0 collective-permute-done.1.rest_2_
  18.0 1.6 %collective-permute-start.9 = (bf16[2,64,1024]{2,1,0:T(8,128)(2,1)S(1)}, bf16[2,64,1024]{2,1,0:T(8,128)(2,1)S(1)}, u32[]{:S(2)}, u32[]{:S(2)}) collective-permute-start(bf16[2,64,1024]{2,1,0:T(8,128)(2,1)S(1)} %pad_maximum_fusion.1), channel_id=1, source_target_pairs={{0,1},{1,0},{2,3},{3,2},{4,5},{5,4},{6,7},{7,6},{8,9},{9,8},{10,11... | collective-permute-start | bytes 786440 | tf_op jit(solution)/shard_map/ppermute | solution.py:398
  19.7 0.0 collective-permute-start.7
  19.7 0.5 %collective-permute-start.8 = (bf16[768,128]{1,0:T(8,128)(2,1)S(1)}, bf16[768,128]{1,0:T(8,128)(2,1)S(1)}, u32[]{:S(2)}, u32[]{:S(2)}) collective-permute-start(bf16[768,128]{1,0:T(8,128)(2,1)S(1)} %collective-permute-done.1.rest_2_), channel_id=1, source_target_pairs={{0,4},{4,0},{8,12},{12,8},{1,5},{5,1},{9,13},{13,9},{2,6},{6,2},{1... | collective-permute-start | bytes 589832 | tf_op jit(solution)/shard_map/ppermute | solution.py:392
  20.2 0.0 copy-done.5
  20.2 0.0 collective-permute-start.5
  20.2 0.9 %collective-permute-done.7.rest_3_ = bf16[768,128]{1,0:T(8,128)(2,1)S(1)} collective-permute-done((bf16[768,128]{1,0:T(8,128)(2,1)S(1)}, bf16[768,128]{1,0:T(8,128)(2,1)S(1)}, u32[]{:S(2)}, u32[]{:S(2)}) %collective-permute-start.7) | collective-permute-done | bytes 196640 | tf_op jit(solution)/shard_map/ppermute | solution.py:392
  21.1 0.3 collective-permute-done.8.rest_4_
  21.4 5.2 %attend.3 = (bf16[256,128]{1,0:T(8,128)(2,1)S(1)}, bf16[256,128]{1,0:T(8,128)(2,1)S(1)}, bf16[256,128]{1,0:T(8,128)(2,1)S(1)}, bf16[256,128]{1,0:T(8,128)(2,1)S(1)}) custom-call(bf16[2,1024,128]{2,1,0:T(8,128)(2,1)S(1)} %get-tuple-element.53.q_ref, f32[32,128]{1,0:T(8,128)S(1)} %get-tuple-element.51.bias_ref, f32[2,1024,128]{2,1,0:T(8,128)S(1)} %get-tuple-element.54.rest_0_, ...), custom_call_target="tpu_custom_call" | custom-call | flops 536870912 | tf_op jit(solution)/shard_map/attend/pallas_call | solution.py:308
  26.6 0.0 collective-permute-done.9
  26.6 0.0 collective-permute-done.6.rest_2_
  26.6 0.3 collective-permute-start.10
  27.0 1.6 %collective-permute-start.14 = (bf16[3,64,1024]{2,1,0:T(8,128)(2,1)S(1)}, bf16[3,64,1024]{2,1,0:T(8,128)(2,1)S(1)}, u32[]{:S(2)}, u32[]{:S(2)}) collective-permute-start(bf16[3,64,1024]{2,1,0:T(8,128)(2,1)S(1)} %constant_dynamic-update-slice_fusion), channel_id=1, source_target_pairs={{0,16},{16,0},{1,17},{17,1},{2,18},{18,2},{3,19},{19,3},{4,20},{20... | collective-permute-start | bytes 1179656 | tf_op jit(solution)/shard_map/ppermute | solution.py:419
  28.6 0.4 collective-permute-start.11
  29.0 2.2 %collective-permute-start.12 = (bf16[256,128]{1,0:T(8,128)(2,1)S(1)}, bf16[256,128]{1,0:T(8,128)(2,1)S(1)}, u32[]{:S(2)}, u32[]{:S(2)}) collective-permute-start(bf16[256,128]{1,0:T(8,128)(2,1)S(1)} %get-tuple-element.64), channel_id=1, source_target_pairs={{0,2},{1,3},{2,0},{3,1},{4,6},{5,7},{6,4},{7,5},{8,10},{9,11},{10,... | collective-permute-start | bytes 196616 | tf_op jit(solution)/shard_map/ppermute | solution.py:398
  31.2 0.0 collective-permute-done.5.rest_1_
  31.2 1.7 %collective-permute-start.13 = (bf16[256,128]{1,0:T(8,128)(2,1)S(1)}, bf16[256,128]{1,0:T(8,128)(2,1)S(1)}, u32[]{:S(2)}, u32[]{:S(2)}) collective-permute-start(bf16[256,128]{1,0:T(8,128)(2,1)S(1)} %get-tuple-element.65), channel_id=1, source_target_pairs={{0,3},{1,2},{2,1},{3,0},{4,7},{5,6},{6,5},{7,4},{8,11},{9,10},{10,... | collective-permute-start | bytes 196616 | tf_op jit(solution)/shard_map/ppermute | solution.py:398
  33.0 0.0 collective-permute-done.10.rest_3_
  33.0 6.5 %attend.4 = (bf16[256,128]{1,0:T(8,128)(2,1)S(1)}, bf16[256,128]{1,0:T(8,128)(2,1)S(1)}, bf16[256,128]{1,0:T(8,128)(2,1)S(1)}) custom-call(bf16[2,1024,128]{2,1,0:T(8,128)(2,1)S(1)} %get-tuple-element.50.q_ref, f32[32,128]{1,0:T(8,128)S(1)} %get-tuple-element.51.bias_ref, bf16[2,768,128]{2,1,0:T(8,128)(2,1)S(1)} %copy-done.5, ...), custom_call_target="tpu_custom_call" | custom-call | flops 2147483648 | tf_op jit(solution)/shard_map/attend/pallas_call | solution.py:308
  39.5 0.0 collective-permute-done.11.rest_4_
  39.5 0.0 collective-permute-done.12.rest_2_
  39.5 0.0 collective-permute-done.13.rest_6_
  39.5 0.0 collective-permute-done.14
  39.5 0.1 pad_maximum_fusion.rest_9_
  39.6 0.1 collective-permute-start.18
  39.7 1.2 %collective-permute-start.15 = (bf16[256,128]{1,0:T(8,128)(2,1)S(1)}, bf16[256,128]{1,0:T(8,128)(2,1)S(1)}, u32[]{:S(2)}, u32[]{:S(2)}) collective-permute-start(bf16[256,128]{1,0:T(8,128)(2,1)S(1)} %get-tuple-element.75), channel_id=1, source_target_pairs={{0,2},{1,3},{2,0},{3,1},{4,6},{5,7},{6,4},{7,5},{8,10},{9,11},{10,... | collective-permute-start | bytes 196616 | tf_op jit(solution)/shard_map/ppermute | solution.py:398
  40.9 1.5 %collective-permute-start.16 = (bf16[256,128]{1,0:T(8,128)(2,1)S(1)}, bf16[256,128]{1,0:T(8,128)(2,1)S(1)}, u32[]{:S(2)}, u32[]{:S(2)}) collective-permute-start(bf16[256,128]{1,0:T(8,128)(2,1)S(1)} %get-tuple-element.77), channel_id=1, source_target_pairs={{0,1},{1,0},{2,3},{3,2},{4,5},{5,4},{6,7},{7,6},{8,9},{9,8},{10,11... | collective-permute-start | bytes 196616 | tf_op jit(solution)/shard_map/ppermute | solution.py:398
  42.4 1.7 %collective-permute-start.17 = (bf16[256,128]{1,0:T(8,128)(2,1)S(1)}, bf16[256,128]{1,0:T(8,128)(2,1)S(1)}, u32[]{:S(2)}, u32[]{:S(2)}) collective-permute-start(bf16[256,128]{1,0:T(8,128)(2,1)S(1)} %get-tuple-element.79), channel_id=1, source_target_pairs={{0,3},{1,2},{2,1},{3,0},{4,7},{5,6},{6,5},{7,4},{8,11},{9,10},{10,... | collective-permute-start | bytes 196616 | tf_op jit(solution)/shard_map/ppermute | solution.py:398
  44.1 3.4 %attend.5.rest_1_ = bf16[256,128]{1,0:T(8,128)(2,1)S(1)} custom-call(bf16[2,1024,128]{2,1,0:T(8,128)(2,1)S(1)} %get-tuple-element.50.q_ref, f32[32,128]{1,0:T(8,128)S(1)} %get-tuple-element.51.bias_ref, bf16[2,768,128]{2,1,0:T(8,128)(2,1)S(1)} %copy-done.5, bf16[2,768,128]{2,1,0:T(8,128)(2,1)S(1)} %collective-permute-done.5.rest_1_, ...), custom_call_target="tpu_custom_call" | custom-call | flops 8589934592 | tf_op jit(solution)/shard_map/attend/pallas_call | solution.py:308
  47.6 0.0 collective-permute-done.15.rest_3_
  47.6 0.0 collective-permute-done.16.rest_5_
  47.6 0.9 %collective-permute-done.17.rest_7_ = bf16[256,128]{1,0:T(8,128)(2,1)S(1)} collective-permute-done((bf16[256,128]{1,0:T(8,128)(2,1)S(1)}, bf16[256,128]{1,0:T(8,128)(2,1)S(1)}, u32[]{:S(2)}, u32[]{:S(2)}) %collective-permute-start.17) | collective-permute-done | bytes 65568 | tf_op jit(solution)/shard_map/ppermute | solution.py:398
  48.5 0.0 collective-permute-done.18.rest_10_
  48.5 1.7 %project_out.1 = bf16[256,1024]{1,0:T(8,128)(2,1)} custom-call(bf16[256,128]{1,0:T(8,128)(2,1)S(1)} %get-tuple-element.70.rest_0_, bf16[256,128]{1,0:T(8,128)(2,1)S(1)} %attend.5.rest_1_, bf16[256,128]{1,0:T(8,128)(2,1)S(1)} %collective-permute-done.12.rest_2_, bf16[256,128]{1,0:T(8,128)(2,1)S(1)} %collective-permute-done.15.rest_3_, ...), custom_call_target="tpu_custom_call" | custom-call | tf_op jit(solution)/shard_map/project_out/pallas_call | solution.py:375
  (13 shorter events, 0.1 us)
Async XLA Ops:
  0.0 11.7 %copy-start.4 = (s32[32,32]{1,0:T(8,128)S(1)}, s32[32,32]{1,0:T(8,128)}, u32[]{:S(2)}) copy-start(s32[32,32]{1,0:T(8,128)} %mask_ref.1) | copy-start | bytes 12292
  0.0 11.7 %copy-start = (bf16[1024,1024]{1,0:T(8,128)(2,1)S(1)}, bf16[1024,1024]{1,0:T(8,128)(2,1)}, u32[]{:S(2)}) copy-start(bf16[1024,1024]{1,0:T(8,128)(2,1)} %tok.1) | copy-start | bytes 6291460
  0.0 7.2 %copy-start.1 = (bf16[256,1024]{1,0:T(8,128)(2,1)S(1)}, bf16[256,1024]{1,0:T(8,128)(2,1)}, u32[]{:S(2)}) copy-start(bf16[256,1024]{1,0:T(8,128)(2,1)} %rest_8_.1) | copy-start | bytes 1572868
  0.0 11.7 %copy-start.2 = (bf16[1024,256]{1,0:T(8,128)(2,1)S(1)}, bf16[1024,256]{1,0:T(8,128)(2,1)}, u32[]{:S(2)}) copy-start(bf16[1024,256]{1,0:T(8,128)(2,1)} %w_any.1) | copy-start | bytes 1572868
  3.7 6.5 %collective-permute-start.2 = (bf16[768,128]{1,0:T(8,128)(2,1)}, bf16[768,128]{1,0:T(8,128)(2,1)}, u32[]{:S(2)}, u32[]{:S(2)}) collective-permute-start(bf16[768,128]{1,0:T(8,128)(2,1)} %get-tuple-element.43), channel_id=1, source_target_pairs={{0,4},{4,0},{8,12},{12,8},{1,5},{5,1},{9,13},{13,9},{2,6},{6,2},{1... | collective-permute-start | bytes 589832 | tf_op jit(solution)/shard_map/ppermute | solution.py:392
  4.2 13.7 %collective-permute-start = (bf16[768,128]{1,0:T(8,128)(2,1)}, bf16[768,128]{1,0:T(8,128)(2,1)S(1)}, u32[]{:S(2)}, u32[]{:S(2)}) collective-permute-start(bf16[768,128]{1,0:T(8,128)(2,1)} %get-tuple-element.43), channel_id=1, source_target_pairs={{0,8},{4,12},{8,0},{12,4},{1,9},{5,13},{9,1},{13,5},{2,10},{6,14},... | collective-permute-start | bytes 589832 | tf_op jit(solution)/shard_map/ppermute | solution.py:392
  6.8 4.9 %collective-permute-start.3 = (bf16[768,128]{1,0:T(8,128)(2,1)}, bf16[768,128]{1,0:T(8,128)(2,1)}, u32[]{:S(2)}, u32[]{:S(2)}) collective-permute-start(bf16[768,128]{1,0:T(8,128)(2,1)} %get-tuple-element.44), channel_id=1, source_target_pairs={{0,4},{4,0},{8,12},{12,8},{1,5},{5,1},{9,13},{13,9},{2,6},{6,2},{1... | collective-permute-start | bytes 589832 | tf_op jit(solution)/shard_map/ppermute | solution.py:392
  7.0 11.0 %collective-permute-start.1 = (bf16[768,128]{1,0:T(8,128)(2,1)}, bf16[768,128]{1,0:T(8,128)(2,1)S(1)}, u32[]{:S(2)}, u32[]{:S(2)}) collective-permute-start(bf16[768,128]{1,0:T(8,128)(2,1)} %get-tuple-element.44), channel_id=1, source_target_pairs={{0,8},{4,12},{8,0},{12,4},{1,9},{5,13},{9,1},{13,5},{2,10},{6,14},... | collective-permute-start | bytes 589832 | tf_op jit(solution)/shard_map/ppermute | solution.py:392
  7.3 10.7 %collective-permute-start.4 = (bf16[1,64,1024]{2,1,0:T(8,128)(2,1)S(1)}, bf16[1,64,1024]{2,1,0:T(8,128)(2,1)S(1)}, u32[]{:S(2)}, u32[]{:S(2)}) collective-permute-start(bf16[1,64,1024]{2,1,0:T(8,128)(2,1)S(1)} %bitcast.1), channel_id=1, source_target_pairs={{0,2},{1,3},{2,0},{3,1},{4,6},{5,7},{6,4},{7,5},{8,10},{9,11},{10,... | collective-permute-start | bytes 393224 | tf_op jit(solution)/shard_map/ppermute | solution.py:398
  10.2 16.5 %collective-permute-start.6 = (bf16[2,768,128]{2,1,0:T(8,128)(2,1)}, bf16[2,768,128]{2,1,0:T(8,128)(2,1)S(1)}, u32[]{:S(2)}, u32[]{:S(2)}) collective-permute-start(bf16[2,768,128]{2,1,0:T(8,128)(2,1)} %get-tuple-element.52.rest_0_), channel_id=1, source_target_pairs={{0,8},{4,12},{8,0},{12,4},{1,9},{5,13},{9,1},{13,5},{2,10},{6,14},... | collective-permute-start | bytes 1179656 | tf_op jit(solution)/shard_map/ppermute | solution.py:392
  11.7 1.0 %copy-start.3 = (bf16[2,768,128]{2,1,0:T(8,128)(2,1)S(1)}, bf16[2,768,128]{2,1,0:T(8,128)(2,1)}, u32[]{:S(2)}) copy-start(bf16[2,768,128]{2,1,0:T(8,128)(2,1)} %get-tuple-element.45.rest_0_) | copy-start | bytes 1179652
  12.7 7.5 %copy-start.5 = (bf16[2,768,128]{2,1,0:T(8,128)(2,1)S(1)}, bf16[2,768,128]{2,1,0:T(8,128)(2,1)}, u32[]{:S(2)}) copy-start(bf16[2,768,128]{2,1,0:T(8,128)(2,1)} %get-tuple-element.52.rest_0_) | copy-start | bytes 1179652
  18.0 8.6 %collective-permute-start.9 = (bf16[2,64,1024]{2,1,0:T(8,128)(2,1)S(1)}, bf16[2,64,1024]{2,1,0:T(8,128)(2,1)S(1)}, u32[]{:S(2)}, u32[]{:S(2)}) collective-permute-start(bf16[2,64,1024]{2,1,0:T(8,128)(2,1)S(1)} %pad_maximum_fusion.1), channel_id=1, source_target_pairs={{0,1},{1,0},{2,3},{3,2},{4,5},{5,4},{6,7},{7,6},{8,9},{9,8},{10,11... | collective-permute-start | bytes 786440 | tf_op jit(solution)/shard_map/ppermute | solution.py:398
  19.7 1.4 %collective-permute-start.7 = (bf16[768,128]{1,0:T(8,128)(2,1)S(1)}, bf16[768,128]{1,0:T(8,128)(2,1)S(1)}, u32[]{:S(2)}, u32[]{:S(2)}) collective-permute-start(bf16[768,128]{1,0:T(8,128)(2,1)S(1)} %collective-permute-done.rest_1_), channel_id=1, source_target_pairs={{0,4},{4,0},{8,12},{12,8},{1,5},{5,1},{9,13},{13,9},{2,6},{6,2},{1... | collective-permute-start | bytes 589832 | tf_op jit(solution)/shard_map/ppermute | solution.py:392
  19.7 1.7 %collective-permute-start.8 = (bf16[768,128]{1,0:T(8,128)(2,1)S(1)}, bf16[768,128]{1,0:T(8,128)(2,1)S(1)}, u32[]{:S(2)}, u32[]{:S(2)}) collective-permute-start(bf16[768,128]{1,0:T(8,128)(2,1)S(1)} %collective-permute-done.1.rest_2_), channel_id=1, source_target_pairs={{0,4},{4,0},{8,12},{12,8},{1,5},{5,1},{9,13},{13,9},{2,6},{6,2},{1... | collective-permute-start | bytes 589832 | tf_op jit(solution)/shard_map/ppermute | solution.py:392
  20.2 11.0 %collective-permute-start.5 = (bf16[2,768,128]{2,1,0:T(8,128)(2,1)S(1)}, bf16[2,768,128]{2,1,0:T(8,128)(2,1)S(1)}, u32[]{:S(2)}, u32[]{:S(2)}) collective-permute-start(bf16[2,768,128]{2,1,0:T(8,128)(2,1)S(1)} %copy-done.5), channel_id=1, source_target_pairs={{0,4},{4,0},{8,12},{12,8},{1,5},{5,1},{9,13},{13,9},{2,6},{6,2},{1... | collective-permute-start | bytes 1179656 | tf_op jit(solution)/shard_map/ppermute | solution.py:392
  26.6 6.3 %collective-permute-start.10 = (bf16[2,768,128]{2,1,0:T(8,128)(2,1)S(1)}, bf16[2,768,128]{2,1,0:T(8,128)(2,1)S(1)}, u32[]{:S(2)}, u32[]{:S(2)}) collective-permute-start(bf16[2,768,128]{2,1,0:T(8,128)(2,1)S(1)} %collective-permute-done.6.rest_2_), channel_id=1, source_target_pairs={{0,4},{4,0},{8,12},{12,8},{1,5},{5,1},{9,13},{13,9},{2,6},{6,2},{1... | collective-permute-start | bytes 1179656 | tf_op jit(solution)/shard_map/ppermute | solution.py:392
  27.0 12.5 %collective-permute-start.14 = (bf16[3,64,1024]{2,1,0:T(8,128)(2,1)S(1)}, bf16[3,64,1024]{2,1,0:T(8,128)(2,1)S(1)}, u32[]{:S(2)}, u32[]{:S(2)}) collective-permute-start(bf16[3,64,1024]{2,1,0:T(8,128)(2,1)S(1)} %constant_dynamic-update-slice_fusion), channel_id=1, source_target_pairs={{0,16},{16,0},{1,17},{17,1},{2,18},{18,2},{3,19},{19,3},{4,20},{20... | collective-permute-start | bytes 1179656 | tf_op jit(solution)/shard_map/ppermute | solution.py:419
  28.6 10.9 %collective-permute-start.11 = (bf16[256,128]{1,0:T(8,128)(2,1)S(1)}, bf16[256,128]{1,0:T(8,128)(2,1)S(1)}, u32[]{:S(2)}, u32[]{:S(2)}) collective-permute-start(bf16[256,128]{1,0:T(8,128)(2,1)S(1)} %get-tuple-element.63), channel_id=1, source_target_pairs={{0,1},{1,0},{2,3},{3,2},{4,5},{5,4},{6,7},{7,6},{8,9},{9,8},{10,11... | collective-permute-start | bytes 196616 | tf_op jit(solution)/shard_map/ppermute | solution.py:398
  29.0 10.5 %collective-permute-start.12 = (bf16[256,128]{1,0:T(8,128)(2,1)S(1)}, bf16[256,128]{1,0:T(8,128)(2,1)S(1)}, u32[]{:S(2)}, u32[]{:S(2)}) collective-permute-start(bf16[256,128]{1,0:T(8,128)(2,1)S(1)} %get-tuple-element.64), channel_id=1, source_target_pairs={{0,2},{1,3},{2,0},{3,1},{4,6},{5,7},{6,4},{7,5},{8,10},{9,11},{10,... | collective-permute-start | bytes 196616 | tf_op jit(solution)/shard_map/ppermute | solution.py:398
  31.2 8.3 %collective-permute-start.13 = (bf16[256,128]{1,0:T(8,128)(2,1)S(1)}, bf16[256,128]{1,0:T(8,128)(2,1)S(1)}, u32[]{:S(2)}, u32[]{:S(2)}) collective-permute-start(bf16[256,128]{1,0:T(8,128)(2,1)S(1)} %get-tuple-element.65), channel_id=1, source_target_pairs={{0,3},{1,2},{2,1},{3,0},{4,7},{5,6},{6,5},{7,4},{8,11},{9,10},{10,... | collective-permute-start | bytes 196616 | tf_op jit(solution)/shard_map/ppermute | solution.py:398
  39.6 8.9 %collective-permute-start.18 = (bf16[3,128,1024]{2,1,0:T(8,128)(2,1)S(1)}, bf16[3,128,1024]{2,1,0:T(8,128)(2,1)S(1)}, u32[]{:S(2)}, u32[]{:S(2)}) collective-permute-start(bf16[3,128,1024]{2,1,0:T(8,128)(2,1)S(1)} %pad_maximum_fusion.rest_9_), channel_id=1, source_target_pairs={{0,4},{4,0},{8,12},{12,8},{1,5},{5,1},{9,13},{13,9},{2,6},{6,2},{1... | collective-permute-start | bytes 2359304 | tf_op jit(solution)/shard_map/ppermute | solution.py:392
  39.7 7.9 %collective-permute-start.15 = (bf16[256,128]{1,0:T(8,128)(2,1)S(1)}, bf16[256,128]{1,0:T(8,128)(2,1)S(1)}, u32[]{:S(2)}, u32[]{:S(2)}) collective-permute-start(bf16[256,128]{1,0:T(8,128)(2,1)S(1)} %get-tuple-element.75), channel_id=1, source_target_pairs={{0,2},{1,3},{2,0},{3,1},{4,6},{5,7},{6,4},{7,5},{8,10},{9,11},{10,... | collective-permute-start | bytes 196616 | tf_op jit(solution)/shard_map/ppermute | solution.py:398
  40.9 6.7 %collective-permute-start.16 = (bf16[256,128]{1,0:T(8,128)(2,1)S(1)}, bf16[256,128]{1,0:T(8,128)(2,1)S(1)}, u32[]{:S(2)}, u32[]{:S(2)}) collective-permute-start(bf16[256,128]{1,0:T(8,128)(2,1)S(1)} %get-tuple-element.77), channel_id=1, source_target_pairs={{0,1},{1,0},{2,3},{3,2},{4,5},{5,4},{6,7},{7,6},{8,9},{9,8},{10,11... | collective-permute-start | bytes 196616 | tf_op jit(solution)/shard_map/ppermute | solution.py:398
  42.4 6.1 %collective-permute-start.17 = (bf16[256,128]{1,0:T(8,128)(2,1)S(1)}, bf16[256,128]{1,0:T(8,128)(2,1)S(1)}, u32[]{:S(2)}, u32[]{:S(2)}) collective-permute-start(bf16[256,128]{1,0:T(8,128)(2,1)S(1)} %get-tuple-element.79), channel_id=1, source_target_pairs={{0,3},{1,2},{2,1},{3,0},{4,7},{5,6},{6,5},{7,4},{8,11},{9,10},{10,... | collective-permute-start | bytes 196616 | tf_op jit(solution)/shard_map/ppermute | solution.py:398

commit v8 on v6

--- a/solution.py
+++ b/solution.py
@@ -455,7 +455,7 @@
                 arriving = other_tiles(w_mine)
             exchange(pieces, 0)
         else:
-            pieces = attend(queries[p], held, sources, bias, first, heads, 1, heads - 1, 2**31)
+            pieces = attend(queries[p], held, sources, bias, first, heads, 1, heads - 1, 3 * 2**29)
             pieces, attended, sources[-1] = lax.optimization_barrier((pieces, attended, sources[-1]))
             exchange(pieces, 1)
             arriving, sources[-1] = lax.optimization_barrier((arriving, sources[-1]))

time: 50.4 us -> 50.4 us (level)
  no operation moved by 1% of the time
where the time goes in v8:
time: 50.4 us; the launch traced here: 50.2 us
  Pallas kernels  25.8 us (51%)
  starting transfers between devices  20.9 us (41%)
  waiting for transfers between devices  2.18 us (4%)
  local copies, waits for them, and re-layouts  1.05 us (2%)
    pallas_call x3, Pallas kernels, attend(): pl.pallas_call(kernel, out_shape=[jax.ShapeDtypeStruct((part, LANES), jnp...  15.2 us
    ppermute x8, starting transfers between devices, along_head(): return lax.ppermute(array, 'head', [(i, i ^ k) for i in range(heads)])  13.4 us
    ppermute x10, starting transfers between devices, along_band(): return lax.ppermute(array, 'band', [(i, goes_to(i)) for i in range(bands)])  5.91 us
    pallas_call x1, Pallas kernels, begin_attention(): pl.pallas_call(kernel, out_shape=[jax.ShapeDtypeStruct((2, rows, LANES),...  5.25 us
    pallas_call x1, Pallas kernels, project_kv(): pl.pallas_call(kernel, out_shape=[jax.ShapeDtypeStruct((rows, LANES), jnp...  3.69 us
    pallas_call x1, Pallas kernels, project_out(): pl.pallas_call(kernel, out_shape=jax.ShapeDtypeStruct((rows, width), jnp....  1.72 us
    ppermute x1, starting transfers between devices, other_tiles(): lax.ppermute(array, 'tiles', [(i, i ^ s) for i in range(tiles)])  1.58 us
    ppermute x10, waiting for transfers between devices, along_band(): return lax.ppermute(array, 'band', [(i, goes_to(i)) for i in range(bands)])  1.23 us
  transfers between devices with their start and end apart: 19, of which 3 were waited for; matrix products, arithmetic and copies ran while one was open for 0% of the time, Pallas kernels for 41%

profile of v8, /device:TPU:0, one launch (start us, length us, event | category | flops | bytes accessed | tf_op | source)
XLA Modules:
  0.0 50.2 jit_solution(8108397041032833331)
XLA Ops:
  0.0 3.7 %project_kv.1 = (bf16[768,128]{1,0:T(8,128)(2,1)}, bf16[768,128]{1,0:T(8,128)(2,1)}, bf16[2,768,128]{2,1,0:T(8,128)(2,1)}, bf16[2,768,128]{2,1,0:T(8,128)(2,1)}) custom-call(s32[32,32]{1,0:T(8,128)} %mask_ref.1, bf16[1024,1024]{1,0:T(8,128)(2,1)} %tok.1, bf16[1024,256]{1,0:T(8,128)(2,1)} %wk_ref.1, bf16[1024,256]{1,0:T(8,128)(2,1)} %wv_ref.1), custom_call_target="tpu_custom_call" | custom-call | tf_op jit(solution)/shard_map/project_kv/pallas_call | solution.py:115
  3.7 0.5 %collective-permute-start.2 = (bf16[768,128]{1,0:T(8,128)(2,1)}, bf16[768,128]{1,0:T(8,128)(2,1)}, u32[]{:S(2)}, u32[]{:S(2)}) collective-permute-start(bf16[768,128]{1,0:T(8,128)(2,1)} %get-tuple-element.43), channel_id=1, source_target_pairs={{0,4},{4,0},{8,12},{12,8},{1,5},{5,1},{9,13},{13,9},{2,6},{6,2},{1... | collective-permute-start | bytes 589832 | tf_op jit(solution)/shard_map/ppermute | solution.py:392
  4.2 2.6 %collective-permute-start = (bf16[768,128]{1,0:T(8,128)(2,1)}, bf16[768,128]{1,0:T(8,128)(2,1)S(1)}, u32[]{:S(2)}, u32[]{:S(2)}) collective-permute-start(bf16[768,128]{1,0:T(8,128)(2,1)} %get-tuple-element.43), channel_id=1, source_target_pairs={{0,8},{4,12},{8,0},{12,4},{1,9},{5,13},{9,1},{13,5},{2,10},{6,14},... | collective-permute-start | bytes 589832 | tf_op jit(solution)/shard_map/ppermute | solution.py:392
  6.8 0.2 collective-permute-start.3
  7.0 0.3 collective-permute-start.1
  7.2 0.0 copy-done.1
  7.3 2.9 %collective-permute-start.4 = (bf16[1,64,1024]{2,1,0:T(8,128)(2,1)S(1)}, bf16[1,64,1024]{2,1,0:T(8,128)(2,1)S(1)}, u32[]{:S(2)}, u32[]{:S(2)}) collective-permute-start(bf16[1,64,1024]{2,1,0:T(8,128)(2,1)S(1)} %bitcast.1), channel_id=1, source_target_pairs={{0,2},{1,3},{2,0},{3,1},{4,6},{5,7},{6,4},{7,5},{8,10},{9,11},{10,... | collective-permute-start | bytes 393224 | tf_op jit(solution)/shard_map/ppermute | solution.py:398
  10.2 0.0 collective-permute-done.2.rest_1_
  10.2 1.5 %collective-permute-start.6 = (bf16[2,768,128]{2,1,0:T(8,128)(2,1)}, bf16[2,768,128]{2,1,0:T(8,128)(2,1)S(1)}, u32[]{:S(2)}, u32[]{:S(2)}) collective-permute-start(bf16[2,768,128]{2,1,0:T(8,128)(2,1)} %get-tuple-element.52.rest_0_), channel_id=1, source_target_pairs={{0,8},{4,12},{8,0},{12,4},{1,9},{5,13},{9,1},{13,5},{2,10},{6,14},... | collective-permute-start | bytes 1179656 | tf_op jit(solution)/shard_map/ppermute | solution.py:392
  11.7 0.0 collective-permute-done.3.rest_2_
  11.7 1.0 %copy-done.3 = bf16[2,768,128]{2,1,0:T(8,128)(2,1)S(1)} copy-done((bf16[2,768,128]{2,1,0:T(8,128)(2,1)S(1)}, bf16[2,768,128]{2,1,0:T(8,128)(2,1)}, u32[]{:S(2)}) %copy-start.3) | copy-done | bytes 393240
  12.7 5.2 %begin_attention.1 = (bf16[2,1024,128]{2,1,0:T(8,128)(2,1)S(1)}, bf16[2,1024,128]{2,1,0:T(8,128)(2,1)S(1)}, f32[32,128]{1,0:T(8,128)S(1)}, f32[2,1024,128]{2,1,0:T(8,128)S(1)}) custom-call(s32[32,32]{1,0:T(8,128)S(1)} %copy-done.4, bf16[1024,1024]{1,0:T(8,128)(2,1)S(1)} %copy-done, bf16[1024,256]{1,0:T(8,128)(2,1)S(1)} %copy-done.2, ...), custom_call_target="tpu_custom_call" | custom-call | tf_op jit(solution)/shard_map/begin_attention/pallas_call | solution.py:257
  18.0 0.0 collective-permute-done.4
  18.0 0.0 collective-permute-done.rest_1_
  18.0 0.0 collective-permute-done.1.rest_2_
  18.0 1.6 %collective-permute-start.9 = (bf16[2,64,1024]{2,1,0:T(8,128)(2,1)S(1)}, bf16[2,64,1024]{2,1,0:T(8,128)(2,1)S(1)}, u32[]{:S(2)}, u32[]{:S(2)}) collective-permute-start(bf16[2,64,1024]{2,1,0:T(8,128)(2,1)S(1)} %pad_maximum_fusion.1), channel_id=1, source_target_pairs={{0,1},{1,0},{2,3},{3,2},{4,5},{5,4},{6,7},{7,6},{8,9},{9,8},{10,11... | collective-permute-start | bytes 786440 | tf_op jit(solution)/shard_map/ppermute | solution.py:398
  19.7 0.0 collective-permute-start.7
  19.7 0.5 %collective-permute-start.8 = (bf16[768,128]{1,0:T(8,128)(2,1)S(1)}, bf16[768,128]{1,0:T(8,128)(2,1)S(1)}, u32[]{:S(2)}, u32[]{:S(2)}) collective-permute-start(bf16[768,128]{1,0:T(8,128)(2,1)S(1)} %collective-permute-done.1.rest_2_), channel_id=1, source_target_pairs={{0,4},{4,0},{8,12},{12,8},{1,5},{5,1},{9,13},{13,9},{2,6},{6,2},{1... | collective-permute-start | bytes 589832 | tf_op jit(solution)/shard_map/ppermute | solution.py:392
  20.2 0.0 copy-done.5
  20.2 0.0 collective-permute-start.5
  20.2 0.9 %collective-permute-done.7.rest_3_ = bf16[768,128]{1,0:T(8,128)(2,1)S(1)} collective-permute-done((bf16[768,128]{1,0:T(8,128)(2,1)S(1)}, bf16[768,128]{1,0:T(8,128)(2,1)S(1)}, u32[]{:S(2)}, u32[]{:S(2)}) %collective-permute-start.7) | collective-permute-done | bytes 196640 | tf_op jit(solution)/shard_map/ppermute | solution.py:392
  21.1 0.3 collective-permute-done.8.rest_4_
  21.4 5.2 %attend.3 = (bf16[256,128]{1,0:T(8,128)(2,1)S(1)}, bf16[256,128]{1,0:T(8,128)(2,1)S(1)}, bf16[256,128]{1,0:T(8,128)(2,1)S(1)}, bf16[256,128]{1,0:T(8,128)(2,1)S(1)}) custom-call(bf16[2,1024,128]{2,1,0:T(8,128)(2,1)S(1)} %get-tuple-element.53.q_ref, f32[32,128]{1,0:T(8,128)S(1)} %get-tuple-element.51.bias_ref, f32[2,1024,128]{2,1,0:T(8,128)S(1)} %get-tuple-element.54.rest_0_, ...), custom_call_target="tpu_custom_call" | custom-call | tf_op jit(solution)/shard_map/attend/pallas_call | solution.py:308
  26.6 0.0 collective-permute-done.9
  26.6 0.0 collective-permute-done.6.rest_2_
  26.6 0.3 collective-permute-start.10
  27.0 1.6 %collective-permute-start.14 = (bf16[3,64,1024]{2,1,0:T(8,128)(2,1)S(1)}, bf16[3,64,1024]{2,1,0:T(8,128)(2,1)S(1)}, u32[]{:S(2)}, u32[]{:S(2)}) collective-permute-start(bf16[3,64,1024]{2,1,0:T(8,128)(2,1)S(1)} %constant_dynamic-update-slice_fusion), channel_id=1, source_target_pairs={{0,16},{16,0},{1,17},{17,1},{2,18},{18,2},{3,19},{19,3},{4,20},{20... | collective-permute-start | bytes 1179656 | tf_op jit(solution)/shard_map/ppermute | solution.py:419
  28.6 0.4 collective-permute-start.11
  29.0 2.2 %collective-permute-start.12 = (bf16[256,128]{1,0:T(8,128)(2,1)S(1)}, bf16[256,128]{1,0:T(8,128)(2,1)S(1)}, u32[]{:S(2)}, u32[]{:S(2)}) collective-permute-start(bf16[256,128]{1,0:T(8,128)(2,1)S(1)} %get-tuple-element.64), channel_id=1, source_target_pairs={{0,2},{1,3},{2,0},{3,1},{4,6},{5,7},{6,4},{7,5},{8,10},{9,11},{10,... | collective-permute-start | bytes 196616 | tf_op jit(solution)/shard_map/ppermute | solution.py:398
  31.2 0.0 collective-permute-done.5.rest_1_
  31.2 1.7 %collective-permute-start.13 = (bf16[256,128]{1,0:T(8,128)(2,1)S(1)}, bf16[256,128]{1,0:T(8,128)(2,1)S(1)}, u32[]{:S(2)}, u32[]{:S(2)}) collective-permute-start(bf16[256,128]{1,0:T(8,128)(2,1)S(1)} %get-tuple-element.65), channel_id=1, source_target_pairs={{0,3},{1,2},{2,1},{3,0},{4,7},{5,6},{6,5},{7,4},{8,11},{9,10},{10,... | collective-permute-start | bytes 196616 | tf_op jit(solution)/shard_map/ppermute | solution.py:398
  33.0 0.0 collective-permute-done.10.rest_3_
  33.0 6.5 %attend.4 = (bf16[256,128]{1,0:T(8,128)(2,1)S(1)}, bf16[256,128]{1,0:T(8,128)(2,1)S(1)}, bf16[256,128]{1,0:T(8,128)(2,1)S(1)}) custom-call(bf16[2,1024,128]{2,1,0:T(8,128)(2,1)S(1)} %get-tuple-element.50.q_ref, f32[32,128]{1,0:T(8,128)S(1)} %get-tuple-element.51.bias_ref, bf16[2,768,128]{2,1,0:T(8,128)(2,1)S(1)} %copy-done.5, ...), custom_call_target="tpu_custom_call" | custom-call | flops 1610612736 | tf_op jit(solution)/shard_map/attend/pallas_call | solution.py:308
  39.5 0.0 collective-permute-done.11.rest_4_
  39.5 0.0 collective-permute-done.12.rest_2_
  39.5 0.0 collective-permute-done.13.rest_6_
  39.5 0.0 collective-permute-done.14
  39.5 0.1 pad_maximum_fusion.rest_9_
  39.6 0.1 collective-permute-start.18
  39.7 1.2 %collective-permute-start.15 = (bf16[256,128]{1,0:T(8,128)(2,1)S(1)}, bf16[256,128]{1,0:T(8,128)(2,1)S(1)}, u32[]{:S(2)}, u32[]{:S(2)}) collective-permute-start(bf16[256,128]{1,0:T(8,128)(2,1)S(1)} %get-tuple-element.75), channel_id=1, source_target_pairs={{0,2},{1,3},{2,0},{3,1},{4,6},{5,7},{6,4},{7,5},{8,10},{9,11},{10,... | collective-permute-start | bytes 196616 | tf_op jit(solution)/shard_map/ppermute | solution.py:398
  40.9 1.5 %collective-permute-start.16 = (bf16[256,128]{1,0:T(8,128)(2,1)S(1)}, bf16[256,128]{1,0:T(8,128)(2,1)S(1)}, u32[]{:S(2)}, u32[]{:S(2)}) collective-permute-start(bf16[256,128]{1,0:T(8,128)(2,1)S(1)} %get-tuple-element.77), channel_id=1, source_target_pairs={{0,1},{1,0},{2,3},{3,2},{4,5},{5,4},{6,7},{7,6},{8,9},{9,8},{10,11... | collective-permute-start | bytes 196616 | tf_op jit(solution)/shard_map/ppermute | solution.py:398
  42.4 1.7 %collective-permute-start.17 = (bf16[256,128]{1,0:T(8,128)(2,1)S(1)}, bf16[256,128]{1,0:T(8,128)(2,1)S(1)}, u32[]{:S(2)}, u32[]{:S(2)}) collective-permute-start(bf16[256,128]{1,0:T(8,128)(2,1)S(1)} %get-tuple-element.79), channel_id=1, source_target_pairs={{0,3},{1,2},{2,1},{3,0},{4,7},{5,6},{6,5},{7,4},{8,11},{9,10},{10,... | collective-permute-start | bytes 196616 | tf_op jit(solution)/shard_map/ppermute | solution.py:398
  44.1 3.4 %attend.5.rest_1_ = bf16[256,128]{1,0:T(8,128)(2,1)S(1)} custom-call(bf16[2,1024,128]{2,1,0:T(8,128)(2,1)S(1)} %get-tuple-element.50.q_ref, f32[32,128]{1,0:T(8,128)S(1)} %get-tuple-element.51.bias_ref, bf16[2,768,128]{2,1,0:T(8,128)(2,1)S(1)} %copy-done.5, bf16[2,768,128]{2,1,0:T(8,128)(2,1)S(1)} %collective-permute-done.5.rest_1_, ...), custom_call_target="tpu_custom_call" | custom-call | flops 8589934592 | tf_op jit(solution)/shard_map/attend/pallas_call | solution.py:308
  47.6 0.0 collective-permute-done.15.rest_3_
  47.6 0.0 collective-permute-done.16.rest_5_
  47.6 0.9 %collective-permute-done.17.rest_7_ = bf16[256,128]{1,0:T(8,128)(2,1)S(1)} collective-permute-done((bf16[256,128]{1,0:T(8,128)(2,1)S(1)}, bf16[256,128]{1,0:T(8,128)(2,1)S(1)}, u32[]{:S(2)}, u32[]{:S(2)}) %collective-permute-start.17) | collective-permute-done | bytes 65568 | tf_op jit(solution)/shard_map/ppermute | solution.py:398
  48.5 0.0 collective-permute-done.18.rest_10_
  48.5 1.7 %project_out.1 = bf16[256,1024]{1,0:T(8,128)(2,1)} custom-call(bf16[256,128]{1,0:T(8,128)(2,1)S(1)} %get-tuple-element.70.rest_0_, bf16[256,128]{1,0:T(8,128)(2,1)S(1)} %attend.5.rest_1_, bf16[256,128]{1,0:T(8,128)(2,1)S(1)} %collective-permute-done.12.rest_2_, bf16[256,128]{1,0:T(8,128)(2,1)S(1)} %collective-permute-done.15.rest_3_, ...), custom_call_target="tpu_custom_call" | custom-call | tf_op jit(solution)/shard_map/project_out/pallas_call | solution.py:375
  (13 shorter events, 0.1 us)
Async XLA Ops:
  0.0 11.7 %copy-start.4 = (s32[32,32]{1,0:T(8,128)S(1)}, s32[32,32]{1,0:T(8,128)}, u32[]{:S(2)}) copy-start(s32[32,32]{1,0:T(8,128)} %mask_ref.1) | copy-start | bytes 12292
  0.0 11.7 %copy-start = (bf16[1024,1024]{1,0:T(8,128)(2,1)S(1)}, bf16[1024,1024]{1,0:T(8,128)(2,1)}, u32[]{:S(2)}) copy-start(bf16[1024,1024]{1,0:T(8,128)(2,1)} %tok.1) | copy-start | bytes 6291460
  0.0 7.2 %copy-start.1 = (bf16[256,1024]{1,0:T(8,128)(2,1)S(1)}, bf16[256,1024]{1,0:T(8,128)(2,1)}, u32[]{:S(2)}) copy-start(bf16[256,1024]{1,0:T(8,128)(2,1)} %rest_8_.1) | copy-start | bytes 1572868
  0.0 11.7 %copy-start.2 = (bf16[1024,256]{1,0:T(8,128)(2,1)S(1)}, bf16[1024,256]{1,0:T(8,128)(2,1)}, u32[]{:S(2)}) copy-start(bf16[1024,256]{1,0:T(8,128)(2,1)} %w_any.1) | copy-start | bytes 1572868
  3.7 6.5 %collective-permute-start.2 = (bf16[768,128]{1,0:T(8,128)(2,1)}, bf16[768,128]{1,0:T(8,128)(2,1)}, u32[]{:S(2)}, u32[]{:S(2)}) collective-permute-start(bf16[768,128]{1,0:T(8,128)(2,1)} %get-tuple-element.43), channel_id=1, source_target_pairs={{0,4},{4,0},{8,12},{12,8},{1,5},{5,1},{9,13},{13,9},{2,6},{6,2},{1... | collective-permute-start | bytes 589832 | tf_op jit(solution)/shard_map/ppermute | solution.py:392
  4.2 13.7 %collective-permute-start = (bf16[768,128]{1,0:T(8,128)(2,1)}, bf16[768,128]{1,0:T(8,128)(2,1)S(1)}, u32[]{:S(2)}, u32[]{:S(2)}) collective-permute-start(bf16[768,128]{1,0:T(8,128)(2,1)} %get-tuple-element.43), channel_id=1, source_target_pairs={{0,8},{4,12},{8,0},{12,4},{1,9},{5,13},{9,1},{13,5},{2,10},{6,14},... | collective-permute-start | bytes 589832 | tf_op jit(solution)/shard_map/ppermute | solution.py:392
  6.8 4.9 %collective-permute-start.3 = (bf16[768,128]{1,0:T(8,128)(2,1)}, bf16[768,128]{1,0:T(8,128)(2,1)}, u32[]{:S(2)}, u32[]{:S(2)}) collective-permute-start(bf16[768,128]{1,0:T(8,128)(2,1)} %get-tuple-element.44), channel_id=1, source_target_pairs={{0,4},{4,0},{8,12},{12,8},{1,5},{5,1},{9,13},{13,9},{2,6},{6,2},{1... | collective-permute-start | bytes 589832 | tf_op jit(solution)/shard_map/ppermute | solution.py:392
  7.0 11.0 %collective-permute-start.1 = (bf16[768,128]{1,0:T(8,128)(2,1)}, bf16[768,128]{1,0:T(8,128)(2,1)S(1)}, u32[]{:S(2)}, u32[]{:S(2)}) collective-permute-start(bf16[768,128]{1,0:T(8,128)(2,1)} %get-tuple-element.44), channel_id=1, source_target_pairs={{0,8},{4,12},{8,0},{12,4},{1,9},{5,13},{9,1},{13,5},{2,10},{6,14},... | collective-permute-start | bytes 589832 | tf_op jit(solution)/shard_map/ppermute | solution.py:392
  7.3 10.7 %collective-permute-start.4 = (bf16[1,64,1024]{2,1,0:T(8,128)(2,1)S(1)}, bf16[1,64,1024]{2,1,0:T(8,128)(2,1)S(1)}, u32[]{:S(2)}, u32[]{:S(2)}) collective-permute-start(bf16[1,64,1024]{2,1,0:T(8,128)(2,1)S(1)} %bitcast.1), channel_id=1, source_target_pairs={{0,2},{1,3},{2,0},{3,1},{4,6},{5,7},{6,4},{7,5},{8,10},{9,11},{10,... | collective-permute-start | bytes 393224 | tf_op jit(solution)/shard_map/ppermute | solution.py:398
  10.2 16.5 %collective-permute-start.6 = (bf16[2,768,128]{2,1,0:T(8,128)(2,1)}, bf16[2,768,128]{2,1,0:T(8,128)(2,1)S(1)}, u32[]{:S(2)}, u32[]{:S(2)}) collective-permute-start(bf16[2,768,128]{2,1,0:T(8,128)(2,1)} %get-tuple-element.52.rest_0_), channel_id=1, source_target_pairs={{0,8},{4,12},{8,0},{12,4},{1,9},{5,13},{9,1},{13,5},{2,10},{6,14},... | collective-permute-start | bytes 1179656 | tf_op jit(solution)/shard_map/ppermute | solution.py:392
  11.7 1.0 %copy-start.3 = (bf16[2,768,128]{2,1,0:T(8,128)(2,1)S(1)}, bf16[2,768,128]{2,1,0:T(8,128)(2,1)}, u32[]{:S(2)}) copy-start(bf16[2,768,128]{2,1,0:T(8,128)(2,1)} %get-tuple-element.45.rest_0_) | copy-start | bytes 1179652
  12.7 7.5 %copy-start.5 = (bf16[2,768,128]{2,1,0:T(8,128)(2,1)S(1)}, bf16[2,768,128]{2,1,0:T(8,128)(2,1)}, u32[]{:S(2)}) copy-start(bf16[2,768,128]{2,1,0:T(8,128)(2,1)} %get-tuple-element.52.rest_0_) | copy-start | bytes 1179652
  18.0 8.6 %collective-permute-start.9 = (bf16[2,64,1024]{2,1,0:T(8,128)(2,1)S(1)}, bf16[2,64,1024]{2,1,0:T(8,128)(2,1)S(1)}, u32[]{:S(2)}, u32[]{:S(2)}) collective-permute-start(bf16[2,64,1024]{2,1,0:T(8,128)(2,1)S(1)} %pad_maximum_fusion.1), channel_id=1, source_target_pairs={{0,1},{1,0},{2,3},{3,2},{4,5},{5,4},{6,7},{7,6},{8,9},{9,8},{10,11... | collective-permute-start | bytes 786440 | tf_op jit(solution)/shard_map/ppermute | solution.py:398
  19.7 1.4 %collective-permute-start.7 = (bf16[768,128]{1,0:T(8,128)(2,1)S(1)}, bf16[768,128]{1,0:T(8,128)(2,1)S(1)}, u32[]{:S(2)}, u32[]{:S(2)}) collective-permute-start(bf16[768,128]{1,0:T(8,128)(2,1)S(1)} %collective-permute-done.rest_1_), channel_id=1, source_target_pairs={{0,4},{4,0},{8,12},{12,8},{1,5},{5,1},{9,13},{13,9},{2,6},{6,2},{1... | collective-permute-start | bytes 589832 | tf_op jit(solution)/shard_map/ppermute | solution.py:392
  19.7 1.7 %collective-permute-start.8 = (bf16[768,128]{1,0:T(8,128)(2,1)S(1)}, bf16[768,128]{1,0:T(8,128)(2,1)S(1)}, u32[]{:S(2)}, u32[]{:S(2)}) collective-permute-start(bf16[768,128]{1,0:T(8,128)(2,1)S(1)} %collective-permute-done.1.rest_2_), channel_id=1, source_target_pairs={{0,4},{4,0},{8,12},{12,8},{1,5},{5,1},{9,13},{13,9},{2,6},{6,2},{1... | collective-permute-start | bytes 589832 | tf_op jit(solution)/shard_map/ppermute | solution.py:392
  20.2 11.0 %collective-permute-start.5 = (bf16[2,768,128]{2,1,0:T(8,128)(2,1)S(1)}, bf16[2,768,128]{2,1,0:T(8,128)(2,1)S(1)}, u32[]{:S(2)}, u32[]{:S(2)}) collective-permute-start(bf16[2,768,128]{2,1,0:T(8,128)(2,1)S(1)} %copy-done.5), channel_id=1, source_target_pairs={{0,4},{4,0},{8,12},{12,8},{1,5},{5,1},{9,13},{13,9},{2,6},{6,2},{1... | collective-permute-start | bytes 1179656 | tf_op jit(solution)/shard_map/ppermute | solution.py:392
  26.6 6.3 %collective-permute-start.10 = (bf16[2,768,128]{2,1,0:T(8,128)(2,1)S(1)}, bf16[2,768,128]{2,1,0:T(8,128)(2,1)S(1)}, u32[]{:S(2)}, u32[]{:S(2)}) collective-permute-start(bf16[2,768,128]{2,1,0:T(8,128)(2,1)S(1)} %collective-permute-done.6.rest_2_), channel_id=1, source_target_pairs={{0,4},{4,0},{8,12},{12,8},{1,5},{5,1},{9,13},{13,9},{2,6},{6,2},{1... | collective-permute-start | bytes 1179656 | tf_op jit(solution)/shard_map/ppermute | solution.py:392
  27.0 12.5 %collective-permute-start.14 = (bf16[3,64,1024]{2,1,0:T(8,128)(2,1)S(1)}, bf16[3,64,1024]{2,1,0:T(8,128)(2,1)S(1)}, u32[]{:S(2)}, u32[]{:S(2)}) collective-permute-start(bf16[3,64,1024]{2,1,0:T(8,128)(2,1)S(1)} %constant_dynamic-update-slice_fusion), channel_id=1, source_target_pairs={{0,16},{16,0},{1,17},{17,1},{2,18},{18,2},{3,19},{19,3},{4,20},{20... | collective-permute-start | bytes 1179656 | tf_op jit(solution)/shard_map/ppermute | solution.py:419
  28.6 10.9 %collective-permute-start.11 = (bf16[256,128]{1,0:T(8,128)(2,1)S(1)}, bf16[256,128]{1,0:T(8,128)(2,1)S(1)}, u32[]{:S(2)}, u32[]{:S(2)}) collective-permute-start(bf16[256,128]{1,0:T(8,128)(2,1)S(1)} %get-tuple-element.63), channel_id=1, source_target_pairs={{0,1},{1,0},{2,3},{3,2},{4,5},{5,4},{6,7},{7,6},{8,9},{9,8},{10,11... | collective-permute-start | bytes 196616 | tf_op jit(solution)/shard_map/ppermute | solution.py:398
  29.0 10.5 %collective-permute-start.12 = (bf16[256,128]{1,0:T(8,128)(2,1)S(1)}, bf16[256,128]{1,0:T(8,128)(2,1)S(1)}, u32[]{:S(2)}, u32[]{:S(2)}) collective-permute-start(bf16[256,128]{1,0:T(8,128)(2,1)S(1)} %get-tuple-element.64), channel_id=1, source_target_pairs={{0,2},{1,3},{2,0},{3,1},{4,6},{5,7},{6,4},{7,5},{8,10},{9,11},{10,... | collective-permute-start | bytes 196616 | tf_op jit(solution)/shard_map/ppermute | solution.py:398
  31.2 8.3 %collective-permute-start.13 = (bf16[256,128]{1,0:T(8,128)(2,1)S(1)}, bf16[256,128]{1,0:T(8,128)(2,1)S(1)}, u32[]{:S(2)}, u32[]{:S(2)}) collective-permute-start(bf16[256,128]{1,0:T(8,128)(2,1)S(1)} %get-tuple-element.65), channel_id=1, source_target_pairs={{0,3},{1,2},{2,1},{3,0},{4,7},{5,6},{6,5},{7,4},{8,11},{9,10},{10,... | collective-permute-start | bytes 196616 | tf_op jit(solution)/shard_map/ppermute | solution.py:398
  39.6 8.9 %collective-permute-start.18 = (bf16[3,128,1024]{2,1,0:T(8,128)(2,1)S(1)}, bf16[3,128,1024]{2,1,0:T(8,128)(2,1)S(1)}, u32[]{:S(2)}, u32[]{:S(2)}) collective-permute-start(bf16[3,128,1024]{2,1,0:T(8,128)(2,1)S(1)} %pad_maximum_fusion.rest_9_), channel_id=1, source_target_pairs={{0,4},{4,0},{8,12},{12,8},{1,5},{5,1},{9,13},{13,9},{2,6},{6,2},{1... | collective-permute-start | bytes 2359304 | tf_op jit(solution)/shard_map/ppermute | solution.py:392
  39.7 7.9 %collective-permute-start.15 = (bf16[256,128]{1,0:T(8,128)(2,1)S(1)}, bf16[256,128]{1,0:T(8,128)(2,1)S(1)}, u32[]{:S(2)}, u32[]{:S(2)}) collective-permute-start(bf16[256,128]{1,0:T(8,128)(2,1)S(1)} %get-tuple-element.75), channel_id=1, source_target_pairs={{0,2},{1,3},{2,0},{3,1},{4,6},{5,7},{6,4},{7,5},{8,10},{9,11},{10,... | collective-permute-start | bytes 196616 | tf_op jit(solution)/shard_map/ppermute | solution.py:398
  40.9 6.7 %collective-permute-start.16 = (bf16[256,128]{1,0:T(8,128)(2,1)S(1)}, bf16[256,128]{1,0:T(8,128)(2,1)S(1)}, u32[]{:S(2)}, u32[]{:S(2)}) collective-permute-start(bf16[256,128]{1,0:T(8,128)(2,1)S(1)} %get-tuple-element.77), channel_id=1, source_target_pairs={{0,1},{1,0},{2,3},{3,2},{4,5},{5,4},{6,7},{7,6},{8,9},{9,8},{10,11... | collective-permute-start | bytes 196616 | tf_op jit(solution)/shard_map/ppermute | solution.py:398
  42.4 6.1 %collective-permute-start.17 = (bf16[256,128]{1,0:T(8,128)(2,1)S(1)}, bf16[256,128]{1,0:T(8,128)(2,1)S(1)}, u32[]{:S(2)}, u32[]{:S(2)}) collective-permute-start(bf16[256,128]{1,0:T(8,128)(2,1)S(1)} %get-tuple-element.79), channel_id=1, source_target_pairs={{0,3},{1,2},{2,1},{3,0},{4,7},{5,6},{6,5},{7,4},{8,11},{9,10},{10,... | collective-permute-start | bytes 196616 | tf_op jit(solution)/shard_map/ppermute | solution.py:398
